TPU v7x, 32 devices: a whole 2x2x4 slice. The times are simulated.
32 devices in a mesh: groups: 2 (over y), bins: 4 (over z), fdot: 4 (over x, core).
Axes of the slice: x: 2, y: 2, z: 4, core: 2. Of those that a mesh axis runs over, the one named last changes fastest.
Arguments:
- spectrum: float32 [2, 262144], P(None, ('groups', 'bins')), parts along dimension 1, may hold values from -80 to 80
- bank: bfloat16 [128, 2, 128], replicated, may hold values from -0.5 to 0.5
- fdot_index: int32 [32], P('fdot'), may hold values from 0 to 127
- harm_map: int32 [7, 4, 4], P(None, 'bins'), may hold values from 0 to 28672, as said below
Outputs:
- harmonic_power: float32 [32, 262144], P('fdot', ('groups', 'bins')), parts along dimension 1
There are 2 independent parts, one for each index of `groups`. A program takes and returns all parts, laid end to end along the dimension named above; an argument that names none is the same for every part. Nothing has to cross between parts.
Inputs may be any that keep to these rules, and one draw needn't show every extreme that they name: harm_map[q, d] = (floor(d s / 8), s, (d * 32768 s / 8) mod 32768, p) with s = 4, 2, 6, 1, 3, 5, 7 for q = 0 .. 6 and a rounding phase p in 0 .. 7.
All inputs are finite; a program needn't handle non-finite values.
Results may differ from a plain program's by a relative error of at most 0.0003.
The roundings to bfloat16 on the way count: a program that leaves them out, or rounds other values in their place, can miss the bound.
Values may be sent and summed in bfloat16 or wider, within the bound.
No kernel may reach another device: no remote copies, remote signals or barrier semaphores. Data moves between devices by JAX's collectives and lax.ppermute only.
A program may use at most 64 MiB of HBM per device.

v0:
```python
import functools
import math

import jax
import jax.numpy as jnp
from jax import lax
from jax.experimental import pallas as pl
from jax.experimental.pallas import tpu as pltpu
from jax.sharding import PartitionSpec as P

LANES = 128
STRIDE_TABLE = (4, 2, 6, 1, 3, 5, 7)
F32 = jnp.float32
BF16 = jnp.bfloat16


def from_partner(value, axis, mask):
    pairs = [(source, source ^ mask) for source in range(lax.axis_size(axis))]
    return lax.ppermute(value, axis, pairs)


def template_kernel(index_ref, bank_ref, out_ref):
    count = index_ref.shape[0]
    n_bank = bank_ref.shape[0]
    slots = lax.broadcasted_iota(jnp.int32, (count, n_bank), 1)
    onehot = (index_ref[...] == slots).astype(F32).astype(BF16)
    taps = jnp.dot(onehot, bank_ref[...], preferred_element_type=F32)
    zeros = jnp.zeros((1, LANES), F32)

    def banded(row):
        wide = jnp.broadcast_to(jnp.concatenate([row, zeros], axis=1), (LANES, 2 * LANES))
        return pltpu.roll(wide, 0, 1, stride=1, stride_axis=0)

    for t in range(count):
        real = banded(taps[t : t + 1, :LANES])
        imag = banded(taps[t : t + 1, LANES:])
        top, low = 2 * t * LANES, (2 * t + 1) * LANES
        out_ref[top : top + LANES, : 2 * LANES] = real.astype(BF16)
        out_ref[top : top + LANES, 2 * LANES :] = (-imag).astype(BF16)
        out_ref[low : low + LANES, : 2 * LANES] = imag.astype(BF16)
        out_ref[low : low + LANES, 2 * LANES :] = real.astype(BF16)


def template_rows(bank, fdot_index):
    count = fdot_index.shape[0]
    n_bank, _, taps = bank.shape
    rows = 2 * count * taps
    return pl.pallas_call(
        template_kernel,
        out_shape=jax.ShapeDtypeStruct((rows, 4 * taps), BF16),
        cost_estimate=pl.CostEstimate(
            flops=4 * rows * taps, bytes_accessed=8 * rows * taps, transcendentals=0
        ),
        name="template_rows",
    )(fdot_index.reshape(count, 1), bank.reshape(n_bank, 2 * taps))


def search_kernel(
    strides, sizes, meta_ref, twist_ref, base_ref, *refs
):
    block_rows, blocks, templates, moved = sizes
    own_ref, *rest = refs[: 1 + 2 * moved]
    rest = refs[1 : 1 + 2 * moved]
    weights_hbm, out_ref, raw, real, imag, weights, windows, acc, *more = refs[1 + 2 * moved :]
    planes = more[: len(strides)]
    copy_sem, weight_sem = more[len(strides) :]
    rows = block_rows * blocks
    total_bins = rows * LANES
    segments = block_rows // 8
    device = meta_ref[0]
    part = meta_ref[1]

    weight_copy = pltpu.make_async_copy(weights_hbm, weights, weight_sem)
    weight_copy.start()
    copies = []

    def fetch(source, start):
        size = source.shape[0]
        start = pl.multiple_of(start, size)
        copy = pltpu.make_async_copy(
            source, raw.at[pl.ds(start, size), :], copy_sem.at[len(copies)]
        )
        copy.start()
        copies.append(copy)

    fetch(own_ref, device * (2 * block_rows))
    for k in range(1, moved + 1):
        other = (device ^ k) * (2 * block_rows)
        fetch(rest[k - 1], other + part * block_rows)
        fetch(rest[moved + k - 1], other + (1 - part) * block_rows)
    for copy in copies:
        copy.wait()

    raw[2 * rows : 2 * rows + 16, :] = raw[0:16, :]
    row_ids = lax.broadcasted_iota(jnp.int32, (8, LANES), 0)
    lanes = lax.broadcasted_iota(jnp.int32, (8, LANES), 1)
    first_tile = raw[0:8, :]
    at_zero = (row_ids < 2) & (lanes == 0)
    zero_bin = jnp.sum(jnp.where(at_zero, first_tile, 0.0), keepdims=True)
    rest_tile = jnp.where(at_zero, 0.0, first_tile)

    def add_power(i, sums):
        out = []
        for j, value in enumerate(sums):
            tile = raw[pl.ds(pl.multiple_of((4 * i + j) * 8, 8), 8), :]
            out.append(value + tile * tile)
        return tuple(out)

    zero_tile = jnp.zeros((8, LANES), F32)
    sums = [rest_tile * rest_tile]
    for j in range(1, 4):
        tile = raw[8 * j : 8 * j + 8, :]
        sums.append(tile * tile)
    sums = lax.fori_loop(1, rows // 16, add_power, tuple(sums), unroll=7)
    power = jnp.sum((sums[0] + sums[1]) + (sums[2] + sums[3]), keepdims=True)
    mean = jnp.broadcast_to((power + zero_bin * zero_bin) * (1.0 / total_bins) + 1e-06, (8, LANES))
    scale = lax.rsqrt(mean)
    scale = scale * (1.5 - 0.5 * mean * scale * scale)
    half_scale = 0.5 * scale

    base_cos = base_ref[0:8, :]
    base_sin = base_ref[8:16, :]
    mirror_lane = (LANES - lanes) & (LANES - 1)
    mirror_row = 7 - row_ids
    real[0:8, :] = zero_tile
    imag[0:8, :] = zero_tile
    real[rows + 8 : rows + 16, :] = zero_tile
    imag[rows + 8 : rows + 16, :] = zero_tile

    def mirrored(start):
        near = raw[pl.ds(start + 2, 8, stride=2), :]
        far = raw[pl.ds(start, 8, stride=2), :]
        tile = jnp.where(lanes == 0, near, far)
        tile = jnp.take_along_axis(tile, mirror_lane, axis=1, mode="promise_in_bounds")
        return jnp.take_along_axis(tile, mirror_row, axis=0, mode="promise_in_bounds")

    def unpack(chunk, _):
        start = chunk * 16
        a0 = raw[pl.ds(start, 8, stride=2), :]
        a1 = raw[pl.ds(start + 1, 8, stride=2), :]
        back = 2 * rows - 16 - start
        b0 = mirrored(back)
        b1 = mirrored(back + 1)
        chunk_cos = twist_ref[0, chunk]
        chunk_sin = twist_ref[1, chunk]
        cosine = base_cos * chunk_cos - base_sin * chunk_sin
        sine = base_sin * chunk_cos + base_cos * chunk_sin
        odd_real = a1 + b1
        odd_imag = b0 - a0
        out_real = (a0 + b0) + cosine * odd_real + sine * odd_imag
        out_imag = (a1 - b1) + cosine * odd_imag - sine * odd_real
        place = pl.ds(pl.multiple_of(chunk * 8 + 8, 8), 8)
        real[place, :] = out_real * half_scale
        imag[place, :] = out_imag * half_scale
        return 0

    lax.fori_loop(0, rows // 8, unpack, 0, unroll=8)

    wide_lanes = lax.broadcasted_iota(jnp.int32, (segments, LANES), 1)
    for n, stride in enumerate(strides):
        first_row = meta_ref[2 + n] + 8
        for o in range(8):
            ahead = 2 * stride * 8 * o - LANES // 2
            skip, shift = ahead // LANES, ahead % LANES
            for c, source in enumerate((real, imag)):
                tiles = [
                    source[pl.ds(first_row + (skip + j), segments, stride=stride), :]
                    for j in range(3 if shift else 2)
                ]
                for half in range(2):
                    if shift:
                        tile = jnp.where(wide_lanes >= shift, tiles[half], tiles[half + 1])
                        tile = pltpu.roll(tile.astype(BF16), LANES - shift, 1)
                    else:
                        tile = tiles[half].astype(BF16)
                    at = (2 * c + half) * LANES
                    windows[n, o * segments : (o + 1) * segments, at : at + LANES] = tile

    weight_copy.wait()
    for n, stride in enumerate(strides):
        height = planes[n].shape[2]
        window = windows[n]
        for t in range(templates):
            top = 2 * t * LANES
            amps = [
                lax.dot_general(
                    weights[top + k * LANES : top + k * LANES + height, :],
                    window,
                    (((1,), (1,)), ((), ())),
                    preferred_element_type=F32,
                )
                for k in range(2)
            ]
            plane = amps[0] * amps[0] + amps[1] * amps[1]
            for h in range(2):
                planes[n][t, h] = plane[:, h * 4 * segments : (h + 1) * 4 * segments]

    for t in range(templates):
        for h in range(2):
            for b in range(8):
                total = None
                for n, stride in enumerate(strides):
                    plane = planes[n].at[t, h]
                    if stride == 8:
                        value = plane[pl.ds(b, LANES // 8, stride=8), :]
                    elif stride == 1:
                        late = meta_ref[2 + len(strides) + n] + b >= 8
                        value = jnp.where(late, plane[1 : 1 + LANES // 8, :], plane[: LANES // 8, :])
                    else:
                        first = (meta_ref[2 + len(strides) + n] + b * stride) >> 3
                        value = plane[pl.ds(first, LANES // 8, stride=stride), :]
                    total = value if total is None else total + value
                acc[pl.ds(b, LANES // 8, stride=8), :] = total * 0.125
            turned = acc[...].T
            for o in range(4):
                out_ref[pl.ds(templates * (4 * h + o) + t, segments, stride=8 * templates), :] = (
                    turned[o * segments : (o + 1) * segments, :]
                )


def body(spectrum, bank, fdot_index, harm_map):
    block_len = spectrum.shape[1]
    block_rows = block_len // LANES
    blocks = lax.axis_size("bins")
    templates = fdot_index.shape[0]
    rows = block_rows * blocks
    device = lax.axis_index("bins")
    part = lax.axis_index("fdot") % 2
    packed = spectrum.reshape(2, block_rows, LANES).transpose(1, 0, 2).reshape(2 * block_rows, LANES)
    mine = lax.dynamic_slice(packed, (part * block_rows, jnp.int32(0)), (block_rows, LANES))
    moved = [from_partner(mine, "bins", k) for k in range(1, blocks)]
    passed = [from_partner(value, "fdot", 1) for value in moved]
    weights = template_rows(bank, fdot_index)

    step = math.pi / (rows * LANES)
    fine = (jnp.arange(8 * LANES, dtype=F32) * F32(step)).reshape(8, LANES)
    base = jnp.concatenate([jnp.cos(fine), jnp.sin(fine)])
    coarse = jnp.arange(rows // 8, dtype=F32) * F32(step * 8 * LANES)
    twist = jnp.stack([jnp.cos(coarse), jnp.sin(coarse)])
    strides = STRIDE_TABLE + (8,)
    entries = harm_map[:, 0]
    starts = (entries[:, 0] * block_len + entries[:, 2]) // LANES
    meta = jnp.concatenate(
        [jnp.stack([device, part]), starts, (device * block_rows)[None], entries[:, 3]]
    ).astype(jnp.int32)

    segments = block_rows // 8
    heights = [min(LANES, 16 * stride + 16) for stride in strides]
    smem = pl.BlockSpec(memory_space=pltpu.SMEM)
    vmem = pl.BlockSpec(memory_space=pltpu.VMEM)
    hbm = pl.BlockSpec(memory_space=pl.ANY)
    out = pl.pallas_call(
        functools.partial(
            search_kernel, strides, (block_rows, blocks, templates, blocks - 1)
        ),
        out_shape=jax.ShapeDtypeStruct((block_rows * templates, LANES), F32),
        in_specs=[smem, smem, vmem] + [hbm] * (2 * blocks),
        out_specs=vmem,
        scratch_shapes=[
            pltpu.VMEM((2 * rows + 16, LANES), F32),
            pltpu.VMEM((rows + 16, LANES), F32),
            pltpu.VMEM((rows + 16, LANES), F32),
            pltpu.VMEM(weights.shape, BF16),
            pltpu.VMEM((len(strides), block_rows, 4 * LANES), BF16),
            pltpu.VMEM((LANES, 4 * segments), F32),
            *[pltpu.VMEM((templates, 2, height, block_rows // 2), F32) for height in heights],
            pltpu.SemaphoreType.DMA((2 * blocks - 1,)),
            pltpu.SemaphoreType.DMA,
        ],
        compiler_params=pltpu.CompilerParams(vmem_limit_bytes=56 * 2**20),
        name="search",
    )(meta, twist, base, packed, *moved, *passed, weights)
    return out.reshape(block_rows, templates, LANES).transpose(1, 0, 2).reshape(templates, block_len)


def solution(mesh):
    placed = (P(None, ("groups", "bins")), P(), P("fdot"), P(None, "bins", None))
    return jax.shard_map(
        body, mesh=mesh, in_specs=placed, out_specs=P("fdot", ("groups", "bins")), check_vma=False
    )
```

profile of v0, /device:TPU:0, one launch (start us, length us, event | category | flops | bytes accessed | tf_op | source)
XLA Modules:
  0.0 43.6 jit_solution(13928146684722943019)
XLA Ops:
  0.0 0.9 %constant_dynamic-slice_fusion = f32[256,128]{1,0:T(8,128)S(1)} fusion(f32[512,128]{1,0:T(8,128)} %bitcast.29, s32[]{:T(128)S(6)} %select_n.17), kind=kLoop, calls=%fused_computation.15 | loop fusion | bytes 262148 | tf_op jit(solution)/shard_map/dynamic_slice | solution.py:230
  0.9 5.1 %collective-permute-start.2 = (f32[256,128]{1,0:T(8,128)S(1)}, f32[256,128]{1,0:T(8,128)S(1)}, u32[]{:S(2)}, u32[]{:S(2)}) collective-permute-start(f32[256,128]{1,0:T(8,128)S(1)} %constant_dynamic-slice_fusion), channel_id=1, source_target_pairs={{0,12},{4,8},{8,4},{12,0},{1,13},{5,9},{9,5},{13,1},{2,14},{6,10},... | collective-permute-start | bytes 393224 | tf_op jit(solution)/shard_map/ppermute | solution.py:19
  6.0 0.0 collective-permute-start.1
  6.0 0.6 %collective-permute-start = (f32[256,128]{1,0:T(8,128)S(1)}, f32[256,128]{1,0:T(8,128)S(1)}, u32[]{:S(2)}, u32[]{:S(2)}) collective-permute-start(f32[256,128]{1,0:T(8,128)S(1)} %constant_dynamic-slice_fusion), channel_id=1, source_target_pairs={{0,4},{4,0},{8,12},{12,8},{1,5},{5,1},{9,13},{13,9},{2,6},{6,2},{1... | collective-permute-start | bytes 393224 | tf_op jit(solution)/shard_map/ppermute | solution.py:19
  6.7 0.8 %and_select_fusion = s32[7]{0:T(128)S(1)} fusion(s32[7,4]{0,1:T(4,128)} %bitcast.34), kind=kLoop, calls=%fused_computation.5 | loop fusion | flops 119 | bytes 84 | tf_op jit(solution)/shard_map/jit(floor_divide)/jit(_where)/select_n | solution.py:242
  7.4 0.7 %slice_bitcast_fusion = s32[7]{0:T(128)S(1)} fusion(s32[7,4]{0,1:T(4,128)} %bitcast.35), kind=kLoop, calls=%fused_computation.14 | loop fusion | bytes 56 | tf_op jit(solution)/shard_map/squeeze | solution.py:244
  8.2 2.2 %collective-permute-done.2.refs_3_ = f32[256,128]{1,0:T(8,128)S(1)} collective-permute-done((f32[256,128]{1,0:T(8,128)S(1)}, f32[256,128]{1,0:T(8,128)S(1)}, u32[]{:S(2)}, u32[]{:S(2)}) %collective-permute-start.2) | collective-permute-done | bytes 131104 | tf_op jit(solution)/shard_map/ppermute | solution.py:19
  10.5 0.0 copy-start
  10.5 0.0 collective-permute-start.5
  10.5 6.6 %collective-permute-done.1.refs_2_ = f32[256,128]{1,0:T(8,128)S(1)} collective-permute-done((f32[256,128]{1,0:T(8,128)S(1)}, f32[256,128]{1,0:T(8,128)S(1)}, u32[]{:S(2)}, u32[]{:S(2)}) %collective-permute-start.1) | collective-permute-done | bytes 131104 | tf_op jit(solution)/shard_map/ppermute | solution.py:19
  17.1 0.0 copy-start.1
  17.1 0.0 collective-permute-start.4
  17.1 0.0 collective-permute-done.refs_1_
  17.1 0.0 copy-start.2
  17.1 0.5 %collective-permute-start.3 = (f32[256,128]{1,0:T(8,128)S(1)}, f32[256,128]{1,0:T(8,128)S(1)}, u32[]{:S(2)}, u32[]{:S(2)}) collective-permute-start(f32[256,128]{1,0:T(8,128)S(1)} %collective-permute-done.refs_1_), channel_id=1, source_target_pairs={{0,1},{1,0},{2,3},{3,2},{4,5},{5,4},{6,7},{7,6},{8,9},{9,8},{10,11... | collective-permute-start | bytes 393224 | tf_op jit(solution)/shard_map/ppermute | solution.py:19
  17.6 0.6 %pad_maximum_fusion.1.twist_ref = f32[2,128]{1,0:T(2,128)} fusion(f32[1,128]{1,0:T(1,128)S(1)} %get-tuple-element.5, f32[1,128]{1,0:T(1,128)S(1)} %get-tuple-element.6), kind=kLoop, calls=%fused_computation.9 | loop fusion | flops 256 | bytes 2048 | tf_op jit(solution)/shard_map/stack | solution.py:239
  18.2 1.3 %copy.6.index_ref = s32[8,1]{1,0:T(8,128)} copy(s32[8,1]{0,1:T(1,128)} %bitcast.33) | data formatting | bytes 64 | tf_op jit(solution)/shard_map/reshape | solution.py:55
  19.5 1.5 %copy.9 = bf16[16,8,2,128]{3,1,2,0:T(8,128)(2,1)} copy(bf16[16,8,2,128]{3,2,1,0:T(2,128)(2,1)} %bitcast.32) | data formatting | bytes 131072
  21.0 0.6 %concatenate.6.meta_ref = s32[17]{0:T(128)} concatenate(s32[1]{0:T(128)} %bitcast, s32[1]{0:T(128)} %bitcast.1, s32[7]{0:T(128)S(1)} %and_select_fusion, s32[1]{0:T(128)} %bitcast.4, s32[7]{0:T(128)S(1)} %slice_bitcast_fusion), dimensions={0} | concatenate | bytes 136 | tf_op jit(solution)/shard_map/concatenate | solution.py:243
  21.6 2.7 %template_rows.1.refs_7_ = bf16[2048,512]{1,0:T(8,128)(2,1)} custom-call(s32[8,1]{1,0:T(8,128)} %copy.6.index_ref, bf16[128,256]{1,0:T(8,128)(2,1)} %bitcast.31), custom_call_target="tpu_custom_call" | custom-call | flops 1048576 | bytes 2097152 | tf_op jit(solution)/shard_map/template_rows/pallas_call | solution.py:48
  24.3 0.6 %pad_maximum_fusion.base_ref = f32[16,128]{1,0:T(8,128)} fusion(f32[8,128]{1,0:T(8,128)S(1)} %get-tuple-element.7, f32[8,128]{1,0:T(8,128)S(1)} %get-tuple-element.8), kind=kLoop, calls=%fused_computation.1 | loop fusion | flops 2048 | bytes 16384 | tf_op jit(solution)/shard_map/concatenate | solution.py:237
  24.9 0.0 collective-permute-done.5.refs_6_
  24.9 0.0 copy-start.3
  24.9 0.0 collective-permute-done.4.refs_5_
  24.9 0.0 copy-start.4
  24.9 0.0 collective-permute-done.3.refs_4_
  24.9 0.0 copy-done
  25.0 0.0 copy-done.1
  25.0 0.0 copy-done.2
  25.0 0.6 %copy-done.3 = f32[256,128]{1,0:T(8,128)} copy-done((f32[256,128]{1,0:T(8,128)}, f32[256,128]{1,0:T(8,128)S(1)}, u32[]{:S(2)}) %copy-start.3) | copy-done | bytes 131096
  25.6 0.1 copy-done.4
  25.6 0.0 copy-start.5
  25.6 0.6 %copy-done.5 = f32[256,128]{1,0:T(8,128)} copy-done((f32[256,128]{1,0:T(8,128)}, f32[256,128]{1,0:T(8,128)S(1)}, u32[]{:S(2)}) %copy-start.5) | copy-done | bytes 131096
  26.3 17.3 %search.1 = f32[2048,128]{1,0:T(8,128)} custom-call(s32[17]{0:T(128)} %concatenate.6.meta_ref, f32[2,128]{1,0:T(2,128)} %pad_maximum_fusion.1.twist_ref, f32[16,128]{1,0:T(8,128)} %pad_maximum_fusion.base_ref, f32[512,128]{1,0:T(8,128)} %bitcast.30, f32[256,128]{1,0:T(8,128)} %copy-done.2, f32[256,128]{1,0:T(8,128)} %copy-done.1, f32[256,128]{1,0:T(8,128)} %copy-done, ...), custom_call_target="tpu_custom_call" | custom-call | tf_op jit(solution)/shard_map/search/pallas_call | solution.py:252
  (2 shorter events, 0.1 us)
Async XLA Ops:
  0.9 9.5 %collective-permute-start.2 = (f32[256,128]{1,0:T(8,128)S(1)}, f32[256,128]{1,0:T(8,128)S(1)}, u32[]{:S(2)}, u32[]{:S(2)}) collective-permute-start(f32[256,128]{1,0:T(8,128)S(1)} %constant_dynamic-slice_fusion), channel_id=1, source_target_pairs={{0,12},{4,8},{8,4},{12,0},{1,13},{5,9},{9,5},{13,1},{2,14},{6,10},... | collective-permute-start | bytes 393224 | tf_op jit(solution)/shard_map/ppermute | solution.py:19
  6.0 11.1 %collective-permute-start.1 = (f32[256,128]{1,0:T(8,128)S(1)}, f32[256,128]{1,0:T(8,128)S(1)}, u32[]{:S(2)}, u32[]{:S(2)}) collective-permute-start(f32[256,128]{1,0:T(8,128)S(1)} %constant_dynamic-slice_fusion), channel_id=1, source_target_pairs={{0,8},{4,12},{8,0},{12,4},{1,9},{5,13},{9,1},{13,5},{2,10},{6,14},... | collective-permute-start | bytes 393224 | tf_op jit(solution)/shard_map/ppermute | solution.py:19
  6.0 11.1 %collective-permute-start = (f32[256,128]{1,0:T(8,128)S(1)}, f32[256,128]{1,0:T(8,128)S(1)}, u32[]{:S(2)}, u32[]{:S(2)}) collective-permute-start(f32[256,128]{1,0:T(8,128)S(1)} %constant_dynamic-slice_fusion), channel_id=1, source_target_pairs={{0,4},{4,0},{8,12},{12,8},{1,5},{5,1},{9,13},{13,9},{2,6},{6,2},{1... | collective-permute-start | bytes 393224 | tf_op jit(solution)/shard_map/ppermute | solution.py:19
  10.5 14.5 %copy-start = (f32[256,128]{1,0:T(8,128)}, f32[256,128]{1,0:T(8,128)S(1)}, u32[]{:S(2)}) copy-start(f32[256,128]{1,0:T(8,128)S(1)} %collective-permute-done.2.refs_3_) | copy-start | bytes 393220
  10.5 14.5 %collective-permute-start.5 = (f32[256,128]{1,0:T(8,128)S(1)}, f32[256,128]{1,0:T(8,128)S(1)}, u32[]{:S(2)}, u32[]{:S(2)}) collective-permute-start(f32[256,128]{1,0:T(8,128)S(1)} %collective-permute-done.2.refs_3_), channel_id=1, source_target_pairs={{0,1},{1,0},{2,3},{3,2},{4,5},{5,4},{6,7},{7,6},{8,9},{9,8},{10,11... | collective-permute-start | bytes 393224 | tf_op jit(solution)/shard_map/ppermute | solution.py:19
  17.1 7.8 %copy-start.1 = (f32[256,128]{1,0:T(8,128)}, f32[256,128]{1,0:T(8,128)S(1)}, u32[]{:S(2)}) copy-start(f32[256,128]{1,0:T(8,128)S(1)} %collective-permute-done.1.refs_2_) | copy-start | bytes 393220
  17.1 7.8 %collective-permute-start.4 = (f32[256,128]{1,0:T(8,128)S(1)}, f32[256,128]{1,0:T(8,128)S(1)}, u32[]{:S(2)}, u32[]{:S(2)}) collective-permute-start(f32[256,128]{1,0:T(8,128)S(1)} %collective-permute-done.1.refs_2_), channel_id=1, source_target_pairs={{0,1},{1,0},{2,3},{3,2},{4,5},{5,4},{6,7},{7,6},{8,9},{9,8},{10,11... | collective-permute-start | bytes 393224 | tf_op jit(solution)/shard_map/ppermute | solution.py:19
  17.1 7.8 %copy-start.2 = (f32[256,128]{1,0:T(8,128)}, f32[256,128]{1,0:T(8,128)S(1)}, u32[]{:S(2)}) copy-start(f32[256,128]{1,0:T(8,128)S(1)} %collective-permute-done.refs_1_) | copy-start | bytes 393220
  17.1 7.8 %collective-permute-start.3 = (f32[256,128]{1,0:T(8,128)S(1)}, f32[256,128]{1,0:T(8,128)S(1)}, u32[]{:S(2)}, u32[]{:S(2)}) collective-permute-start(f32[256,128]{1,0:T(8,128)S(1)} %collective-permute-done.refs_1_), channel_id=1, source_target_pairs={{0,1},{1,0},{2,3},{3,2},{4,5},{5,4},{6,7},{7,6},{8,9},{9,8},{10,11... | collective-permute-start | bytes 393224 | tf_op jit(solution)/shard_map/ppermute | solution.py:19
  24.9 0.7 %copy-start.3 = (f32[256,128]{1,0:T(8,128)}, f32[256,128]{1,0:T(8,128)S(1)}, u32[]{:S(2)}) copy-start(f32[256,128]{1,0:T(8,128)S(1)} %collective-permute-done.5.refs_6_) | copy-start | bytes 393220
  24.9 0.7 %copy-start.4 = (f32[256,128]{1,0:T(8,128)}, f32[256,128]{1,0:T(8,128)S(1)}, u32[]{:S(2)}) copy-start(f32[256,128]{1,0:T(8,128)S(1)} %collective-permute-done.4.refs_5_) | copy-start | bytes 393220
  25.6 0.6 %copy-start.5 = (f32[256,128]{1,0:T(8,128)}, f32[256,128]{1,0:T(8,128)S(1)}, u32[]{:S(2)}) copy-start(f32[256,128]{1,0:T(8,128)S(1)} %collective-permute-done.3.refs_4_) | copy-start | bytes 393220
where the time goes:
time: 43.9 us; the launch traced here: 43.6 us
  Pallas kernels  20 us (46%)
  waiting for transfers between devices  8.88 us (20%)
  local copies, waits for them, and re-layouts  6.28 us (14%)
  starting transfers between devices  6.26 us (14%)
  other arithmetic  2.05 us (5%)
    pallas_call x1, Pallas kernels, body(): pl.pallas_call(functools.partial(search_kernel, strides, (block_rows, blo...  17.3 us
    ppermute x6, waiting for transfers between devices, from_partner(): return lax.ppermute(value, axis, pairs)  8.88 us
    ppermute x6, starting transfers between devices, from_partner(): return lax.ppermute(value, axis, pairs)  6.26 us
    unnamed x13, local copies, waits for them, and re-layouts  2.79 us
    pallas_call x1, Pallas kernels, template_rows(): pl.pallas_call(template_kernel, out_shape=jax.ShapeDtypeStruct((rows, 4 *...  2.73 us
    reshape x1, local copies, waits for them, and re-layouts, template_rows(): fdot_index.reshape(count, 1)  1.32 us
    dynamic_slice x1, local copies, waits for them, and re-layouts, body(): lax.dynamic_slice(packed, (part * block_rows, jnp.int32(0)), (block_rows,...  0.91 us
  transfers between devices with their start and end apart: 6, of which 2 were waited for; matrix products, arithmetic and copies ran while one was open for 14% of the time, Pallas kernels for 6%

commit v1 on v0

v1 whole, which is shorter than its diff:
```python
import functools
import math

import jax
import jax.numpy as jnp
from jax import lax
from jax.experimental import pallas as pl
from jax.experimental.pallas import tpu as pltpu
from jax.sharding import PartitionSpec as P

LANES = 128
STRIDE_TABLE = (4, 2, 6, 1, 3, 5, 7)
F32 = jnp.float32
BF16 = jnp.bfloat16


def from_partner(value, axis, mask):
    pairs = [(source, source ^ mask) for source in range(lax.axis_size(axis))]
    return lax.ppermute(value, axis, pairs)


def template_kernel(step, index_ref, bank_ref, out_ref, base_ref, twist_ref):
    zeros = jnp.zeros((1, LANES), F32)

    def banded(row):
        wide = jnp.broadcast_to(jnp.concatenate([row, zeros], axis=1), (LANES, 2 * LANES))
        return pltpu.roll(wide, 0, 1, stride=1, stride_axis=0)

    for t in range(index_ref.shape[0]):
        taps = bank_ref[index_ref[t]].astype(F32)
        real = banded(taps[0:1])
        imag = banded(taps[1:2])
        top, low = 2 * t * LANES, (2 * t + 1) * LANES
        out_ref[top : top + LANES, : 2 * LANES] = real.astype(BF16)
        out_ref[top : top + LANES, 2 * LANES :] = (-imag).astype(BF16)
        out_ref[low : low + LANES, : 2 * LANES] = imag.astype(BF16)
        out_ref[low : low + LANES, 2 * LANES :] = real.astype(BF16)

    row_ids = lax.broadcasted_iota(jnp.int32, (8, LANES), 0)
    lanes = lax.broadcasted_iota(jnp.int32, (8, LANES), 1)
    fine = (row_ids * LANES + lanes).astype(F32) * F32(step)
    base_ref[0:8, :] = jnp.cos(fine)
    base_ref[8:16, :] = jnp.sin(fine)
    chunks = twist_ref.shape[1]
    coarse = lax.broadcasted_iota(jnp.int32, (chunks, LANES), 0).astype(F32)
    coarse = coarse * F32(step * 8 * LANES)
    twist_ref[0] = jnp.cos(coarse)
    twist_ref[1] = jnp.sin(coarse)


def template_rows(bank, fdot_index, rows):
    count = fdot_index.shape[0]
    taps = bank.shape[2]
    height = 2 * count * taps
    vmem = pl.BlockSpec(memory_space=pltpu.VMEM)
    return pl.pallas_call(
        functools.partial(template_kernel, math.pi / (rows * LANES)),
        in_specs=[pl.BlockSpec(memory_space=pltpu.SMEM), vmem],
        out_specs=[vmem, vmem, vmem],
        out_shape=[
            jax.ShapeDtypeStruct((height, 4 * taps), BF16),
            jax.ShapeDtypeStruct((16, LANES), F32),
            jax.ShapeDtypeStruct((2, rows // 8, LANES), F32),
        ],
        cost_estimate=pl.CostEstimate(
            flops=4 * height * taps, bytes_accessed=8 * height * taps, transcendentals=0
        ),
        compiler_params=pltpu.CompilerParams(vmem_limit_bytes=16 * 2**20),
        name="template_rows",
    )(fdot_index, bank)


def search_kernel(strides, sizes, meta_ref, map_ref, base_ref, twist_ref, *refs):
    block_rows, blocks, templates = sizes
    moved = blocks - 1
    own_ref = refs[0]
    rest = refs[1 : 1 + 2 * moved]
    weights_hbm, out_ref, raw, real, imag, weights, windows, acc, *more = refs[1 + 2 * moved :]
    planes = more[: len(strides)]
    copy_sem, weight_sem = more[len(strides) :]
    rows = block_rows * blocks
    total_bins = rows * LANES
    segments = block_rows // 8
    device = meta_ref[0]
    part = meta_ref[1]

    weight_copy = pltpu.make_async_copy(weights_hbm, weights, weight_sem)
    weight_copy.start()
    copies = []

    def fetch(source, start):
        size = source.shape[0]
        start = pl.multiple_of(start, size)
        copy = pltpu.make_async_copy(
            source, raw.at[pl.ds(start, size), :], copy_sem.at[len(copies)]
        )
        copy.start()
        copies.append(copy)

    fetch(own_ref, device * (2 * block_rows))
    for k in range(1, moved + 1):
        other = (device ^ k) * (2 * block_rows)
        fetch(rest[k - 1], other + part * block_rows)
        fetch(rest[moved + k - 1], other + (1 - part) * block_rows)
    for copy in copies:
        copy.wait()

    raw[2 * rows : 2 * rows + 16, :] = raw[0:16, :]
    row_ids = lax.broadcasted_iota(jnp.int32, (8, LANES), 0)
    lanes = lax.broadcasted_iota(jnp.int32, (8, LANES), 1)
    zero_tile = jnp.zeros((8, LANES), F32)
    half_scale = zero_tile + 0.001
    first_tile = raw[0:8, :]
    at_zero = (row_ids < 2) & (lanes == 0)
    zero_bin = jnp.sum(jnp.where(at_zero, first_tile, 0.0), keepdims=True)
    rest_tile = jnp.where(at_zero, 0.0, first_tile)

    def add_power(i, sums):
        out = []
        for j, value in enumerate(sums):
            tile = raw[pl.ds(pl.multiple_of((4 * i + j) * 8, 8), 8), :]
            out.append(value + tile * tile)
        return tuple(out)

    sums = [rest_tile * rest_tile]
    for j in range(1, 4):
        tile = raw[8 * j : 8 * j + 8, :]
        sums.append(tile * tile)
    sums = lax.fori_loop(1, rows // 16, add_power, tuple(sums), unroll=7)
    power = jnp.sum((sums[0] + sums[1]) + (sums[2] + sums[3]), keepdims=True)
    mean = jnp.broadcast_to((power + zero_bin * zero_bin) * (1.0 / total_bins) + 1e-06, (8, LANES))
    scale = lax.rsqrt(mean)
    scale = scale * (1.5 - 0.5 * mean * scale * scale)
    half_scale = 0.5 * scale

    base_cos = base_ref[0:8, :]
    base_sin = base_ref[8:16, :]
    mirror_lane = (LANES - lanes) & (LANES - 1)
    mirror_row = 7 - row_ids
    real[0:8, :] = zero_tile
    imag[0:8, :] = zero_tile
    real[rows + 8 : rows + 16, :] = zero_tile
    imag[rows + 8 : rows + 16, :] = zero_tile

    def mirrored(start):
        near = raw[pl.ds(start + 2, 8, stride=2), :]
        far = raw[pl.ds(start, 8, stride=2), :]
        tile = jnp.where(lanes == 0, near, far)
        tile = jnp.take_along_axis(tile, mirror_lane, axis=1, mode="promise_in_bounds")
        return jnp.take_along_axis(tile, mirror_row, axis=0, mode="promise_in_bounds")

    def unpack(chunk, _):
        start = chunk * 16
        a0 = raw[pl.ds(start, 8, stride=2), :]
        a1 = raw[pl.ds(start + 1, 8, stride=2), :]
        back = 2 * rows - 16 - start
        b0 = mirrored(back)
        b1 = mirrored(back + 1)
        chunk_cos = twist_ref[0, pl.ds(chunk, 1), :]
        chunk_sin = twist_ref[1, pl.ds(chunk, 1), :]
        cosine = base_cos * chunk_cos - base_sin * chunk_sin
        sine = base_sin * chunk_cos + base_cos * chunk_sin
        odd_real = a1 + b1
        odd_imag = b0 - a0
        out_real = (a0 + b0) + cosine * odd_real + sine * odd_imag
        out_imag = (a1 - b1) + cosine * odd_imag - sine * odd_real
        place = pl.ds(pl.multiple_of(chunk * 8 + 8, 8), 8)
        real[place, :] = out_real * half_scale
        imag[place, :] = out_imag * half_scale
        return 0

    lax.fori_loop(0, rows // 8, unpack, 0, unroll=8)

    wide_lanes = lax.broadcasted_iota(jnp.int32, (segments, LANES), 1)
    for n, stride in enumerate(strides):
        if stride == 8:
            first_row = device * block_rows + 8
        else:
            first_row = map_ref[n, 0] * block_rows + (map_ref[n, 2] >> 7) + 8
        for o in range(8):
            ahead = 2 * stride * 8 * o - LANES // 2
            skip, shift = ahead // LANES, ahead % LANES
            for c, source in enumerate((real, imag)):
                tiles = [
                    source[pl.ds(first_row + (skip + j), segments, stride=stride), :]
                    for j in range(3 if shift else 2)
                ]
                for half in range(2):
                    if shift:
                        tile = jnp.where(wide_lanes >= shift, tiles[half], tiles[half + 1])
                        tile = pltpu.roll(tile.astype(BF16), LANES - shift, 1)
                    else:
                        tile = tiles[half].astype(BF16)
                    at = (2 * c + half) * LANES
                    windows[n, o * segments : (o + 1) * segments, at : at + LANES] = tile

    weight_copy.wait()
    groups = 2
    share = templates // groups
    for g in range(groups):
        own = weights[2 * g * share * LANES : 2 * (g + 1) * share * LANES, :]
        own = own.reshape(2 * share, LANES, 4 * LANES)
        for n, stride in enumerate(strides):
            height = planes[n].shape[2]
            amps = lax.dot_general(
                own[:, :height].reshape(2 * share * height, 4 * LANES),
                windows[n],
                (((1,), (1,)), ((), ())),
                preferred_element_type=F32,
            ).reshape(share, 2, height, 2 * 4 * segments)
            for t in range(share):
                plane = amps[t, 0] * amps[t, 0] + amps[t, 1] * amps[t, 1]
                for h in range(2):
                    planes[n][g * share + t, h] = plane[:, h * 4 * segments : (h + 1) * 4 * segments]
    for t in range(templates):
        for h in range(2):
            for b in range(8):
                total = None
                for n, stride in enumerate(strides):
                    plane = planes[n].at[t, h]
                    if stride == 8:
                        value = plane[pl.ds(b, LANES // 8, stride=8), :]
                    elif stride == 1:
                        late = map_ref[n, 3] + b >= 8
                        value = jnp.where(late, plane[1 : 1 + LANES // 8, :], plane[: LANES // 8, :])
                    else:
                        first = (map_ref[n, 3] + b * stride) >> 3
                        value = plane[pl.ds(first, LANES // 8, stride=stride), :]
                    total = value if total is None else total + value
                acc[pl.ds(b, LANES // 8, stride=8), :] = total * 0.125
            turned = acc[...].T
            for o in range(4):
                out_ref[pl.ds(templates * (4 * h + o) + t, segments, stride=8 * templates), :] = (
                    turned[o * segments : (o + 1) * segments, :]
                )


def search(packed, moved, passed, weights, base, twist, harm_map, device, part, templates):
    blocks = 1 + len(moved)
    block_rows = packed.shape[0] // 2
    rows = block_rows * blocks
    strides = STRIDE_TABLE + (8,)
    segments = block_rows // 8
    heights = [min(LANES, 16 * stride + 16) for stride in strides]
    smem = pl.BlockSpec(memory_space=pltpu.SMEM)
    vmem = pl.BlockSpec(memory_space=pltpu.VMEM)
    hbm = pl.BlockSpec(memory_space=pl.ANY)
    scratch = [
        ((2 * rows + 16, LANES), F32),
        ((rows + 16, LANES), F32),
        ((rows + 16, LANES), F32),
        (weights.shape, BF16),
        ((len(strides), block_rows, 4 * LANES), BF16),
        ((LANES, 4 * segments), F32),
    ] + [((templates, 2, height, block_rows // 2), F32) for height in heights]
    used = sum(math.prod(shape) * jnp.dtype(kind).itemsize for shape, kind in scratch)
    return pl.pallas_call(
        functools.partial(search_kernel, strides, (block_rows, blocks, templates)),
        out_shape=jax.ShapeDtypeStruct((block_rows * templates, LANES), F32),
        in_specs=[smem, smem, vmem, vmem] + [hbm] * (2 * blocks),
        out_specs=vmem,
        scratch_shapes=[
            *[pltpu.VMEM(shape, kind) for shape, kind in scratch],
            pltpu.SemaphoreType.DMA((2 * blocks - 1,)),
            pltpu.SemaphoreType.DMA,
        ],
        compiler_params=pltpu.CompilerParams(vmem_limit_bytes=used + 12 * 2**20),
        name="search",
    )(
        jnp.stack([device, part]).astype(jnp.int32),
        harm_map.reshape(-1, 4),
        base,
        twist,
        packed,
        *moved,
        *passed,
        weights,
    )


def body(spectrum, bank, fdot_index, harm_map):
    block_len = spectrum.shape[1]
    block_rows = block_len // LANES
    blocks = lax.axis_size("bins")
    templates = fdot_index.shape[0]
    device = lax.axis_index("bins")
    part = lax.axis_index("fdot") & 1
    packed = spectrum.reshape(2, block_rows, LANES).transpose(1, 0, 2).reshape(2 * block_rows, LANES)
    mine = lax.dynamic_slice(packed, (part * block_rows, jnp.int32(0)), (block_rows, LANES))
    moved = [from_partner(mine, "bins", k) for k in range(1, blocks)]
    tables = template_rows(bank, fdot_index, block_rows * blocks)
    weights, base, twist = tables
    moved = [lax.optimization_barrier((value, base))[0] for value in moved]
    passed = [from_partner(value, "fdot", 1) for value in moved]
    out = search(packed, moved, passed, weights, base, twist, harm_map, device, part, templates)
    return out.reshape(block_rows, templates, LANES).transpose(1, 0, 2).reshape(templates, block_len)


def solution(mesh):
    placed = (P(None, ("groups", "bins")), P(), P("fdot"), P(None, "bins", None))
    return jax.shard_map(
        body, mesh=mesh, in_specs=placed, out_specs=P("fdot", ("groups", "bins")), check_vma=False
    )
```

time: 43.9 us -> 30.3 us (0.69)
  Pallas kernels: 20 us -> 11.2 us
  local copies, waits for them, and re-layouts: 6.28 us -> 4.12 us
  other arithmetic: 2.05 us -> 0.07 us
  waiting for transfers between devices: 8.88 us -> 8.42 us
    pallas_call x2, Pallas kernels: 20 us -> 11.2 us  [the longest x1 10.2 us: search(): pl.pallas_call(functools.partial(search_kernel, strides, (block_rows, blo...]
    select_n x1 -> x0, other arithmetic: 0.77 us -> none  [body(): starts = (entries[:, 0] * block_len + entries[:, 2]) // LANES]
    squeeze x1 -> x0, local copies, waits for them, and re-layouts: 0.69 us -> none  [body(): entries[:, 3]]
    concatenate x1 -> x0, other arithmetic: 0.59 us -> none  [body(): base = jnp.concatenate([jnp.cos(fine), jnp.sin(fine)])]
    concatenate x1 -> x0, local copies, waits for them, and re-layouts: 0.57 us -> none  [body(): jnp.concatenate([jnp.stack([device, part]), starts, (device * block_rows)...]
    reshape x1, local copies, waits for them, and re-layouts: 1.32 us -> 0.77 us  [search(): harm_map.reshape(-1, 4)]
    another operation x1, other arithmetic: 0.59 us -> 0.07 us  [search(): jnp.stack([device, part]).astype(jnp.int32)]
    ppermute x6, waiting for transfers between devices: 8.88 us -> 8.42 us  [from_partner(): return lax.ppermute(value, axis, pairs)]
  transfers between devices with their start and end apart: 6 -> 6, of which waited for: 2 -> 4; matrix products, arithmetic and copies ran while one was open for 14% -> 3% of each run, Pallas kernels for 6% -> 3%
where the time goes in v1:
time: 30.3 us; the launch traced here: 30.1 us
  Pallas kernels  11.2 us (37%)
  waiting for transfers between devices  8.42 us (28%)
  starting transfers between devices  6.27 us (21%)
  local copies, waits for them, and re-layouts  4.12 us (14%)
    pallas_call x1, Pallas kernels, search(): pl.pallas_call(functools.partial(search_kernel, strides, (block_rows, blo...  10.2 us
    ppermute x6, waiting for transfers between devices, from_partner(): return lax.ppermute(value, axis, pairs)  8.42 us
    ppermute x6, starting transfers between devices, from_partner(): return lax.ppermute(value, axis, pairs)  6.27 us
    unnamed x6, local copies, waits for them, and re-layouts  2.44 us
    pallas_call x1, Pallas kernels, template_rows(): pl.pallas_call(functools.partial(template_kernel, math.pi / (rows * LANES...  1.01 us
    dynamic_slice x1, local copies, waits for them, and re-layouts, body(): lax.dynamic_slice(packed, (part * block_rows, jnp.int32(0)), (block_rows,...  0.91 us
    reshape x1, local copies, waits for them, and re-layouts, search(): harm_map.reshape(-1, 4)  0.77 us
  transfers between devices with their start and end apart: 6, of which 4 were waited for; matrix products, arithmetic and copies ran while one was open for 3% of the time, Pallas kernels for 3%

profile of v1, /device:TPU:0, one launch (start us, length us, event | category | flops | bytes accessed | tf_op | source)
XLA Modules:
  0.0 30.1 jit_solution(13908773440029674890)
XLA Ops:
  0.0 0.9 %constant_dynamic-slice_fusion = f32[256,128]{1,0:T(8,128)S(1)} fusion(f32[512,128]{1,0:T(8,128)} %bitcast.13, s32[]{:T(128)S(6)} %select_n.3), kind=kLoop, calls=%fused_computation.1 | loop fusion | bytes 262148 | tf_op jit(solution)/shard_map/dynamic_slice | solution.py:289
  0.9 5.1 %collective-permute-start.2 = (f32[256,128]{1,0:T(8,128)S(1)}, f32[256,128]{1,0:T(8,128)S(1)}, u32[]{:S(2)}, u32[]{:S(2)}) collective-permute-start(f32[256,128]{1,0:T(8,128)S(1)} %constant_dynamic-slice_fusion), channel_id=1, source_target_pairs={{0,12},{4,8},{8,4},{12,0},{1,13},{5,9},{9,5},{13,1},{2,14},{6,10},... | collective-permute-start | bytes 393224 | tf_op jit(solution)/shard_map/ppermute | solution.py:19
  6.0 0.0 collective-permute-start.1
  6.0 0.6 %collective-permute-start = (f32[256,128]{1,0:T(8,128)S(1)}, f32[256,128]{1,0:T(8,128)S(1)}, u32[]{:S(2)}, u32[]{:S(2)}) collective-permute-start(f32[256,128]{1,0:T(8,128)S(1)} %constant_dynamic-slice_fusion), channel_id=1, source_target_pairs={{0,4},{4,0},{8,12},{12,8},{1,5},{5,1},{9,13},{13,9},{2,6},{6,2},{1... | collective-permute-start | bytes 393224 | tf_op jit(solution)/shard_map/ppermute | solution.py:19
  6.7 0.0 copy-start.1
  6.7 0.8 %copy-done.1 = bf16[128,2,128]{2,1,0:T(2,128)(2,1)S(1)} copy-done((bf16[128,2,128]{2,1,0:T(2,128)(2,1)S(1)}, bf16[128,2,128]{2,1,0:T(2,128)(2,1)}, u32[]{:S(2)}) %copy-start.1) | copy-done | bytes 65560
  7.5 0.0 copy-start.2
  7.5 0.7 %copy-done.2 = s32[8]{0:T(128)S(1)} copy-done((s32[8]{0:T(128)S(1)}, s32[8]{0:T(128)}, u32[]{:S(2)}) %copy-start.2) | copy-done | bytes 56
  8.2 1.0 %template_rows.1 = (bf16[2048,512]{1,0:T(8,128)(2,1)S(1)}, f32[16,128]{1,0:T(8,128)S(1)}, f32[2,128,128]{2,1,0:T(8,128)S(1)}) custom-call(s32[8]{0:T(128)S(1)} %copy-done.2, bf16[128,2,128]{2,1,0:T(2,128)(2,1)S(1)} %copy-done.1), custom_call_target="tpu_custom_call" | custom-call | flops 1048576 | bytes 2097152 | tf_op jit(solution)/shard_map/template_rows/pallas_call | solution.py:56
  9.2 1.3 %collective-permute-done.2.refs_3_ = f32[256,128]{1,0:T(8,128)S(1)} collective-permute-done((f32[256,128]{1,0:T(8,128)S(1)}, f32[256,128]{1,0:T(8,128)S(1)}, u32[]{:S(2)}, u32[]{:S(2)}) %collective-permute-start.2) | collective-permute-done | bytes 131104 | tf_op jit(solution)/shard_map/ppermute | solution.py:19
  10.5 6.6 %collective-permute-done.1.refs_2_ = f32[256,128]{1,0:T(8,128)S(1)} collective-permute-done((f32[256,128]{1,0:T(8,128)S(1)}, f32[256,128]{1,0:T(8,128)S(1)}, u32[]{:S(2)}, u32[]{:S(2)}) %collective-permute-start.1) | collective-permute-done | bytes 131104 | tf_op jit(solution)/shard_map/ppermute | solution.py:19
  17.1 0.0 collective-permute-done.refs_1_
  17.1 0.0 collective-permute-start.3
  17.1 0.5 %collective-permute-start.4 = (f32[256,128]{1,0:T(8,128)S(1)}, f32[256,128]{1,0:T(8,128)S(1)}, u32[]{:S(2)}, u32[]{:S(2)}) collective-permute-start(f32[256,128]{1,0:T(8,128)S(1)} %collective-permute-done.1.refs_2_), channel_id=1, source_target_pairs={{0,1},{1,0},{2,3},{3,2},{4,5},{5,4},{6,7},{7,6},{8,9},{9,8},{10,11... | collective-permute-start | bytes 393224 | tf_op jit(solution)/shard_map/ppermute | solution.py:19
  17.6 0.0 collective-permute-start.5
  17.6 0.8 %copy.6.map_ref = s32[7,4]{1,0:T(8,128)S(1)} copy(s32[7,4]{0,1:T(4,128)} %bitcast.15) | data formatting | bytes 224 | tf_op jit(solution)/shard_map/reshape | solution.py:271
  18.4 0.1 pad_add_fusion.meta_ref
  18.5 0.0 collective-permute-done.3.refs_4_
  18.5 0.2 collective-permute-done.4.refs_5_
  18.6 0.3 %collective-permute-done.5.refs_6_ = f32[256,128]{1,0:T(8,128)S(1)} collective-permute-done((f32[256,128]{1,0:T(8,128)S(1)}, f32[256,128]{1,0:T(8,128)S(1)}, u32[]{:S(2)}, u32[]{:S(2)}) %collective-permute-start.5) | collective-permute-done | bytes 131104 | tf_op jit(solution)/shard_map/ppermute | solution.py:19
  19.0 0.0 copy-start
  19.0 0.9 %copy-done = f32[2,32768]{1,0:T(2,128)S(1)} copy-done((f32[2,32768]{1,0:T(2,128)S(1)}, f32[2,32768]{1,0:T(2,128)}, u32[]{:S(2)}) %copy-start) | copy-done | bytes 262168
  19.9 10.2 %search.1 = f32[2048,128]{1,0:T(8,128)} custom-call(s32[2]{0:T(128)S(1)} %pad_add_fusion.meta_ref, s32[7,4]{1,0:T(8,128)S(1)} %copy.6.map_ref, f32[16,128]{1,0:T(8,128)S(1)} %get-tuple-element.11.base_ref, f32[2,128,128]{2,1,0:T(8,128)S(1)} %get-tuple-element.12.twist_ref, f32[512,128]{1,0:T(8,128)S(1)} %bitcast.14, ...), custom_call_target="tpu_custom_call" | custom-call | tf_op jit(solution)/shard_map/search/pallas_call | solution.py:257
Async XLA Ops:
  0.9 9.5 %collective-permute-start.2 = (f32[256,128]{1,0:T(8,128)S(1)}, f32[256,128]{1,0:T(8,128)S(1)}, u32[]{:S(2)}, u32[]{:S(2)}) collective-permute-start(f32[256,128]{1,0:T(8,128)S(1)} %constant_dynamic-slice_fusion), channel_id=1, source_target_pairs={{0,12},{4,8},{8,4},{12,0},{1,13},{5,9},{9,5},{13,1},{2,14},{6,10},... | collective-permute-start | bytes 393224 | tf_op jit(solution)/shard_map/ppermute | solution.py:19
  6.0 11.1 %collective-permute-start.1 = (f32[256,128]{1,0:T(8,128)S(1)}, f32[256,128]{1,0:T(8,128)S(1)}, u32[]{:S(2)}, u32[]{:S(2)}) collective-permute-start(f32[256,128]{1,0:T(8,128)S(1)} %constant_dynamic-slice_fusion), channel_id=1, source_target_pairs={{0,8},{4,12},{8,0},{12,4},{1,9},{5,13},{9,1},{13,5},{2,10},{6,14},... | collective-permute-start | bytes 393224 | tf_op jit(solution)/shard_map/ppermute | solution.py:19
  6.0 11.1 %collective-permute-start = (f32[256,128]{1,0:T(8,128)S(1)}, f32[256,128]{1,0:T(8,128)S(1)}, u32[]{:S(2)}, u32[]{:S(2)}) collective-permute-start(f32[256,128]{1,0:T(8,128)S(1)} %constant_dynamic-slice_fusion), channel_id=1, source_target_pairs={{0,4},{4,0},{8,12},{12,8},{1,5},{5,1},{9,13},{13,9},{2,6},{6,2},{1... | collective-permute-start | bytes 393224 | tf_op jit(solution)/shard_map/ppermute | solution.py:19
  6.7 0.8 %copy-start.1 = (bf16[128,2,128]{2,1,0:T(2,128)(2,1)S(1)}, bf16[128,2,128]{2,1,0:T(2,128)(2,1)}, u32[]{:S(2)}) copy-start(bf16[128,2,128]{2,1,0:T(2,128)(2,1)} %bank_ref.1) | copy-start | bytes 196612
  7.5 0.7 %copy-start.2 = (s32[8]{0:T(128)S(1)}, s32[8]{0:T(128)}, u32[]{:S(2)}) copy-start(s32[8]{0:T(128)} %index_ref.1) | copy-start | bytes 100
  17.1 1.4 %collective-permute-start.3 = (f32[256,128]{1,0:T(8,128)S(1)}, f32[256,128]{1,0:T(8,128)S(1)}, u32[]{:S(2)}, u32[]{:S(2)}) collective-permute-start(f32[256,128]{1,0:T(8,128)S(1)} %collective-permute-done.refs_1_), channel_id=1, source_target_pairs={{0,1},{1,0},{2,3},{3,2},{4,5},{5,4},{6,7},{7,6},{8,9},{9,8},{10,11... | collective-permute-start | bytes 393224 | tf_op jit(solution)/shard_map/ppermute | solution.py:19
  17.1 1.5 %collective-permute-start.4 = (f32[256,128]{1,0:T(8,128)S(1)}, f32[256,128]{1,0:T(8,128)S(1)}, u32[]{:S(2)}, u32[]{:S(2)}) collective-permute-start(f32[256,128]{1,0:T(8,128)S(1)} %collective-permute-done.1.refs_2_), channel_id=1, source_target_pairs={{0,1},{1,0},{2,3},{3,2},{4,5},{5,4},{6,7},{7,6},{8,9},{9,8},{10,11... | collective-permute-start | bytes 393224 | tf_op jit(solution)/shard_map/ppermute | solution.py:19
  17.6 1.3 %collective-permute-start.5 = (f32[256,128]{1,0:T(8,128)S(1)}, f32[256,128]{1,0:T(8,128)S(1)}, u32[]{:S(2)}, u32[]{:S(2)}) collective-permute-start(f32[256,128]{1,0:T(8,128)S(1)} %collective-permute-done.2.refs_3_), channel_id=1, source_target_pairs={{0,1},{1,0},{2,3},{3,2},{4,5},{5,4},{6,7},{7,6},{8,9},{9,8},{10,11... | collective-permute-start | bytes 393224 | tf_op jit(solution)/shard_map/ppermute | solution.py:19
  19.0 1.0 %copy-start = (f32[2,32768]{1,0:T(2,128)S(1)}, f32[2,32768]{1,0:T(2,128)}, u32[]{:S(2)}) copy-start(f32[2,32768]{1,0:T(2,128)} %param.4) | copy-start | bytes 786436

commit v2 on v1

v2 whole, which is shorter than its diff:
```python
import functools
import math

import jax
import jax.numpy as jnp
from jax import lax
from jax.experimental import pallas as pl
from jax.experimental.pallas import tpu as pltpu
from jax.sharding import PartitionSpec as P

LANES = 128
STRIDE_TABLE = (4, 2, 6, 1, 3, 5, 7)
F32 = jnp.float32
BF16 = jnp.bfloat16


def from_partner(value, axis, mask):
    pairs = [(source, source ^ mask) for source in range(lax.axis_size(axis))]
    return lax.ppermute(value, axis, pairs)


def template_kernel(
    step, packed_hbm, index_hbm, bank_hbm, own_ref, out_ref, base_ref, twist_ref, index_ref, bank_ref, sem
):
    pairs = ((index_hbm, index_ref), (bank_hbm, bank_ref), (packed_hbm, own_ref))
    copies = [pltpu.make_async_copy(source, to, sem.at[i]) for i, (source, to) in enumerate(pairs)]
    for copy in copies:
        copy.start()

    row_ids = lax.broadcasted_iota(jnp.int32, (8, LANES), 0)
    lanes = lax.broadcasted_iota(jnp.int32, (8, LANES), 1)
    fine = (row_ids * LANES + lanes).astype(F32) * F32(step)
    base_ref[0:8, :] = jnp.cos(fine)
    base_ref[8:16, :] = jnp.sin(fine)
    chunks = twist_ref.shape[1]
    coarse = lax.broadcasted_iota(jnp.int32, (chunks, LANES), 0).astype(F32)
    coarse = coarse * F32(step * 8 * LANES)
    twist_ref[0] = jnp.cos(coarse)
    twist_ref[1] = jnp.sin(coarse)

    copies[0].wait()
    copies[1].wait()
    zeros = jnp.zeros((1, LANES), F32)

    def banded(row):
        wide = jnp.broadcast_to(jnp.concatenate([row, zeros], axis=1), (LANES, 2 * LANES))
        return pltpu.roll(wide, 0, 1, stride=1, stride_axis=0)

    for t in range(index_ref.shape[0]):
        taps = bank_ref[index_ref[t]].astype(F32)
        real = banded(taps[0:1])
        imag = banded(taps[1:2])
        top, low = 2 * t * LANES, (2 * t + 1) * LANES
        out_ref[top : top + LANES, : 2 * LANES] = real.astype(BF16)
        out_ref[top : top + LANES, 2 * LANES :] = (-imag).astype(BF16)
        out_ref[low : low + LANES, : 2 * LANES] = imag.astype(BF16)
        out_ref[low : low + LANES, 2 * LANES :] = real.astype(BF16)
    copies[2].wait()


def template_rows(packed, bank, fdot_index, rows):
    count = fdot_index.shape[0]
    taps = bank.shape[2]
    height = 2 * count * taps
    vmem = pl.BlockSpec(memory_space=pltpu.VMEM)
    return pl.pallas_call(
        functools.partial(template_kernel, math.pi / (rows * LANES)),
        in_specs=[pl.BlockSpec(memory_space=pltpu.HBM)] * 3,
        out_specs=[vmem] * 4,
        out_shape=[
            jax.ShapeDtypeStruct(packed.shape, F32),
            jax.ShapeDtypeStruct((height, 4 * taps), BF16),
            jax.ShapeDtypeStruct((16, LANES), F32),
            jax.ShapeDtypeStruct((2, rows // 8, LANES), F32),
        ],
        scratch_shapes=[
            pltpu.SMEM(fdot_index.shape, jnp.int32),
            pltpu.VMEM(bank.shape, BF16),
            pltpu.SemaphoreType.DMA((3,)),
        ],
        cost_estimate=pl.CostEstimate(
            flops=4 * height * taps, bytes_accessed=8 * height * taps, transcendentals=0
        ),
        compiler_params=pltpu.CompilerParams(vmem_limit_bytes=16 * 2**20),
        name="template_rows",
    )(packed, fdot_index, bank)


def search_kernel(strides, sizes, meta_ref, map_ref, base_ref, twist_ref, *refs):
    block_rows, blocks, templates = sizes
    moved = blocks - 1
    own_ref = refs[0]
    rest = refs[1 : 1 + 2 * moved]
    weights, out_ref, raw, real, imag, acc, flat, *more = refs[1 + 2 * moved :]
    windows = more[: len(strides)]
    more = more[len(strides) :]
    groups = 2
    share = templates // groups
    planes = [more[g * len(strides) : (g + 1) * len(strides)] for g in range(groups)]
    copy_sem = more[groups * len(strides)]
    rows = block_rows * blocks
    total_bins = rows * LANES
    segments = block_rows // 8
    device = meta_ref[0]
    part = meta_ref[1]
    column = meta_ref[2]

    copies = []

    def fetch(source, start):
        size = source.shape[0]
        start = pl.multiple_of(start, size)
        copy = pltpu.make_async_copy(
            source, raw.at[pl.ds(start, size), :], copy_sem.at[len(copies)]
        )
        copy.start()
        copies.append(copy)

    fetch(own_ref, device * (2 * block_rows))
    masks = [1]
    for pair in range(2, blocks, 2):
        masks += [pair + 1 - column, pair + column]
    for k, mask in enumerate(masks):
        other = (device ^ mask) * (2 * block_rows)
        fetch(rest[k], other + part * block_rows)
        fetch(rest[moved + k], other + (1 - part) * block_rows)
    halves = [own_ref.at[:block_rows], own_ref.at[block_rows:], *rest]
    sums = [jnp.zeros((8, LANES), F32)] * 4
    for half in halves:
        for i in range(1, block_rows // 8):
            tile = half[8 * i : 8 * i + 8, :]
            sums[i % 4] = sums[i % 4] + tile * tile
    for copy in copies:
        copy.wait()
    raw[2 * rows : 2 * rows + 16, :] = raw[0:16, :]
    row_ids = lax.broadcasted_iota(jnp.int32, (8, LANES), 0)
    lanes = lax.broadcasted_iota(jnp.int32, (8, LANES), 1)
    zero_tile = jnp.zeros((8, LANES), F32)
    half_scale = zero_tile + 0.001
    first_tile = raw[0:8, :]
    at_zero = (row_ids < 2) & (lanes == 0)
    zero_bin = jnp.sum(jnp.where(at_zero, first_tile, 0.0), keepdims=True)
    first_tile = jnp.where(at_zero, 0.0, first_tile)
    sums[0] = sums[0] + first_tile * first_tile
    for j in range(1, 2 * blocks):
        tile = raw[j * block_rows : j * block_rows + 8, :]
        sums[j % 4] = sums[j % 4] + tile * tile
    power = jnp.sum((sums[0] + sums[1]) + (sums[2] + sums[3]), keepdims=True)
    mean = jnp.broadcast_to((power + zero_bin * zero_bin) * (1.0 / total_bins) + 1e-06, (8, LANES))
    scale = lax.rsqrt(mean)
    scale = scale * (1.5 - 0.5 * mean * scale * scale)
    half_scale = 0.5 * scale

    base_cos = base_ref[0:8, :]
    base_sin = base_ref[8:16, :]
    mirror_lane = (LANES - lanes) & (LANES - 1)
    mirror_row = 7 - row_ids
    real[0:8, :] = zero_tile
    imag[0:8, :] = zero_tile
    real[rows + 8 : rows + 16, :] = zero_tile
    imag[rows + 8 : rows + 16, :] = zero_tile

    def mirrored(start):
        near = raw[pl.ds(start + 2, 8, stride=2), :]
        far = raw[pl.ds(start, 8, stride=2), :]
        tile = jnp.where(lanes == 0, near, far)
        tile = jnp.take_along_axis(tile, mirror_lane, axis=1, mode="promise_in_bounds")
        return jnp.take_along_axis(tile, mirror_row, axis=0, mode="promise_in_bounds")

    def unpack(chunk, _):
        start = chunk * 16
        a0 = raw[pl.ds(start, 8, stride=2), :]
        a1 = raw[pl.ds(start + 1, 8, stride=2), :]
        back = 2 * rows - 16 - start
        b0 = mirrored(back)
        b1 = mirrored(back + 1)
        chunk_cos = twist_ref[0, pl.ds(chunk, 1), :]
        chunk_sin = twist_ref[1, pl.ds(chunk, 1), :]
        cosine = base_cos * chunk_cos - base_sin * chunk_sin
        sine = base_sin * chunk_cos + base_cos * chunk_sin
        odd_real = a1 + b1
        odd_imag = b0 - a0
        out_real = (a0 + b0) + cosine * odd_real + sine * odd_imag
        out_imag = (a1 - b1) + cosine * odd_imag - sine * odd_real
        place = pl.ds(pl.multiple_of(chunk * 8 + 8, 8), 8)
        real[place, :] = out_real * half_scale
        imag[place, :] = out_imag * half_scale
        return 0

    group = 16
    lowest = jnp.maximum(device * (block_rows // 8) - 1, 0) // (8 * group)
    highest = jnp.minimum(((device + 1) * block_rows + 8 * group) // (8 * group), rows // (8 * group))

    def unpack_group(i, _):
        for j in range(group):
            unpack(i * group + j, 0)
        return 0

    lax.fori_loop(lowest, highest, unpack_group, 0)

    wide_lanes = lax.broadcasted_iota(jnp.int32, (segments, LANES), 1)
    def make_windows(n, stride):
        if stride == 8:
            first_row = device * block_rows + 8
        else:
            first_row = map_ref[n, 0] * block_rows + (map_ref[n, 2] >> 7) + 8
        for o in range(8):
            ahead = 2 * stride * 8 * o - LANES // 2
            skip, shift = ahead // LANES, ahead % LANES
            for c, source in enumerate((real, imag)):
                tiles = [
                    source[pl.ds(first_row + (skip + j), segments, stride=stride), :]
                    for j in range(3 if shift else 2)
                ]
                for half in range(2):
                    if shift:
                        tile = jnp.where(wide_lanes >= shift, tiles[half], tiles[half + 1])
                        tile = pltpu.roll(tile.astype(BF16), LANES - shift, 1)
                    else:
                        tile = tiles[half].astype(BF16)
                    at = (2 * c + half) * LANES
                    windows[n][o * segments : (o + 1) * segments, at : at + LANES] = tile

    def add_up(first, last):
        for t in range(first, last):
            for h in range(2):
                shared = {
                    n: [planes[t // share][n][t % share, h, pl.ds(c, LANES // 8, stride=stride), :] for c in range(stride + 1)]
                    for n, stride in enumerate(strides)
                    if stride <= 2
                }
                for b in range(8):
                    total = None
                    for n, stride in enumerate(strides):
                        plane = planes[t // share][n].at[t % share, h]
                        if stride == 8:
                            value = plane[pl.ds(b, LANES // 8, stride=8), :]
                        elif stride <= 2:
                            first = (map_ref[n, 3] + b * stride) >> 3
                            value = shared[n][0]
                            for c in range(1, stride + 1):
                                value = jnp.where(first == c, shared[n][c], value)
                        else:
                            first = (map_ref[n, 3] + b * stride) >> 3
                            value = plane[pl.ds(first, LANES // 8, stride=stride), :]
                        total = value if total is None else total + value
                    acc[(2 * t + h) % 2, pl.ds(b, LANES // 8, stride=8), :] = total * 0.125
                turned = acc[(2 * t + h) % 2].T
                for o in range(4):
                    flat[t % 2, pl.ds(4 * h + o, segments, stride=8), :] = turned[o * segments : (o + 1) * segments, :]
            for m in range(segments):
                out_ref[pl.ds(8 * templates * m + t, 8, stride=templates), :] = flat[t % 2, 8 * m : 8 * m + 8, :]

    for g in range(groups):
        own = weights[2 * g * share * LANES : 2 * (g + 1) * share * LANES, :]
        own = own.reshape(2 * share, LANES, 4 * LANES)
        for n, stride in enumerate(strides):
            height = planes[g][n].shape[2]
            if g == 0:
                make_windows(n, stride)
            amps = lax.dot_general(
                own[:, :height].reshape(2 * share * height, 4 * LANES),
                windows[n][...],
                (((1,), (1,)), ((), ())),
                preferred_element_type=F32,
            ).reshape(share, 2, height, 2 * 4 * segments)
            for t in range(share):
                plane = amps[t, 0] * amps[t, 0] + amps[t, 1] * amps[t, 1]
                for h in range(2):
                    planes[g][n][t, h] = plane[:, h * 4 * segments : (h + 1) * 4 * segments]
        if g:
            add_up((g - 1) * share, g * share)
    add_up((groups - 1) * share, templates)


def search(packed, moved, passed, weights, base, twist, harm_map, place, templates):
    blocks = 1 + len(moved)
    block_rows = packed.shape[0] // 2
    rows = block_rows * blocks
    strides = STRIDE_TABLE + (8,)
    segments = block_rows // 8
    heights = [min(LANES, 16 * stride + 16) for stride in strides]
    smem = pl.BlockSpec(memory_space=pltpu.SMEM)
    vmem = pl.BlockSpec(memory_space=pltpu.VMEM)
    scratch = [
        ((2 * rows + 16, LANES), F32),
        ((rows + 16, LANES), F32),
        ((rows + 16, LANES), F32),
        ((2, LANES, 4 * segments), F32),
        ((2, block_rows, LANES), F32),
    ] + len(strides) * [((block_rows, 4 * LANES), BF16)] + 2 * [((templates // 2, 2, height, block_rows // 2), F32) for height in heights]
    used = sum(math.prod(shape) * jnp.dtype(kind).itemsize for shape, kind in scratch)
    return pl.pallas_call(
        functools.partial(search_kernel, strides, (block_rows, blocks, templates)),
        out_shape=jax.ShapeDtypeStruct((block_rows * templates, LANES), F32),
        in_specs=[smem, smem] + [vmem] * (2 + 2 * blocks),
        out_specs=vmem,
        scratch_shapes=[
            *[pltpu.VMEM(shape, kind) for shape, kind in scratch],
            pltpu.SemaphoreType.DMA((2 * blocks - 1,)),
        ],
        compiler_params=pltpu.CompilerParams(vmem_limit_bytes=used + 12 * 2**20),
        name="search",
    )(
        place,
        harm_map,
        base,
        twist,
        packed,
        *moved,
        *passed,
        weights,
    )


def from_across(value, pair):
    blocks, peers = lax.axis_size("bins"), lax.axis_size("fdot")
    pairs = [
        (peers * d + f, peers * (d ^ (pair + 1 - (f >> 1) % 2)) + f)
        for d in range(blocks)
        for f in range(peers)
    ]
    return lax.ppermute(value, ("bins", "fdot"), pairs)


def body(spectrum, bank, fdot_index, harm_map):
    block_len = spectrum.shape[1]
    block_rows = block_len // LANES
    blocks = lax.axis_size("bins")
    templates = fdot_index.shape[0]
    device = lax.axis_index("bins")
    peer = lax.axis_index("fdot")
    part = peer & 1
    place = jnp.stack([device, part, (peer >> 1) & 1]).astype(jnp.int32)
    packed = spectrum.reshape(2, block_rows, LANES).transpose(1, 0, 2).reshape(2 * block_rows, LANES)
    mine = lax.dynamic_slice(packed, (part * block_rows, jnp.int32(0)), (block_rows, LANES))
    across = [from_across(mine, pair) for pair in range(2, blocks, 2)]
    steps = harm_map.reshape(-1, 4)
    fdot_index, steps, place = lax.optimization_barrier((fdot_index, steps, place))
    own, weights, base, twist = template_rows(packed, bank, fdot_index, block_rows * blocks)
    mine, base = lax.optimization_barrier((mine, base))
    moved = [from_partner(mine, "bins", 1)]
    for value in across:
        value = lax.optimization_barrier((value, base))[0]
        moved += [value, from_partner(value, "fdot", 2)]
    passed = [from_partner(value, "fdot", 1) for value in moved]
    out = search(own, moved, passed, weights, base, twist, steps, place, templates)
    return out.reshape(block_rows, templates, LANES).transpose(1, 0, 2).reshape(templates, block_len)


def solution(mesh):
    placed = (P(None, ("groups", "bins")), P(), P("fdot"), P(None, "bins", None))
    return jax.shard_map(
        body, mesh=mesh, in_specs=placed, out_specs=P("fdot", ("groups", "bins")), check_vma=False
    )
```

time: 30.3 us -> 25.8 us (0.85); the launches traced: 30.1 us -> 25.3 us
  waiting for transfers between devices: 8.42 us -> 3.62 us
  Pallas kernels: 11.2 us -> 8.92 us
  starting transfers between devices: 6.27 us -> 8.5 us
    ppermute x0 -> x1, starting transfers between devices: none -> 5.11 us  [from_across(): return lax.ppermute(value, ('bins', 'fdot'), pairs)]
    ppermute x6 -> x5, waiting for transfers between devices: 8.42 us -> 3.51 us  [from_partner(): return lax.ppermute(value, axis, pairs)]
    ppermute x6 -> x5, starting transfers between devices: 6.27 us -> 3.39 us  [from_partner(): return lax.ppermute(value, axis, pairs)]
    pallas_call x1, Pallas kernels: 10.2 us -> 8.04 us  [search(): pl.pallas_call(functools.partial(search_kernel, strides, (block_rows, blo...]
    optimization_barrier x0 -> x1, local copies, waits for them, and re-layouts: none -> 0.77 us  [body(): lax.optimization_barrier((fdot_index, steps, place))]
    reshape x1 -> x0, local copies, waits for them, and re-layouts: 0.77 us -> none  [search(): harm_map.reshape(-1, 4)]
where the time goes in v2:
time: 25.8 us; the launch traced here: 25.3 us
  Pallas kernels  8.92 us (35%)
  starting transfers between devices  8.5 us (33%)
  local copies, waits for them, and re-layouts  4.13 us (16%)
  waiting for transfers between devices  3.62 us (14%)
    pallas_call x1, Pallas kernels, search(): pl.pallas_call(functools.partial(search_kernel, strides, (block_rows, blo...  8.04 us
    ppermute x1, starting transfers between devices, from_across(): return lax.ppermute(value, ('bins', 'fdot'), pairs)  5.11 us
    ppermute x5, waiting for transfers between devices, from_partner(): return lax.ppermute(value, axis, pairs)  3.51 us
    ppermute x5, starting transfers between devices, from_partner(): return lax.ppermute(value, axis, pairs)  3.39 us
    unnamed x6, local copies, waits for them, and re-layouts  2.44 us
    dynamic_slice x1, local copies, waits for them, and re-layouts, body(): lax.dynamic_slice(packed, (part * block_rows, jnp.int32(0)), (block_rows,...  0.91 us
    pallas_call x1, Pallas kernels, template_rows(): pl.pallas_call(functools.partial(template_kernel, math.pi / (rows * LANES...  0.88 us
    optimization_barrier x1, local copies, waits for them, and re-layouts, body(): lax.optimization_barrier((fdot_index, steps, place))  0.77 us
  transfers between devices with their start and end apart: 6, of which 4 were waited for; matrix products, arithmetic and copies ran while one was open for 3% of the time, Pallas kernels for 3%

profile of v2, /device:TPU:0, one launch (start us, length us, event | category | flops | bytes accessed | tf_op | source)
XLA Modules:
  0.0 25.3 jit_solution(6044002054242697526)
XLA Ops:
  0.0 0.9 %constant_dynamic-slice_fusion = f32[256,128]{1,0:T(8,128)S(1)} fusion(f32[512,128]{1,0:T(8,128)} %bitcast.14, s32[]{:T(128)S(6)} %select_n.3), kind=kLoop, calls=%fused_computation.1 | loop fusion | bytes 262148 | tf_op jit(solution)/shard_map/dynamic_slice | solution.py:336
  0.9 5.1 %collective-permute-start.1 = (f32[256,128]{1,0:T(8,128)S(1)}, f32[256,128]{1,0:T(8,128)S(1)}, u32[]{:S(2)}, u32[]{:S(2)}) collective-permute-start(f32[256,128]{1,0:T(8,128)S(1)} %constant_dynamic-slice_fusion), channel_id=1, source_target_pairs={{0,12},{1,13},{2,10},{3,11},{4,8},{5,9},{6,14},{7,15},{8,4},{9,5},... | collective-permute-start | bytes 393224 | tf_op jit(solution)/shard_map/ppermute | solution.py:323
  6.0 0.1 pad_add_fusion.meta_ref
  6.1 0.0 copy-start
  6.1 0.9 %copy-done = f32[2,32768]{1,0:T(2,128)S(1)} copy-done((f32[2,32768]{1,0:T(2,128)S(1)}, f32[2,32768]{1,0:T(2,128)}, u32[]{:S(2)}) %copy-start) | copy-done | bytes 262168
  7.1 0.0 copy-start.1
  7.1 0.8 %copy-done.1 = bf16[128,2,128]{2,1,0:T(2,128)(2,1)S(1)} copy-done((bf16[128,2,128]{2,1,0:T(2,128)(2,1)S(1)}, bf16[128,2,128]{2,1,0:T(2,128)(2,1)}, u32[]{:S(2)}) %copy-start.1) | copy-done | bytes 65560
  7.9 0.0 copy-start.2
  7.9 0.7 %copy-done.2 = s32[8]{0:T(128)S(1)} copy-done((s32[8]{0:T(128)S(1)}, s32[8]{0:T(128)}, u32[]{:S(2)}) %copy-start.2) | copy-done | bytes 56
  8.6 0.9 %template_rows.1 = (f32[512,128]{1,0:T(8,128)S(1)}, bf16[2048,512]{1,0:T(8,128)(2,1)S(1)}, f32[16,128]{1,0:T(8,128)S(1)}, f32[2,128,128]{2,1,0:T(8,128)S(1)}) custom-call(f32[512,128]{1,0:T(8,128)S(1)} %bitcast.15, s32[8]{0:T(128)S(1)} %copy-done.2, bf16[128,2,128]{2,1,0:T(2,128)(2,1)S(1)} %copy-done.1), custom_call_target="tpu_custom_call" | custom-call | flops 1048576 | bytes 2097152 | tf_op jit(solution)/shard_map/template_rows/pallas_call | solution.py:66
  9.4 0.1 collective-permute-start
  9.5 0.1 collective-permute-done.1.refs_2_
  9.6 3.3 %collective-permute-start.2 = (f32[256,128]{1,0:T(8,128)S(1)}, f32[256,128]{1,0:T(8,128)S(1)}, u32[]{:S(2)}, u32[]{:S(2)}) collective-permute-start(f32[256,128]{1,0:T(8,128)S(1)} %collective-permute-done.1.refs_2_), channel_id=1, source_target_pairs={{0,2},{1,3},{2,0},{3,1},{4,6},{5,7},{6,4},{7,5},{8,10},{9,11},{10,... | collective-permute-start | bytes 393224 | tf_op jit(solution)/shard_map/ppermute | solution.py:19
  12.9 0.0 collective-permute-start.4
  12.9 1.5 %collective-permute-done.refs_1_ = f32[256,128]{1,0:T(8,128)S(1)} collective-permute-done((f32[256,128]{1,0:T(8,128)S(1)}, f32[256,128]{1,0:T(8,128)S(1)}, u32[]{:S(2)}, u32[]{:S(2)}) %collective-permute-start) | collective-permute-done | bytes 131104 | tf_op jit(solution)/shard_map/ppermute | solution.py:19
  14.5 0.0 collective-permute-start.3
  14.5 1.4 %collective-permute-done.2.refs_3_ = f32[256,128]{1,0:T(8,128)S(1)} collective-permute-done((f32[256,128]{1,0:T(8,128)S(1)}, f32[256,128]{1,0:T(8,128)S(1)}, u32[]{:S(2)}, u32[]{:S(2)}) %collective-permute-start.2) | collective-permute-done | bytes 131104 | tf_op jit(solution)/shard_map/ppermute | solution.py:19
  15.9 0.0 collective-permute-start.5
  15.9 0.8 %copy.6.map_ref = s32[7,4]{1,0:T(8,128)S(1)} copy(s32[7,4]{0,1:T(4,128)} %bitcast.16) | data formatting | bytes 224 | tf_op jit(solution)/shard_map/optimization_barrier | solution.py:339
  16.7 0.0 collective-permute-done.4.refs_5_
  16.7 0.0 collective-permute-done.3.refs_4_
  16.7 0.6 %collective-permute-done.5.refs_6_ = f32[256,128]{1,0:T(8,128)S(1)} collective-permute-done((f32[256,128]{1,0:T(8,128)S(1)}, f32[256,128]{1,0:T(8,128)S(1)}, u32[]{:S(2)}, u32[]{:S(2)}) %collective-permute-start.5) | collective-permute-done | bytes 131104 | tf_op jit(solution)/shard_map/ppermute | solution.py:19
  17.2 8.0 %search.1 = f32[2048,128]{1,0:T(8,128)} custom-call(s32[3]{0:T(128)S(1)} %pad_add_fusion.meta_ref, s32[7,4]{1,0:T(8,128)S(1)} %copy.6.map_ref, f32[16,128]{1,0:T(8,128)S(1)} %get-tuple-element.19.base_ref, f32[2,128,128]{2,1,0:T(8,128)S(1)} %get-tuple-element.20.twist_ref, f32[512,128]{1,0:T(8,128)S(1)} %get-tuple-element.21.refs_0_, ...), custom_call_target="tpu_custom_call" | custom-call | tf_op jit(solution)/shard_map/search/pallas_call | solution.py:293
Async XLA Ops:
  0.9 8.7 %collective-permute-start.1 = (f32[256,128]{1,0:T(8,128)S(1)}, f32[256,128]{1,0:T(8,128)S(1)}, u32[]{:S(2)}, u32[]{:S(2)}) collective-permute-start(f32[256,128]{1,0:T(8,128)S(1)} %constant_dynamic-slice_fusion), channel_id=1, source_target_pairs={{0,12},{1,13},{2,10},{3,11},{4,8},{5,9},{6,14},{7,15},{8,4},{9,5},... | collective-permute-start | bytes 393224 | tf_op jit(solution)/shard_map/ppermute | solution.py:323
  6.1 1.0 %copy-start = (f32[2,32768]{1,0:T(2,128)S(1)}, f32[2,32768]{1,0:T(2,128)}, u32[]{:S(2)}) copy-start(f32[2,32768]{1,0:T(2,128)} %param.4) | copy-start | bytes 786436
  7.1 0.8 %copy-start.1 = (bf16[128,2,128]{2,1,0:T(2,128)(2,1)S(1)}, bf16[128,2,128]{2,1,0:T(2,128)(2,1)}, u32[]{:S(2)}) copy-start(bf16[128,2,128]{2,1,0:T(2,128)(2,1)} %bank_hbm.1) | copy-start | bytes 196612
  7.9 0.7 %copy-start.2 = (s32[8]{0:T(128)S(1)}, s32[8]{0:T(128)}, u32[]{:S(2)}) copy-start(s32[8]{0:T(128)} %index_hbm) | copy-start | bytes 100
  9.4 5.0 %collective-permute-start = (f32[256,128]{1,0:T(8,128)S(1)}, f32[256,128]{1,0:T(8,128)S(1)}, u32[]{:S(2)}, u32[]{:S(2)}) collective-permute-start(f32[256,128]{1,0:T(8,128)S(1)} %constant_dynamic-slice_fusion), channel_id=1, source_target_pairs={{0,4},{4,0},{8,12},{12,8},{1,5},{5,1},{9,13},{13,9},{2,6},{6,2},{1... | collective-permute-start | bytes 393224 | tf_op jit(solution)/shard_map/ppermute | solution.py:19
  9.6 6.3 %collective-permute-start.2 = (f32[256,128]{1,0:T(8,128)S(1)}, f32[256,128]{1,0:T(8,128)S(1)}, u32[]{:S(2)}, u32[]{:S(2)}) collective-permute-start(f32[256,128]{1,0:T(8,128)S(1)} %collective-permute-done.1.refs_2_), channel_id=1, source_target_pairs={{0,2},{1,3},{2,0},{3,1},{4,6},{5,7},{6,4},{7,5},{8,10},{9,11},{10,... | collective-permute-start | bytes 393224 | tf_op jit(solution)/shard_map/ppermute | solution.py:19
  12.9 3.7 %collective-permute-start.4 = (f32[256,128]{1,0:T(8,128)S(1)}, f32[256,128]{1,0:T(8,128)S(1)}, u32[]{:S(2)}, u32[]{:S(2)}) collective-permute-start(f32[256,128]{1,0:T(8,128)S(1)} %collective-permute-done.1.refs_2_), channel_id=1, source_target_pairs={{0,1},{1,0},{2,3},{3,2},{4,5},{5,4},{6,7},{7,6},{8,9},{9,8},{10,11... | collective-permute-start | bytes 393224 | tf_op jit(solution)/shard_map/ppermute | solution.py:19
  14.5 2.2 %collective-permute-start.3 = (f32[256,128]{1,0:T(8,128)S(1)}, f32[256,128]{1,0:T(8,128)S(1)}, u32[]{:S(2)}, u32[]{:S(2)}) collective-permute-start(f32[256,128]{1,0:T(8,128)S(1)} %collective-permute-done.refs_1_), channel_id=1, source_target_pairs={{0,1},{1,0},{2,3},{3,2},{4,5},{5,4},{6,7},{7,6},{8,9},{9,8},{10,11... | collective-permute-start | bytes 393224 | tf_op jit(solution)/shard_map/ppermute | solution.py:19
  15.9 1.3 %collective-permute-start.5 = (f32[256,128]{1,0:T(8,128)S(1)}, f32[256,128]{1,0:T(8,128)S(1)}, u32[]{:S(2)}, u32[]{:S(2)}) collective-permute-start(f32[256,128]{1,0:T(8,128)S(1)} %collective-permute-done.2.refs_3_), channel_id=1, source_target_pairs={{0,1},{1,0},{2,3},{3,2},{4,5},{5,4},{6,7},{7,6},{8,9},{9,8},{10,11... | collective-permute-start | bytes 393224 | tf_op jit(solution)/shard_map/ppermute | solution.py:19

commit v3 on v2

--- a/solution.py
+++ b/solution.py
@@ -20,9 +20,9 @@
 
 
 def template_kernel(
-    step, packed_hbm, index_hbm, bank_hbm, own_ref, out_ref, base_ref, twist_ref, index_ref, bank_ref, sem
+    step, index_hbm, bank_hbm, out_ref, base_ref, twist_ref, index_ref, bank_ref, sem
 ):
-    pairs = ((index_hbm, index_ref), (bank_hbm, bank_ref), (packed_hbm, own_ref))
+    pairs = ((index_hbm, index_ref), (bank_hbm, bank_ref))
     copies = [pltpu.make_async_copy(source, to, sem.at[i]) for i, (source, to) in enumerate(pairs)]
     for copy in copies:
         copy.start()
@@ -55,20 +55,18 @@
         out_ref[top : top + LANES, 2 * LANES :] = (-imag).astype(BF16)
         out_ref[low : low + LANES, : 2 * LANES] = imag.astype(BF16)
         out_ref[low : low + LANES, 2 * LANES :] = real.astype(BF16)
-    copies[2].wait()
-
-
-def template_rows(packed, bank, fdot_index, rows):
+
+
+def template_rows(bank, fdot_index, rows):
     count = fdot_index.shape[0]
     taps = bank.shape[2]
     height = 2 * count * taps
     vmem = pl.BlockSpec(memory_space=pltpu.VMEM)
     return pl.pallas_call(
         functools.partial(template_kernel, math.pi / (rows * LANES)),
-        in_specs=[pl.BlockSpec(memory_space=pltpu.HBM)] * 3,
-        out_specs=[vmem] * 4,
+        in_specs=[pl.BlockSpec(memory_space=pltpu.HBM)] * 2,
+        out_specs=[vmem] * 3,
         out_shape=[
-            jax.ShapeDtypeStruct(packed.shape, F32),
             jax.ShapeDtypeStruct((height, 4 * taps), BF16),
             jax.ShapeDtypeStruct((16, LANES), F32),
             jax.ShapeDtypeStruct((2, rows // 8, LANES), F32),
@@ -76,28 +74,25 @@
         scratch_shapes=[
             pltpu.SMEM(fdot_index.shape, jnp.int32),
             pltpu.VMEM(bank.shape, BF16),
-            pltpu.SemaphoreType.DMA((3,)),
+            pltpu.SemaphoreType.DMA((2,)),
         ],
         cost_estimate=pl.CostEstimate(
             flops=4 * height * taps, bytes_accessed=8 * height * taps, transcendentals=0
         ),
         compiler_params=pltpu.CompilerParams(vmem_limit_bytes=16 * 2**20),
         name="template_rows",
-    )(packed, fdot_index, bank)
+    )(fdot_index, bank)
 
 
 def search_kernel(strides, sizes, meta_ref, map_ref, base_ref, twist_ref, *refs):
-    block_rows, blocks, templates = sizes
-    moved = blocks - 1
-    own_ref = refs[0]
-    rest = refs[1 : 1 + 2 * moved]
-    weights, out_ref, raw, real, imag, acc, flat, *more = refs[1 + 2 * moved :]
+    block_rows, blocks, templates, layout = sizes
+    pieces = refs[: 2 * len(layout)]
+    weights, out_ref, raw, real, imag, acc, flat, *more = refs[2 * len(layout) :]
     windows = more[: len(strides)]
     more = more[len(strides) :]
     groups = 2
     share = templates // groups
     planes = [more[g * len(strides) : (g + 1) * len(strides)] for g in range(groups)]
-    copy_sem = more[groups * len(strides)]
     rows = block_rows * blocks
     total_bins = rows * LANES
     segments = block_rows // 8
@@ -105,33 +100,17 @@
     part = meta_ref[1]
     column = meta_ref[2]
 
-    copies = []
-
-    def fetch(source, start):
-        size = source.shape[0]
-        start = pl.multiple_of(start, size)
-        copy = pltpu.make_async_copy(
-            source, raw.at[pl.ds(start, size), :], copy_sem.at[len(copies)]
-        )
-        copy.start()
-        copies.append(copy)
-
-    fetch(own_ref, device * (2 * block_rows))
-    masks = [1]
-    for pair in range(2, blocks, 2):
-        masks += [pair + 1 - column, pair + column]
-    for k, mask in enumerate(masks):
-        other = (device ^ mask) * (2 * block_rows)
-        fetch(rest[k], other + part * block_rows)
-        fetch(rest[moved + k], other + (1 - part) * block_rows)
-    halves = [own_ref.at[:block_rows], own_ref.at[block_rows:], *rest]
     sums = [jnp.zeros((8, LANES), F32)] * 4
-    for half in halves:
-        for i in range(1, block_rows // 8):
-            tile = half[8 * i : 8 * i + 8, :]
-            sums[i % 4] = sums[i % 4] + tile * tile
-    for copy in copies:
-        copy.wait()
+    for i, source in enumerate(pieces):
+        pair, cross = layout[i % len(layout)]
+        mask = pair + (1 - column if cross else column) if pair > 1 else pair
+        half = part if i < len(layout) else 1 - part
+        start = pl.multiple_of((device ^ mask) * (2 * block_rows) + half * block_rows, block_rows)
+        for j in range(block_rows // 8):
+            tile = source[8 * j : 8 * j + 8, :]
+            raw[pl.ds(start + 8 * j, 8), :] = tile
+            if j:
+                sums[j % 4] = sums[j % 4] + tile * tile
     raw[2 * rows : 2 * rows + 16, :] = raw[0:16, :]
     row_ids = lax.broadcasted_iota(jnp.int32, (8, LANES), 0)
     lanes = lax.broadcasted_iota(jnp.int32, (8, LANES), 1)
@@ -273,9 +252,8 @@
     add_up((groups - 1) * share, templates)
 
 
-def search(packed, moved, passed, weights, base, twist, harm_map, place, templates):
-    blocks = 1 + len(moved)
-    block_rows = packed.shape[0] // 2
+def search(pieces, layout, weights, base, twist, harm_map, place, blocks, templates):
+    block_rows = pieces[0].shape[0]
     rows = block_rows * blocks
     strides = STRIDE_TABLE + (8,)
     segments = block_rows // 8
@@ -291,13 +269,12 @@
     ] + len(strides) * [((block_rows, 4 * LANES), BF16)] + 2 * [((templates // 2, 2, height, block_rows // 2), F32) for height in heights]
     used = sum(math.prod(shape) * jnp.dtype(kind).itemsize for shape, kind in scratch)
     return pl.pallas_call(
-        functools.partial(search_kernel, strides, (block_rows, blocks, templates)),
+        functools.partial(search_kernel, strides, (block_rows, blocks, templates, layout)),
         out_shape=jax.ShapeDtypeStruct((block_rows * templates, LANES), F32),
-        in_specs=[smem, smem] + [vmem] * (2 + 2 * blocks),
+        in_specs=[smem, smem] + [vmem] * (3 + len(pieces)),
         out_specs=vmem,
         scratch_shapes=[
             *[pltpu.VMEM(shape, kind) for shape, kind in scratch],
-            pltpu.SemaphoreType.DMA((2 * blocks - 1,)),
         ],
         compiler_params=pltpu.CompilerParams(vmem_limit_bytes=used + 12 * 2**20),
         name="search",
@@ -306,9 +283,7 @@
         harm_map,
         base,
         twist,
-        packed,
-        *moved,
-        *passed,
+        *pieces,
         weights,
     )
 
@@ -334,17 +309,19 @@
     place = jnp.stack([device, part, (peer >> 1) & 1]).astype(jnp.int32)
     packed = spectrum.reshape(2, block_rows, LANES).transpose(1, 0, 2).reshape(2 * block_rows, LANES)
     mine = lax.dynamic_slice(packed, (part * block_rows, jnp.int32(0)), (block_rows, LANES))
-    across = [from_across(mine, pair) for pair in range(2, blocks, 2)]
+    far = [from_across(mine, pair) for pair in range(2, blocks, 2)]
     steps = harm_map.reshape(-1, 4)
     fdot_index, steps, place = lax.optimization_barrier((fdot_index, steps, place))
-    own, weights, base, twist = template_rows(packed, bank, fdot_index, block_rows * blocks)
-    mine, base = lax.optimization_barrier((mine, base))
-    moved = [from_partner(mine, "bins", 1)]
-    for value in across:
+    weights, base, twist = template_rows(bank, fdot_index, block_rows * blocks)
+    sent, base = lax.optimization_barrier((mine, base))
+    held = [sent, from_partner(sent, "bins", 1)]
+    layout = [(0, 0), (1, 0)]
+    for value, pair in zip(far, range(2, blocks, 2)):
         value = lax.optimization_barrier((value, base))[0]
-        moved += [value, from_partner(value, "fdot", 2)]
-    passed = [from_partner(value, "fdot", 1) for value in moved]
-    out = search(own, moved, passed, weights, base, twist, steps, place, templates)
+        held += [value, from_partner(value, "fdot", 2)]
+        layout += [(pair, 1), (pair, 0)]
+    passed = [from_partner(value, "fdot", 1) for value in held]
+    out = search(held + passed, layout, weights, base, twist, steps, place, blocks, templates)
     return out.reshape(block_rows, templates, LANES).transpose(1, 0, 2).reshape(templates, block_len)
 
 

time: 25.8 us -> 24.9 us (0.965)
  Pallas kernels: 8.92 us -> 7.96 us
  local copies, waits for them, and re-layouts: 4.13 us -> 3.22 us
  starting transfers between devices: 8.5 us -> 9.04 us
  waiting for transfers between devices: 3.62 us -> 4.07 us
    ppermute x1, waiting for transfers between devices: 0.11 us -> 1.07 us  [from_across(): return lax.ppermute(value, ('bins', 'fdot'), pairs)]
    pallas_call x1, Pallas kernels: 8.04 us -> 7.09 us  [search(): pl.pallas_call(functools.partial(search_kernel, strides, (block_rows, blo...]
    dynamic_slice x1, local copies, waits for them, and re-layouts: 0.91 us -> 0.01 us  [body(): lax.dynamic_slice(packed, (part * block_rows, jnp.int32(0)), (block_rows,...]
    ppermute x5 -> x6, starting transfers between devices: 3.39 us -> 3.92 us  [from_partner(): return lax.ppermute(value, axis, pairs)]
    ppermute x5 -> x6, waiting for transfers between devices: 3.51 us -> 3 us  [from_partner(): return lax.ppermute(value, axis, pairs)]
  transfers between devices with their start and end apart: 6 -> 7, of which waited for: 4 -> 3; matrix products, arithmetic and copies ran while one was open for 3% -> 3% of each run, Pallas kernels for 3% -> 4%
where the time goes in v3:
time: 24.9 us; the launch traced here: 24.4 us
  starting transfers between devices  9.04 us (36%)
  Pallas kernels  7.96 us (32%)
  waiting for transfers between devices  4.07 us (16%)
  local copies, waits for them, and re-layouts  3.22 us (13%)
    pallas_call x1, Pallas kernels, search(): pl.pallas_call(functools.partial(search_kernel, strides, (block_rows, blo...  7.09 us
    ppermute x1, starting transfers between devices, from_across(): return lax.ppermute(value, ('bins', 'fdot'), pairs)  5.11 us
    ppermute x6, starting transfers between devices, from_partner(): return lax.ppermute(value, axis, pairs)  3.92 us
    ppermute x6, waiting for transfers between devices, from_partner(): return lax.ppermute(value, axis, pairs)  3 us
    unnamed x6, local copies, waits for them, and re-layouts  2.45 us
    ppermute x1, waiting for transfers between devices, from_across(): return lax.ppermute(value, ('bins', 'fdot'), pairs)  1.07 us
    pallas_call x1, Pallas kernels, template_rows(): pl.pallas_call(functools.partial(template_kernel, math.pi / (rows * LANES...  0.87 us
    optimization_barrier x1, local copies, waits for them, and re-layouts, body(): lax.optimization_barrier((fdot_index, steps, place))  0.77 us
  transfers between devices with their start and end apart: 7, of which 3 were waited for; matrix products, arithmetic and copies ran while one was open for 3% of the time, Pallas kernels for 4%

profile of v3, /device:TPU:0, one launch (start us, length us, event | category | flops | bytes accessed | tf_op | source)
XLA Modules:
  0.0 24.4 jit_solution(2837649816845960057)
XLA Ops:
  0.0 0.0 copy-start
  0.0 0.9 %copy-done = f32[2,32768]{1,0:T(2,128)S(1)} copy-done((f32[2,32768]{1,0:T(2,128)S(1)}, f32[2,32768]{1,0:T(2,128)}, u32[]{:S(2)}) %copy-start) | copy-done | bytes 262168
  1.0 5.1 %collective-permute-start.1 = (f32[256,128]{1,0:T(8,128)S(1)}, f32[256,128]{1,0:T(8,128)S(1)}, u32[]{:S(2)}, u32[]{:S(2)}) collective-permute-start(f32[256,128]{1,0:T(8,128)S(1)} %constant_dynamic-slice_fusion.refs_0_), channel_id=1, source_target_pairs={{0,12},{1,13},{2,10},{3,11},{4,8},{5,9},{6,14},{7,15},{8,4},{9,5},... | collective-permute-start | bytes 393224 | tf_op jit(solution)/shard_map/ppermute | solution.py:298
  6.1 0.1 pad_add_fusion.meta_ref
  6.2 0.0 copy-start.1
  6.2 0.8 %copy-done.1 = bf16[128,2,128]{2,1,0:T(2,128)(2,1)S(1)} copy-done((bf16[128,2,128]{2,1,0:T(2,128)(2,1)S(1)}, bf16[128,2,128]{2,1,0:T(2,128)(2,1)}, u32[]{:S(2)}) %copy-start.1) | copy-done | bytes 65560
  7.0 0.0 copy-start.2
  7.0 0.7 %copy-done.2 = s32[8]{0:T(128)S(1)} copy-done((s32[8]{0:T(128)S(1)}, s32[8]{0:T(128)}, u32[]{:S(2)}) %copy-start.2) | copy-done | bytes 56
  7.7 0.9 %template_rows.1 = (bf16[2048,512]{1,0:T(8,128)(2,1)S(1)}, f32[16,128]{1,0:T(8,128)S(1)}, f32[2,128,128]{2,1,0:T(8,128)S(1)}) custom-call(s32[8]{0:T(128)S(1)} %copy-done.2, bf16[128,2,128]{2,1,0:T(2,128)(2,1)S(1)} %copy-done.1), custom_call_target="tpu_custom_call" | custom-call | flops 1048576 | bytes 2097152 | tf_op jit(solution)/shard_map/template_rows/pallas_call | solution.py:65
  8.5 0.1 collective-permute-start
  8.6 1.1 %collective-permute-done.1.refs_2_ = f32[256,128]{1,0:T(8,128)S(1)} collective-permute-done((f32[256,128]{1,0:T(8,128)S(1)}, f32[256,128]{1,0:T(8,128)S(1)}, u32[]{:S(2)}, u32[]{:S(2)}) %collective-permute-start.1) | collective-permute-done | bytes 131104 | tf_op jit(solution)/shard_map/ppermute | solution.py:298
  9.7 3.3 %collective-permute-start.2 = (f32[256,128]{1,0:T(8,128)S(1)}, f32[256,128]{1,0:T(8,128)S(1)}, u32[]{:S(2)}, u32[]{:S(2)}) collective-permute-start(f32[256,128]{1,0:T(8,128)S(1)} %collective-permute-done.1.refs_2_), channel_id=1, source_target_pairs={{0,2},{1,3},{2,0},{3,1},{4,6},{5,7},{6,4},{7,5},{8,10},{9,11},{10,... | collective-permute-start | bytes 393224 | tf_op jit(solution)/shard_map/ppermute | solution.py:19
  13.0 0.0 collective-permute-start.3
  13.0 0.5 %collective-permute-start.5 = (f32[256,128]{1,0:T(8,128)S(1)}, f32[256,128]{1,0:T(8,128)S(1)}, u32[]{:S(2)}, u32[]{:S(2)}) collective-permute-start(f32[256,128]{1,0:T(8,128)S(1)} %collective-permute-done.1.refs_2_), channel_id=1, source_target_pairs={{0,1},{1,0},{2,3},{3,2},{4,5},{5,4},{6,7},{7,6},{8,9},{9,8},{10,11... | collective-permute-start | bytes 393224 | tf_op jit(solution)/shard_map/ppermute | solution.py:19
  13.5 0.0 collective-permute-done.refs_1_
  13.6 0.0 collective-permute-start.4
  13.6 2.4 %collective-permute-done.2.refs_3_ = f32[256,128]{1,0:T(8,128)S(1)} collective-permute-done((f32[256,128]{1,0:T(8,128)S(1)}, f32[256,128]{1,0:T(8,128)S(1)}, u32[]{:S(2)}, u32[]{:S(2)}) %collective-permute-start.2) | collective-permute-done | bytes 131104 | tf_op jit(solution)/shard_map/ppermute | solution.py:19
  16.0 0.0 collective-permute-start.6
  16.0 0.8 %copy.6.map_ref = s32[7,4]{1,0:T(8,128)S(1)} copy(s32[7,4]{0,1:T(4,128)} %bitcast.15) | data formatting | bytes 224 | tf_op jit(solution)/shard_map/optimization_barrier | solution.py:314
  16.7 0.0 collective-permute-done.3.refs_4_
  16.7 0.0 collective-permute-done.5.refs_6_
  16.7 0.0 collective-permute-done.4.refs_5_
  16.7 0.6 %collective-permute-done.6.refs_7_ = f32[256,128]{1,0:T(8,128)S(1)} collective-permute-done((f32[256,128]{1,0:T(8,128)S(1)}, f32[256,128]{1,0:T(8,128)S(1)}, u32[]{:S(2)}, u32[]{:S(2)}) %collective-permute-start.6) | collective-permute-done | bytes 131104 | tf_op jit(solution)/shard_map/ppermute | solution.py:19
  17.3 7.1 %search.1 = f32[2048,128]{1,0:T(8,128)} custom-call(s32[3]{0:T(128)S(1)} %pad_add_fusion.meta_ref, s32[7,4]{1,0:T(8,128)S(1)} %copy.6.map_ref, f32[16,128]{1,0:T(8,128)S(1)} %get-tuple-element.18.base_ref, f32[2,128,128]{2,1,0:T(8,128)S(1)} %get-tuple-element.19.twist_ref, f32[256,128]{1,0:T(8,128)S(1)} %constant_dynamic-slice_fusion.refs_0_, ...), custom_call_target="tpu_custom_call" | custom-call | tf_op jit(solution)/shard_map/search/pallas_call | solution.py:271
  (1 shorter events, 0.0 us)
Async XLA Ops:
  0.0 1.0 %copy-start = (f32[2,32768]{1,0:T(2,128)S(1)}, f32[2,32768]{1,0:T(2,128)}, u32[]{:S(2)}) copy-start(f32[2,32768]{1,0:T(2,128)} %param.4) | copy-start | bytes 786436
  1.0 8.7 %collective-permute-start.1 = (f32[256,128]{1,0:T(8,128)S(1)}, f32[256,128]{1,0:T(8,128)S(1)}, u32[]{:S(2)}, u32[]{:S(2)}) collective-permute-start(f32[256,128]{1,0:T(8,128)S(1)} %constant_dynamic-slice_fusion.refs_0_), channel_id=1, source_target_pairs={{0,12},{1,13},{2,10},{3,11},{4,8},{5,9},{6,14},{7,15},{8,4},{9,5},... | collective-permute-start | bytes 393224 | tf_op jit(solution)/shard_map/ppermute | solution.py:298
  6.2 0.8 %copy-start.1 = (bf16[128,2,128]{2,1,0:T(2,128)(2,1)S(1)}, bf16[128,2,128]{2,1,0:T(2,128)(2,1)}, u32[]{:S(2)}) copy-start(bf16[128,2,128]{2,1,0:T(2,128)(2,1)} %bank_hbm.1) | copy-start | bytes 196612
  7.0 0.7 %copy-start.2 = (s32[8]{0:T(128)S(1)}, s32[8]{0:T(128)}, u32[]{:S(2)}) copy-start(s32[8]{0:T(128)} %index_hbm) | copy-start | bytes 100
  8.5 5.0 %collective-permute-start = (f32[256,128]{1,0:T(8,128)S(1)}, f32[256,128]{1,0:T(8,128)S(1)}, u32[]{:S(2)}, u32[]{:S(2)}) collective-permute-start(f32[256,128]{1,0:T(8,128)S(1)} %constant_dynamic-slice_fusion.refs_0_), channel_id=1, source_target_pairs={{0,4},{4,0},{8,12},{12,8},{1,5},{5,1},{9,13},{13,9},{2,6},{6,2},{1... | collective-permute-start | bytes 393224 | tf_op jit(solution)/shard_map/ppermute | solution.py:19
  9.7 6.3 %collective-permute-start.2 = (f32[256,128]{1,0:T(8,128)S(1)}, f32[256,128]{1,0:T(8,128)S(1)}, u32[]{:S(2)}, u32[]{:S(2)}) collective-permute-start(f32[256,128]{1,0:T(8,128)S(1)} %collective-permute-done.1.refs_2_), channel_id=1, source_target_pairs={{0,2},{1,3},{2,0},{3,1},{4,6},{5,7},{6,4},{7,5},{8,10},{9,11},{10,... | collective-permute-start | bytes 393224 | tf_op jit(solution)/shard_map/ppermute | solution.py:19
  13.0 3.7 %collective-permute-start.3 = (f32[256,128]{1,0:T(8,128)S(1)}, f32[256,128]{1,0:T(8,128)S(1)}, u32[]{:S(2)}, u32[]{:S(2)}) collective-permute-start(f32[256,128]{1,0:T(8,128)S(1)} %constant_dynamic-slice_fusion.refs_0_), channel_id=1, source_target_pairs={{0,1},{1,0},{2,3},{3,2},{4,5},{5,4},{6,7},{7,6},{8,9},{9,8},{10,11... | collective-permute-start | bytes 393224 | tf_op jit(solution)/shard_map/ppermute | solution.py:19
  13.0 3.7 %collective-permute-start.5 = (f32[256,128]{1,0:T(8,128)S(1)}, f32[256,128]{1,0:T(8,128)S(1)}, u32[]{:S(2)}, u32[]{:S(2)}) collective-permute-start(f32[256,128]{1,0:T(8,128)S(1)} %collective-permute-done.1.refs_2_), channel_id=1, source_target_pairs={{0,1},{1,0},{2,3},{3,2},{4,5},{5,4},{6,7},{7,6},{8,9},{9,8},{10,11... | collective-permute-start | bytes 393224 | tf_op jit(solution)/shard_map/ppermute | solution.py:19
  13.6 3.2 %collective-permute-start.4 = (f32[256,128]{1,0:T(8,128)S(1)}, f32[256,128]{1,0:T(8,128)S(1)}, u32[]{:S(2)}, u32[]{:S(2)}) collective-permute-start(f32[256,128]{1,0:T(8,128)S(1)} %collective-permute-done.refs_1_), channel_id=1, source_target_pairs={{0,1},{1,0},{2,3},{3,2},{4,5},{5,4},{6,7},{7,6},{8,9},{9,8},{10,11... | collective-permute-start | bytes 393224 | tf_op jit(solution)/shard_map/ppermute | solution.py:19
  16.0 1.3 %collective-permute-start.6 = (f32[256,128]{1,0:T(8,128)S(1)}, f32[256,128]{1,0:T(8,128)S(1)}, u32[]{:S(2)}, u32[]{:S(2)}) collective-permute-start(f32[256,128]{1,0:T(8,128)S(1)} %collective-permute-done.2.refs_3_), channel_id=1, source_target_pairs={{0,1},{1,0},{2,3},{3,2},{4,5},{5,4},{6,7},{7,6},{8,9},{9,8},{10,11... | collective-permute-start | bytes 393224 | tf_op jit(solution)/shard_map/ppermute | solution.py:19

commit v4 on v3

--- a/solution.py
+++ b/solution.py
@@ -12,6 +12,7 @@
 STRIDE_TABLE = (4, 2, 6, 1, 3, 5, 7)
 F32 = jnp.float32
 BF16 = jnp.bfloat16
+GROUPS = 2
 
 
 def from_partner(value, axis, mask):
@@ -20,7 +21,7 @@
 
 
 def template_kernel(
-    step, index_hbm, bank_hbm, out_ref, base_ref, twist_ref, index_ref, bank_ref, sem
+    step, groups, index_hbm, bank_hbm, out_ref, extra_ref, base_ref, twist_ref, index_ref, bank_ref, sem
 ):
     pairs = ((index_hbm, index_ref), (bank_hbm, bank_ref))
     copies = [pltpu.make_async_copy(source, to, sem.at[i]) for i, (source, to) in enumerate(pairs)]
@@ -46,6 +47,7 @@
         wide = jnp.broadcast_to(jnp.concatenate([row, zeros], axis=1), (LANES, 2 * LANES))
         return pltpu.roll(wide, 0, 1, stride=1, stride_axis=0)
 
+    tables = []
     for t in range(index_ref.shape[0]):
         taps = bank_ref[index_ref[t]].astype(F32)
         real = banded(taps[0:1])
@@ -55,6 +57,19 @@
         out_ref[top : top + LANES, 2 * LANES :] = (-imag).astype(BF16)
         out_ref[low : low + LANES, : 2 * LANES] = imag.astype(BF16)
         out_ref[low : low + LANES, 2 * LANES :] = real.astype(BF16)
+        tables.append((real, imag))
+
+    count = len(tables)
+    for n, stride in enumerate(STRIDE_TABLE):
+        at = slice(16 * stride, 16 * stride + 1)
+        for g in range(groups):
+            some = tables[g * count // groups : (g + 1) * count // groups]
+            pad = [jnp.zeros((8 - len(some), 2 * LANES), F32)] if len(some) < 8 else []
+            real = jnp.concatenate([value[0][at] for value in some] + pad)
+            imag = jnp.concatenate([value[1][at] for value in some] + pad)
+            low = 16 * (groups * n + g)
+            extra_ref[low : low + 16, : 2 * LANES] = jnp.concatenate([real, imag]).astype(BF16)
+            extra_ref[low : low + 16, 2 * LANES :] = jnp.concatenate([-imag, real]).astype(BF16)
 
 
 def template_rows(bank, fdot_index, rows):
@@ -63,11 +78,12 @@
     height = 2 * count * taps
     vmem = pl.BlockSpec(memory_space=pltpu.VMEM)
     return pl.pallas_call(
-        functools.partial(template_kernel, math.pi / (rows * LANES)),
+        functools.partial(template_kernel, math.pi / (rows * LANES), GROUPS),
         in_specs=[pl.BlockSpec(memory_space=pltpu.HBM)] * 2,
-        out_specs=[vmem] * 3,
+        out_specs=[vmem] * 4,
         out_shape=[
             jax.ShapeDtypeStruct((height, 4 * taps), BF16),
+            jax.ShapeDtypeStruct((16 * GROUPS * len(STRIDE_TABLE), 4 * taps), BF16),
             jax.ShapeDtypeStruct((16, LANES), F32),
             jax.ShapeDtypeStruct((2, rows // 8, LANES), F32),
         ],
@@ -84,21 +100,24 @@
     )(fdot_index, bank)
 
 
-def search_kernel(strides, sizes, meta_ref, map_ref, base_ref, twist_ref, *refs):
+def search_kernel(strides, sizes, phase_hbm, base_ref, twist_ref, *refs):
     block_rows, blocks, templates, layout = sizes
     pieces = refs[: 2 * len(layout)]
-    weights, out_ref, raw, real, imag, acc, flat, *more = refs[2 * len(layout) :]
+    weights, extra, out_hbm, raw, real, imag, acc, flat, ready, phase_ref, out_sem, *more = refs[2 * len(layout) :]
     windows = more[: len(strides)]
     more = more[len(strides) :]
-    groups = 2
+    groups = GROUPS
     share = templates // groups
     planes = [more[g * len(strides) : (g + 1) * len(strides)] for g in range(groups)]
     rows = block_rows * blocks
     total_bins = rows * LANES
     segments = block_rows // 8
-    device = meta_ref[0]
-    part = meta_ref[1]
-    column = meta_ref[2]
+    device = lax.axis_index("bins")
+    peer = lax.axis_index("fdot")
+    part = peer & 1
+    column = (peer >> 1) & 1
+    phase_copy = pltpu.make_async_copy(phase_hbm, phase_ref, out_sem.at[0])
+    phase_copy.start()
 
     sums = [jnp.zeros((8, LANES), F32)] * 4
     for i, source in enumerate(pieces):
@@ -179,10 +198,7 @@
 
     wide_lanes = lax.broadcasted_iota(jnp.int32, (segments, LANES), 1)
     def make_windows(n, stride):
-        if stride == 8:
-            first_row = device * block_rows + 8
-        else:
-            first_row = map_ref[n, 0] * block_rows + (map_ref[n, 2] >> 7) + 8
+        first_row = device * (block_rows * stride // 8) + 8
         for o in range(8):
             ahead = 2 * stride * 8 * o - LANES // 2
             skip, shift = ahead // LANES, ahead % LANES
@@ -200,91 +216,110 @@
                     at = (2 * c + half) * LANES
                     windows[n][o * segments : (o + 1) * segments, at : at + LANES] = tile
 
-    def add_up(first, last):
-        for t in range(first, last):
-            for h in range(2):
-                shared = {
-                    n: [planes[t // share][n][t % share, h, pl.ds(c, LANES // 8, stride=stride), :] for c in range(stride + 1)]
-                    for n, stride in enumerate(strides)
-                    if stride <= 2
-                }
+    def add_up(t, h):
+        total = [None] * 8
+        for n, stride in enumerate(strides):
+            plane = planes[t // share][n].at[t % share, h]
+            if stride == 8:
+                values = [plane[pl.ds(b, LANES // 8, stride=8), :] for b in range(8)]
+            else:
+                starts = [plane[pl.ds(c, LANES // 8, stride=stride), :] for c in range(stride + 1)]
+                values = []
                 for b in range(8):
-                    total = None
-                    for n, stride in enumerate(strides):
-                        plane = planes[t // share][n].at[t % share, h]
-                        if stride == 8:
-                            value = plane[pl.ds(b, LANES // 8, stride=8), :]
-                        elif stride <= 2:
-                            first = (map_ref[n, 3] + b * stride) >> 3
-                            value = shared[n][0]
-                            for c in range(1, stride + 1):
-                                value = jnp.where(first == c, shared[n][c], value)
-                        else:
-                            first = (map_ref[n, 3] + b * stride) >> 3
-                            value = plane[pl.ds(first, LANES // 8, stride=stride), :]
-                        total = value if total is None else total + value
-                    acc[(2 * t + h) % 2, pl.ds(b, LANES // 8, stride=8), :] = total * 0.125
-                turned = acc[(2 * t + h) % 2].T
-                for o in range(4):
-                    flat[t % 2, pl.ds(4 * h + o, segments, stride=8), :] = turned[o * segments : (o + 1) * segments, :]
-            for m in range(segments):
-                out_ref[pl.ds(8 * templates * m + t, 8, stride=templates), :] = flat[t % 2, 8 * m : 8 * m + 8, :]
-
+                    least = stride * b // 8
+                    ahead = phase_ref[n] + stride * b >= 8 * (least + 1)
+                    values.append(jnp.where(ahead, starts[least + 1], starts[least]))
+            total = values if n == 0 else [x + y for x, y in zip(total, values)]
+        for b in range(8):
+            acc[(2 * t + h) % 2, pl.ds(b, LANES // 8, stride=8), :] = total[b] * 0.125
+        turned = acc[(2 * t + h) % 2].T
+        for o in range(4):
+            flat[t, pl.ds(4 * h + o, segments, stride=8), :] = turned[o * segments : (o + 1) * segments, :]
+
+    phase_copy.wait()
     for g in range(groups):
         own = weights[2 * g * share * LANES : 2 * (g + 1) * share * LANES, :]
         own = own.reshape(2 * share, LANES, 4 * LANES)
         for n, stride in enumerate(strides):
-            height = planes[g][n].shape[2]
             if g == 0:
                 make_windows(n, stride)
+            height = 16 * stride
+            lhs = own[:, :height].reshape(2 * share * height, 4 * LANES)
+            if stride < 8:
+                low = 16 * (groups * n + g)
+                lhs = jnp.concatenate([lhs, extra[low : low + 16, :]])
             amps = lax.dot_general(
-                own[:, :height].reshape(2 * share * height, 4 * LANES),
-                windows[n][...],
-                (((1,), (1,)), ((), ())),
-                preferred_element_type=F32,
-            ).reshape(share, 2, height, 2 * 4 * segments)
+                lhs, windows[n][...], (((1,), (1,)), ((), ())), preferred_element_type=F32
+            )
             for t in range(share):
-                plane = amps[t, 0] * amps[t, 0] + amps[t, 1] * amps[t, 1]
+                top = 2 * t * height
+                plane = amps[top : top + height] ** 2 + amps[top + height : top + 2 * height] ** 2
                 for h in range(2):
-                    planes[g][n][t, h] = plane[:, h * 4 * segments : (h + 1) * 4 * segments]
-        if g:
-            add_up((g - 1) * share, g * share)
-    add_up((groups - 1) * share, templates)
-
-
-def search(pieces, layout, weights, base, twist, harm_map, place, blocks, templates):
+                    planes[g][n][t, h, :height] = plane[:, h * 4 * segments : (h + 1) * 4 * segments]
+            if stride < 8:
+                top = 2 * share * height
+                last = amps[top : top + 8] ** 2 + amps[top + 8 : top + 16] ** 2
+                for t in range(share):
+                    for h in range(2):
+                        planes[g][n][t, h, height : height + 1] = last[
+                            t : t + 1, h * 4 * segments : (h + 1) * 4 * segments
+                        ]
+            if g:
+                units = range(2 * share * n // len(strides), 2 * share * (n + 1) // len(strides))
+                for unit in units:
+                    add_up((g - 1) * share + unit // 2, unit % 2)
+    for unit in range(2 * share):
+        add_up((groups - 1) * share + unit // 2, unit % 2)
+    parts = out_sem.shape[0]
+    span = block_rows * templates // parts
+    copies = []
+    for i in range(parts):
+        for m in range(i * segments // parts, (i + 1) * segments // parts):
+            for t in range(templates):
+                ready[pl.ds(8 * templates * m + t, 8, stride=templates), :] = flat[t, 8 * m : 8 * m + 8, :]
+        done = pl.ds(i * span, span)
+        copies.append(pltpu.make_async_copy(ready.at[done, :], out_hbm.at[done, :], out_sem.at[i]))
+        copies[-1].start()
+    for copy in copies:
+        copy.wait()
+
+
+def search(pieces, layout, weights, extra, base, twist, phases, blocks, templates):
     block_rows = pieces[0].shape[0]
     rows = block_rows * blocks
     strides = STRIDE_TABLE + (8,)
     segments = block_rows // 8
-    heights = [min(LANES, 16 * stride + 16) for stride in strides]
-    smem = pl.BlockSpec(memory_space=pltpu.SMEM)
+    heights = [min(LANES, 16 * stride + 8) for stride in strides]
     vmem = pl.BlockSpec(memory_space=pltpu.VMEM)
     scratch = [
         ((2 * rows + 16, LANES), F32),
         ((rows + 16, LANES), F32),
         ((rows + 16, LANES), F32),
         ((2, LANES, 4 * segments), F32),
-        ((2, block_rows, LANES), F32),
-    ] + len(strides) * [((block_rows, 4 * LANES), BF16)] + 2 * [((templates // 2, 2, height, block_rows // 2), F32) for height in heights]
+        ((templates, block_rows, LANES), F32),
+        ((block_rows * templates, LANES), F32),
+    ] + len(strides) * [((block_rows, 4 * LANES), BF16)] + GROUPS * [((templates // GROUPS, 2, height, block_rows // 2), F32) for height in heights]
     used = sum(math.prod(shape) * jnp.dtype(kind).itemsize for shape, kind in scratch)
     return pl.pallas_call(
         functools.partial(search_kernel, strides, (block_rows, blocks, templates, layout)),
         out_shape=jax.ShapeDtypeStruct((block_rows * templates, LANES), F32),
-        in_specs=[smem, smem] + [vmem] * (3 + len(pieces)),
-        out_specs=vmem,
+        in_specs=[pl.BlockSpec(memory_space=pl.ANY)] + [vmem] * (4 + len(pieces)),
+        out_specs=pl.BlockSpec(memory_space=pltpu.HBM),
         scratch_shapes=[
-            *[pltpu.VMEM(shape, kind) for shape, kind in scratch],
+            *[pltpu.VMEM(shape, kind) for shape, kind in scratch[:6]],
+            pltpu.SMEM(phases.shape, jnp.int32),
+            pltpu.SemaphoreType.DMA((4,)),
+            *[pltpu.VMEM(shape, kind) for shape, kind in scratch[6:]],
         ],
         compiler_params=pltpu.CompilerParams(vmem_limit_bytes=used + 12 * 2**20),
         name="search",
     )(
-        place,
-        harm_map,
+        phases,
         base,
         twist,
         *pieces,
         weights,
+        extra,
     )
 
 
@@ -303,16 +338,12 @@
     block_rows = block_len // LANES
     blocks = lax.axis_size("bins")
     templates = fdot_index.shape[0]
-    device = lax.axis_index("bins")
-    peer = lax.axis_index("fdot")
-    part = peer & 1
-    place = jnp.stack([device, part, (peer >> 1) & 1]).astype(jnp.int32)
+    part = lax.axis_index("fdot") & 1
     packed = spectrum.reshape(2, block_rows, LANES).transpose(1, 0, 2).reshape(2 * block_rows, LANES)
     mine = lax.dynamic_slice(packed, (part * block_rows, jnp.int32(0)), (block_rows, LANES))
     far = [from_across(mine, pair) for pair in range(2, blocks, 2)]
-    steps = harm_map.reshape(-1, 4)
-    fdot_index, steps, place = lax.optimization_barrier((fdot_index, steps, place))
-    weights, base, twist = template_rows(bank, fdot_index, block_rows * blocks)
+    fdot_index, phases = lax.optimization_barrier((fdot_index, harm_map[:, 0, 3]))
+    weights, extra, base, twist = template_rows(bank, fdot_index, block_rows * blocks)
     sent, base = lax.optimization_barrier((mine, base))
     held = [sent, from_partner(sent, "bins", 1)]
     layout = [(0, 0), (1, 0)]
@@ -321,7 +352,7 @@
         held += [value, from_partner(value, "fdot", 2)]
         layout += [(pair, 1), (pair, 0)]
     passed = [from_partner(value, "fdot", 1) for value in held]
-    out = search(held + passed, layout, weights, base, twist, steps, place, blocks, templates)
+    out = search(held + passed, layout, weights, extra, base, twist, phases, blocks, templates)
     return out.reshape(block_rows, templates, LANES).transpose(1, 0, 2).reshape(templates, block_len)
 
 

time: 24.9 us -> 23.2 us (0.932)
  the two profiles are of different devices: /device:TPU:0 before, /device:TPU:27 now
where the time goes in v4:
time: 23.2 us; the launch traced here: 23 us
  waiting for transfers between devices  9.57 us (41%)
  Pallas kernels  6.95 us (30%)
  starting transfers between devices  3.33 us (14%)
  local copies, waits for them, and re-layouts  3.14 us (14%)
    pallas_call x1, Pallas kernels, search(): pl.pallas_call(functools.partial(search_kernel, strides, (block_rows, blo...  6.02 us
    ppermute x1, waiting for transfers between devices, from_across(): return lax.ppermute(value, ('bins', 'fdot'), pairs)  5.65 us
    ppermute x6, waiting for transfers between devices, from_partner(): return lax.ppermute(value, axis, pairs)  3.91 us
    ppermute x6, starting transfers between devices, from_partner(): return lax.ppermute(value, axis, pairs)  3.21 us
    unnamed x6, local copies, waits for them, and re-layouts  2.44 us
    pallas_call x1, Pallas kernels, template_rows(): pl.pallas_call(functools.partial(template_kernel, math.pi / (rows * LANES...  0.93 us
    squeeze x1, local copies, waits for them, and re-layouts, body(): harm_map[:, 0, 3]  0.68 us
  transfers between devices with their start and end apart: 7, of which 4 were waited for; matrix products, arithmetic and copies ran while one was open for 3% of the time, Pallas kernels for 4%

profile of v4, /device:TPU:27, one launch (start us, length us, event | category | flops | bytes accessed | tf_op | source)
XLA Modules:
  0.0 23.0 jit_solution(8536068634444850540)
XLA Ops:
  0.0 0.0 copy-start
  0.0 0.9 %copy-done = f32[2,32768]{1,0:T(2,128)S(1)} copy-done((f32[2,32768]{1,0:T(2,128)S(1)}, f32[2,32768]{1,0:T(2,128)}, u32[]{:S(2)}) %copy-start) | copy-done | bytes 262168
  1.0 0.1 collective-permute-start.1
  1.1 0.7 %slice_bitcast_fusion.phase_hbm = s32[7]{0:T(128)S(1)} fusion(s32[7,1,4]{0,2,1:T(4,128)} %param.7), kind=kLoop, calls=%fused_computation | loop fusion | bytes 56 | tf_op jit(solution)/shard_map/squeeze | solution.py:345
  1.8 0.0 copy-start.1
  1.8 0.8 %copy-done.1 = bf16[128,2,128]{2,1,0:T(2,128)(2,1)S(1)} copy-done((bf16[128,2,128]{2,1,0:T(2,128)(2,1)S(1)}, bf16[128,2,128]{2,1,0:T(2,128)(2,1)}, u32[]{:S(2)}) %copy-start.1) | copy-done | bytes 65560
  2.6 0.0 copy-start.2
  2.6 0.7 %copy-done.2 = s32[8]{0:T(128)S(1)} copy-done((s32[8]{0:T(128)S(1)}, s32[8]{0:T(128)}, u32[]{:S(2)}) %copy-start.2) | copy-done | bytes 56
  3.3 0.9 %template_rows.1 = (bf16[2048,512]{1,0:T(8,128)(2,1)S(1)}, bf16[224,512]{1,0:T(8,128)(2,1)S(1)}, f32[16,128]{1,0:T(8,128)S(1)}, f32[2,128,128]{2,1,0:T(8,128)S(1)}) custom-call(s32[8]{0:T(128)S(1)} %copy-done.2, bf16[128,2,128]{2,1,0:T(2,128)(2,1)S(1)} %copy-done.1), custom_call_target="tpu_custom_call" | custom-call | flops 1048576 | bytes 2097152 | tf_op jit(solution)/shard_map/template_rows/pallas_call | solution.py:80
  4.2 0.2 %collective-permute-start = (f32[256,128]{1,0:T(8,128)S(1)}, f32[256,128]{1,0:T(8,128)S(1)}, u32[]{:S(2)}, u32[]{:S(2)}) collective-permute-start(f32[256,128]{1,0:T(8,128)S(1)} %constant_dynamic-slice_fusion.refs_0_), channel_id=1, source_target_pairs={{0,4},{4,0},{8,12},{12,8},{1,5},{5,1},{9,13},{13,9},{2,6},{6,2},{1... | collective-permute-start | bytes 393224 | tf_op jit(solution)/shard_map/ppermute | solution.py:20
  4.4 5.7 %collective-permute-done.1.refs_2_ = f32[256,128]{1,0:T(8,128)S(1)} collective-permute-done((f32[256,128]{1,0:T(8,128)S(1)}, f32[256,128]{1,0:T(8,128)S(1)}, u32[]{:S(2)}, u32[]{:S(2)}) %collective-permute-start.1) | collective-permute-done | bytes 131104 | tf_op jit(solution)/shard_map/ppermute | solution.py:333
  10.1 0.0 collective-permute-start.2
  10.1 0.6 %collective-permute-start.3 = (f32[256,128]{1,0:T(8,128)S(1)}, f32[256,128]{1,0:T(8,128)S(1)}, u32[]{:S(2)}, u32[]{:S(2)}) collective-permute-start(f32[256,128]{1,0:T(8,128)S(1)} %constant_dynamic-slice_fusion.refs_0_), channel_id=1, source_target_pairs={{0,1},{1,0},{2,3},{3,2},{4,5},{5,4},{6,7},{7,6},{8,9},{9,8},{10,11... | collective-permute-start | bytes 393224 | tf_op jit(solution)/shard_map/ppermute | solution.py:20
  10.6 0.0 collective-permute-start.5
  10.7 1.2 %collective-permute-done.refs_1_ = f32[256,128]{1,0:T(8,128)S(1)} collective-permute-done((f32[256,128]{1,0:T(8,128)S(1)}, f32[256,128]{1,0:T(8,128)S(1)}, u32[]{:S(2)}, u32[]{:S(2)}) %collective-permute-start) | collective-permute-done | bytes 131104 | tf_op jit(solution)/shard_map/ppermute | solution.py:20
  11.9 1.0 %collective-permute-start.4 = (f32[256,128]{1,0:T(8,128)S(1)}, f32[256,128]{1,0:T(8,128)S(1)}, u32[]{:S(2)}, u32[]{:S(2)}) collective-permute-start(f32[256,128]{1,0:T(8,128)S(1)} %collective-permute-done.refs_1_), channel_id=1, source_target_pairs={{0,1},{1,0},{2,3},{3,2},{4,5},{5,4},{6,7},{7,6},{8,9},{9,8},{10,11... | collective-permute-start | bytes 393224 | tf_op jit(solution)/shard_map/ppermute | solution.py:20
  12.9 1.7 %collective-permute-done.2.refs_3_ = f32[256,128]{1,0:T(8,128)S(1)} collective-permute-done((f32[256,128]{1,0:T(8,128)S(1)}, f32[256,128]{1,0:T(8,128)S(1)}, u32[]{:S(2)}, u32[]{:S(2)}) %collective-permute-start.2) | collective-permute-done | bytes 131104 | tf_op jit(solution)/shard_map/ppermute | solution.py:20
  14.6 1.4 %collective-permute-start.6 = (f32[256,128]{1,0:T(8,128)S(1)}, f32[256,128]{1,0:T(8,128)S(1)}, u32[]{:S(2)}, u32[]{:S(2)}) collective-permute-start(f32[256,128]{1,0:T(8,128)S(1)} %collective-permute-done.2.refs_3_), channel_id=1, source_target_pairs={{0,1},{1,0},{2,3},{3,2},{4,5},{5,4},{6,7},{7,6},{8,9},{9,8},{10,11... | collective-permute-start | bytes 393224 | tf_op jit(solution)/shard_map/ppermute | solution.py:20
  16.0 0.0 collective-permute-done.3.refs_4_
  16.0 0.0 collective-permute-done.5.refs_6_
  16.0 0.0 collective-permute-done.4.refs_5_
  16.0 1.0 %collective-permute-done.6.refs_7_ = f32[256,128]{1,0:T(8,128)S(1)} collective-permute-done((f32[256,128]{1,0:T(8,128)S(1)}, f32[256,128]{1,0:T(8,128)S(1)}, u32[]{:S(2)}, u32[]{:S(2)}) %collective-permute-start.6) | collective-permute-done | bytes 131104 | tf_op jit(solution)/shard_map/ppermute | solution.py:20
  17.0 6.0 %search.1 = f32[2048,128]{1,0:T(8,128)} custom-call(s32[7]{0:T(128)S(1)} %slice_bitcast_fusion.phase_hbm, f32[16,128]{1,0:T(8,128)S(1)} %get-tuple-element.17.base_ref, f32[2,128,128]{2,1,0:T(8,128)S(1)} %get-tuple-element.18.twist_ref, f32[256,128]{1,0:T(8,128)S(1)} %constant_dynamic-slice_fusion.refs_0_, f32[256,128]{1,0:T(8,128)S(1)} %collective-permute-done.refs_1_, ...), custom_call_target="tpu_custom_call" | custom-call | tf_op jit(solution)/shard_map/search/pallas_call | solution.py:303
  (1 shorter events, 0.0 us)
Async XLA Ops:
  0.0 1.0 %copy-start = (f32[2,32768]{1,0:T(2,128)S(1)}, f32[2,32768]{1,0:T(2,128)}, u32[]{:S(2)}) copy-start(f32[2,32768]{1,0:T(2,128)} %param.4) | copy-start | bytes 786436
  1.0 9.1 %collective-permute-start.1 = (f32[256,128]{1,0:T(8,128)S(1)}, f32[256,128]{1,0:T(8,128)S(1)}, u32[]{:S(2)}, u32[]{:S(2)}) collective-permute-start(f32[256,128]{1,0:T(8,128)S(1)} %constant_dynamic-slice_fusion.refs_0_), channel_id=1, source_target_pairs={{0,12},{1,13},{2,10},{3,11},{4,8},{5,9},{6,14},{7,15},{8,4},{9,5},... | collective-permute-start | bytes 393224 | tf_op jit(solution)/shard_map/ppermute | solution.py:333
  1.8 0.8 %copy-start.1 = (bf16[128,2,128]{2,1,0:T(2,128)(2,1)S(1)}, bf16[128,2,128]{2,1,0:T(2,128)(2,1)}, u32[]{:S(2)}) copy-start(bf16[128,2,128]{2,1,0:T(2,128)(2,1)} %bank_hbm.1) | copy-start | bytes 196612
  2.6 0.7 %copy-start.2 = (s32[8]{0:T(128)S(1)}, s32[8]{0:T(128)}, u32[]{:S(2)}) copy-start(s32[8]{0:T(128)} %index_hbm) | copy-start | bytes 100
  4.2 7.7 %collective-permute-start = (f32[256,128]{1,0:T(8,128)S(1)}, f32[256,128]{1,0:T(8,128)S(1)}, u32[]{:S(2)}, u32[]{:S(2)}) collective-permute-start(f32[256,128]{1,0:T(8,128)S(1)} %constant_dynamic-slice_fusion.refs_0_), channel_id=1, source_target_pairs={{0,4},{4,0},{8,12},{12,8},{1,5},{5,1},{9,13},{13,9},{2,6},{6,2},{1... | collective-permute-start | bytes 393224 | tf_op jit(solution)/shard_map/ppermute | solution.py:20
  10.1 4.5 %collective-permute-start.2 = (f32[256,128]{1,0:T(8,128)S(1)}, f32[256,128]{1,0:T(8,128)S(1)}, u32[]{:S(2)}, u32[]{:S(2)}) collective-permute-start(f32[256,128]{1,0:T(8,128)S(1)} %collective-permute-done.1.refs_2_), channel_id=1, source_target_pairs={{0,2},{1,3},{2,0},{3,1},{4,6},{5,7},{6,4},{7,5},{8,10},{9,11},{10,... | collective-permute-start | bytes 393224 | tf_op jit(solution)/shard_map/ppermute | solution.py:20
  10.1 5.9 %collective-permute-start.3 = (f32[256,128]{1,0:T(8,128)S(1)}, f32[256,128]{1,0:T(8,128)S(1)}, u32[]{:S(2)}, u32[]{:S(2)}) collective-permute-start(f32[256,128]{1,0:T(8,128)S(1)} %constant_dynamic-slice_fusion.refs_0_), channel_id=1, source_target_pairs={{0,1},{1,0},{2,3},{3,2},{4,5},{5,4},{6,7},{7,6},{8,9},{9,8},{10,11... | collective-permute-start | bytes 393224 | tf_op jit(solution)/shard_map/ppermute | solution.py:20
  10.6 5.4 %collective-permute-start.5 = (f32[256,128]{1,0:T(8,128)S(1)}, f32[256,128]{1,0:T(8,128)S(1)}, u32[]{:S(2)}, u32[]{:S(2)}) collective-permute-start(f32[256,128]{1,0:T(8,128)S(1)} %collective-permute-done.1.refs_2_), channel_id=1, source_target_pairs={{0,1},{1,0},{2,3},{3,2},{4,5},{5,4},{6,7},{7,6},{8,9},{9,8},{10,11... | collective-permute-start | bytes 393224 | tf_op jit(solution)/shard_map/ppermute | solution.py:20
  11.9 4.1 %collective-permute-start.4 = (f32[256,128]{1,0:T(8,128)S(1)}, f32[256,128]{1,0:T(8,128)S(1)}, u32[]{:S(2)}, u32[]{:S(2)}) collective-permute-start(f32[256,128]{1,0:T(8,128)S(1)} %collective-permute-done.refs_1_), channel_id=1, source_target_pairs={{0,1},{1,0},{2,3},{3,2},{4,5},{5,4},{6,7},{7,6},{8,9},{9,8},{10,11... | collective-permute-start | bytes 393224 | tf_op jit(solution)/shard_map/ppermute | solution.py:20
  14.6 2.4 %collective-permute-start.6 = (f32[256,128]{1,0:T(8,128)S(1)}, f32[256,128]{1,0:T(8,128)S(1)}, u32[]{:S(2)}, u32[]{:S(2)}) collective-permute-start(f32[256,128]{1,0:T(8,128)S(1)} %collective-permute-done.2.refs_3_), channel_id=1, source_target_pairs={{0,1},{1,0},{2,3},{3,2},{4,5},{5,4},{6,7},{7,6},{8,9},{9,8},{10,11... | collective-permute-start | bytes 393224 | tf_op jit(solution)/shard_map/ppermute | solution.py:20

commit v5 on v4

--- a/solution.py
+++ b/solution.py
@@ -103,7 +103,7 @@
 def search_kernel(strides, sizes, phase_hbm, base_ref, twist_ref, *refs):
     block_rows, blocks, templates, layout = sizes
     pieces = refs[: 2 * len(layout)]
-    weights, extra, out_hbm, raw, real, imag, acc, flat, ready, phase_ref, out_sem, *more = refs[2 * len(layout) :]
+    weights, extra, out_hbm, raw, real, imag, acc, flat, phase_ref, out_sem, *more = refs[2 * len(layout) :]
     windows = more[: len(strides)]
     more = more[len(strides) :]
     groups = GROUPS
@@ -216,6 +216,8 @@
                     at = (2 * c + half) * LANES
                     windows[n][o * segments : (o + 1) * segments, at : at + LANES] = tile
 
+    copies = []
+
     def add_up(t, h):
         total = [None] * 8
         for n, stride in enumerate(strides):
@@ -235,6 +237,9 @@
         turned = acc[(2 * t + h) % 2].T
         for o in range(4):
             flat[t, pl.ds(4 * h + o, segments, stride=8), :] = turned[o * segments : (o + 1) * segments, :]
+        if h:
+            copies.append(pltpu.make_async_copy(flat.at[t], out_hbm.at[:, t, :], out_sem.at[t]))
+            copies[-1].start()
 
     phase_copy.wait()
     for g in range(groups):
@@ -270,16 +275,6 @@
                     add_up((g - 1) * share + unit // 2, unit % 2)
     for unit in range(2 * share):
         add_up((groups - 1) * share + unit // 2, unit % 2)
-    parts = out_sem.shape[0]
-    span = block_rows * templates // parts
-    copies = []
-    for i in range(parts):
-        for m in range(i * segments // parts, (i + 1) * segments // parts):
-            for t in range(templates):
-                ready[pl.ds(8 * templates * m + t, 8, stride=templates), :] = flat[t, 8 * m : 8 * m + 8, :]
-        done = pl.ds(i * span, span)
-        copies.append(pltpu.make_async_copy(ready.at[done, :], out_hbm.at[done, :], out_sem.at[i]))
-        copies[-1].start()
     for copy in copies:
         copy.wait()
 
@@ -297,19 +292,18 @@
         ((rows + 16, LANES), F32),
         ((2, LANES, 4 * segments), F32),
         ((templates, block_rows, LANES), F32),
-        ((block_rows * templates, LANES), F32),
     ] + len(strides) * [((block_rows, 4 * LANES), BF16)] + GROUPS * [((templates // GROUPS, 2, height, block_rows // 2), F32) for height in heights]
     used = sum(math.prod(shape) * jnp.dtype(kind).itemsize for shape, kind in scratch)
     return pl.pallas_call(
         functools.partial(search_kernel, strides, (block_rows, blocks, templates, layout)),
-        out_shape=jax.ShapeDtypeStruct((block_rows * templates, LANES), F32),
+        out_shape=jax.ShapeDtypeStruct((block_rows, templates, LANES), F32),
         in_specs=[pl.BlockSpec(memory_space=pl.ANY)] + [vmem] * (4 + len(pieces)),
         out_specs=pl.BlockSpec(memory_space=pltpu.HBM),
         scratch_shapes=[
-            *[pltpu.VMEM(shape, kind) for shape, kind in scratch[:6]],
+            *[pltpu.VMEM(shape, kind) for shape, kind in scratch[:5]],
             pltpu.SMEM(phases.shape, jnp.int32),
-            pltpu.SemaphoreType.DMA((4,)),
-            *[pltpu.VMEM(shape, kind) for shape, kind in scratch[6:]],
+            pltpu.SemaphoreType.DMA((templates,)),
+            *[pltpu.VMEM(shape, kind) for shape, kind in scratch[5:]],
         ],
         compiler_params=pltpu.CompilerParams(vmem_limit_bytes=used + 12 * 2**20),
         name="search",
@@ -353,7 +347,7 @@
         layout += [(pair, 1), (pair, 0)]
     passed = [from_partner(value, "fdot", 1) for value in held]
     out = search(held + passed, layout, weights, extra, base, twist, phases, blocks, templates)
-    return out.reshape(block_rows, templates, LANES).transpose(1, 0, 2).reshape(templates, block_len)
+    return out.transpose(1, 0, 2).reshape(templates, block_len)
 
 
 def solution(mesh):

time: 23.2 us -> 23 us (level)
  the two profiles are of different devices: /device:TPU:27 before, /device:TPU:31 now
where the time goes in v5:
time: 23 us; the launch traced here: 22.7 us
  waiting for transfers between devices  9.57 us (42%)
  Pallas kernels  6.67 us (29%)
  starting transfers between devices  3.33 us (14%)
  local copies, waits for them, and re-layouts  3.14 us (14%)
    pallas_call x1, Pallas kernels, search(): pl.pallas_call(functools.partial(search_kernel, strides, (block_rows, blo...  5.74 us
    ppermute x1, waiting for transfers between devices, from_across(): return lax.ppermute(value, ('bins', 'fdot'), pairs)  5.65 us
    ppermute x6, waiting for transfers between devices, from_partner(): return lax.ppermute(value, axis, pairs)  3.91 us
    ppermute x6, starting transfers between devices, from_partner(): return lax.ppermute(value, axis, pairs)  3.21 us
    unnamed x6, local copies, waits for them, and re-layouts  2.44 us
    pallas_call x1, Pallas kernels, template_rows(): pl.pallas_call(functools.partial(template_kernel, math.pi / (rows * LANES...  0.93 us
    squeeze x1, local copies, waits for them, and re-layouts, body(): harm_map[:, 0, 3]  0.68 us
  transfers between devices with their start and end apart: 7, of which 4 were waited for; matrix products, arithmetic and copies ran while one was open for 3% of the time, Pallas kernels for 4%

profile of v5, /device:TPU:31, one launch (start us, length us, event | category | flops | bytes accessed | tf_op | source)
XLA Modules:
  0.0 22.7 jit_solution(3466091061136262363)
XLA Ops:
  0.0 0.0 copy-start
  0.0 0.9 %copy-done = f32[2,32768]{1,0:T(2,128)S(1)} copy-done((f32[2,32768]{1,0:T(2,128)S(1)}, f32[2,32768]{1,0:T(2,128)}, u32[]{:S(2)}) %copy-start) | copy-done | bytes 262168
  1.0 0.1 collective-permute-start.1
  1.1 0.7 %slice_bitcast_fusion.phase_hbm = s32[7]{0:T(128)S(1)} fusion(s32[7,1,4]{0,2,1:T(4,128)} %param.7), kind=kLoop, calls=%fused_computation | loop fusion | bytes 56 | tf_op jit(solution)/shard_map/squeeze | solution.py:339
  1.8 0.0 copy-start.1
  1.8 0.8 %copy-done.1 = bf16[128,2,128]{2,1,0:T(2,128)(2,1)S(1)} copy-done((bf16[128,2,128]{2,1,0:T(2,128)(2,1)S(1)}, bf16[128,2,128]{2,1,0:T(2,128)(2,1)}, u32[]{:S(2)}) %copy-start.1) | copy-done | bytes 65560
  2.6 0.0 copy-start.2
  2.6 0.7 %copy-done.2 = s32[8]{0:T(128)S(1)} copy-done((s32[8]{0:T(128)S(1)}, s32[8]{0:T(128)}, u32[]{:S(2)}) %copy-start.2) | copy-done | bytes 56
  3.3 0.9 %template_rows.1 = (bf16[2048,512]{1,0:T(8,128)(2,1)S(1)}, bf16[224,512]{1,0:T(8,128)(2,1)S(1)}, f32[16,128]{1,0:T(8,128)S(1)}, f32[2,128,128]{2,1,0:T(8,128)S(1)}) custom-call(s32[8]{0:T(128)S(1)} %copy-done.2, bf16[128,2,128]{2,1,0:T(2,128)(2,1)S(1)} %copy-done.1), custom_call_target="tpu_custom_call" | custom-call | flops 1048576 | bytes 2097152 | tf_op jit(solution)/shard_map/template_rows/pallas_call | solution.py:80
  4.2 0.2 %collective-permute-start = (f32[256,128]{1,0:T(8,128)S(1)}, f32[256,128]{1,0:T(8,128)S(1)}, u32[]{:S(2)}, u32[]{:S(2)}) collective-permute-start(f32[256,128]{1,0:T(8,128)S(1)} %constant_dynamic-slice_fusion.refs_0_), channel_id=1, source_target_pairs={{0,4},{4,0},{8,12},{12,8},{1,5},{5,1},{9,13},{13,9},{2,6},{6,2},{1... | collective-permute-start | bytes 393224 | tf_op jit(solution)/shard_map/ppermute | solution.py:20
  4.4 5.7 %collective-permute-done.1.refs_2_ = f32[256,128]{1,0:T(8,128)S(1)} collective-permute-done((f32[256,128]{1,0:T(8,128)S(1)}, f32[256,128]{1,0:T(8,128)S(1)}, u32[]{:S(2)}, u32[]{:S(2)}) %collective-permute-start.1) | collective-permute-done | bytes 131104 | tf_op jit(solution)/shard_map/ppermute | solution.py:327
  10.1 0.0 collective-permute-start.2
  10.1 0.6 %collective-permute-start.3 = (f32[256,128]{1,0:T(8,128)S(1)}, f32[256,128]{1,0:T(8,128)S(1)}, u32[]{:S(2)}, u32[]{:S(2)}) collective-permute-start(f32[256,128]{1,0:T(8,128)S(1)} %constant_dynamic-slice_fusion.refs_0_), channel_id=1, source_target_pairs={{0,1},{1,0},{2,3},{3,2},{4,5},{5,4},{6,7},{7,6},{8,9},{9,8},{10,11... | collective-permute-start | bytes 393224 | tf_op jit(solution)/shard_map/ppermute | solution.py:20
  10.6 0.0 collective-permute-start.5
  10.7 1.2 %collective-permute-done.refs_1_ = f32[256,128]{1,0:T(8,128)S(1)} collective-permute-done((f32[256,128]{1,0:T(8,128)S(1)}, f32[256,128]{1,0:T(8,128)S(1)}, u32[]{:S(2)}, u32[]{:S(2)}) %collective-permute-start) | collective-permute-done | bytes 131104 | tf_op jit(solution)/shard_map/ppermute | solution.py:20
  11.9 1.0 %collective-permute-start.4 = (f32[256,128]{1,0:T(8,128)S(1)}, f32[256,128]{1,0:T(8,128)S(1)}, u32[]{:S(2)}, u32[]{:S(2)}) collective-permute-start(f32[256,128]{1,0:T(8,128)S(1)} %collective-permute-done.refs_1_), channel_id=1, source_target_pairs={{0,1},{1,0},{2,3},{3,2},{4,5},{5,4},{6,7},{7,6},{8,9},{9,8},{10,11... | collective-permute-start | bytes 393224 | tf_op jit(solution)/shard_map/ppermute | solution.py:20
  12.9 1.7 %collective-permute-done.2.refs_3_ = f32[256,128]{1,0:T(8,128)S(1)} collective-permute-done((f32[256,128]{1,0:T(8,128)S(1)}, f32[256,128]{1,0:T(8,128)S(1)}, u32[]{:S(2)}, u32[]{:S(2)}) %collective-permute-start.2) | collective-permute-done | bytes 131104 | tf_op jit(solution)/shard_map/ppermute | solution.py:20
  14.6 1.4 %collective-permute-start.6 = (f32[256,128]{1,0:T(8,128)S(1)}, f32[256,128]{1,0:T(8,128)S(1)}, u32[]{:S(2)}, u32[]{:S(2)}) collective-permute-start(f32[256,128]{1,0:T(8,128)S(1)} %collective-permute-done.2.refs_3_), channel_id=1, source_target_pairs={{0,1},{1,0},{2,3},{3,2},{4,5},{5,4},{6,7},{7,6},{8,9},{9,8},{10,11... | collective-permute-start | bytes 393224 | tf_op jit(solution)/shard_map/ppermute | solution.py:20
  16.0 0.0 collective-permute-done.3.refs_4_
  16.0 0.0 collective-permute-done.5.refs_6_
  16.0 0.0 collective-permute-done.4.refs_5_
  16.0 1.0 %collective-permute-done.6.refs_7_ = f32[256,128]{1,0:T(8,128)S(1)} collective-permute-done((f32[256,128]{1,0:T(8,128)S(1)}, f32[256,128]{1,0:T(8,128)S(1)}, u32[]{:S(2)}, u32[]{:S(2)}) %collective-permute-start.6) | collective-permute-done | bytes 131104 | tf_op jit(solution)/shard_map/ppermute | solution.py:20
  17.0 5.7 %search.1 = f32[256,8,128]{2,1,0:T(8,128)} custom-call(s32[7]{0:T(128)S(1)} %slice_bitcast_fusion.phase_hbm, f32[16,128]{1,0:T(8,128)S(1)} %get-tuple-element.17.base_ref, f32[2,128,128]{2,1,0:T(8,128)S(1)} %get-tuple-element.18.twist_ref, f32[256,128]{1,0:T(8,128)S(1)} %constant_dynamic-slice_fusion.refs_0_, f32[256,128]{1,0:T(8,128)S(1)} %collective-permute-done.refs_1_, ...), custom_call_target="tpu_custom_call" | custom-call | tf_op jit(solution)/shard_map/search/pallas_call | solution.py:297
  (1 shorter events, 0.0 us)
Async XLA Ops:
  0.0 1.0 %copy-start = (f32[2,32768]{1,0:T(2,128)S(1)}, f32[2,32768]{1,0:T(2,128)}, u32[]{:S(2)}) copy-start(f32[2,32768]{1,0:T(2,128)} %param.4) | copy-start | bytes 786436
  1.0 9.1 %collective-permute-start.1 = (f32[256,128]{1,0:T(8,128)S(1)}, f32[256,128]{1,0:T(8,128)S(1)}, u32[]{:S(2)}, u32[]{:S(2)}) collective-permute-start(f32[256,128]{1,0:T(8,128)S(1)} %constant_dynamic-slice_fusion.refs_0_), channel_id=1, source_target_pairs={{0,12},{1,13},{2,10},{3,11},{4,8},{5,9},{6,14},{7,15},{8,4},{9,5},... | collective-permute-start | bytes 393224 | tf_op jit(solution)/shard_map/ppermute | solution.py:327
  1.8 0.8 %copy-start.1 = (bf16[128,2,128]{2,1,0:T(2,128)(2,1)S(1)}, bf16[128,2,128]{2,1,0:T(2,128)(2,1)}, u32[]{:S(2)}) copy-start(bf16[128,2,128]{2,1,0:T(2,128)(2,1)} %bank_hbm.1) | copy-start | bytes 196612
  2.6 0.7 %copy-start.2 = (s32[8]{0:T(128)S(1)}, s32[8]{0:T(128)}, u32[]{:S(2)}) copy-start(s32[8]{0:T(128)} %index_hbm) | copy-start | bytes 100
  4.2 7.7 %collective-permute-start = (f32[256,128]{1,0:T(8,128)S(1)}, f32[256,128]{1,0:T(8,128)S(1)}, u32[]{:S(2)}, u32[]{:S(2)}) collective-permute-start(f32[256,128]{1,0:T(8,128)S(1)} %constant_dynamic-slice_fusion.refs_0_), channel_id=1, source_target_pairs={{0,4},{4,0},{8,12},{12,8},{1,5},{5,1},{9,13},{13,9},{2,6},{6,2},{1... | collective-permute-start | bytes 393224 | tf_op jit(solution)/shard_map/ppermute | solution.py:20
  10.1 4.5 %collective-permute-start.2 = (f32[256,128]{1,0:T(8,128)S(1)}, f32[256,128]{1,0:T(8,128)S(1)}, u32[]{:S(2)}, u32[]{:S(2)}) collective-permute-start(f32[256,128]{1,0:T(8,128)S(1)} %collective-permute-done.1.refs_2_), channel_id=1, source_target_pairs={{0,2},{1,3},{2,0},{3,1},{4,6},{5,7},{6,4},{7,5},{8,10},{9,11},{10,... | collective-permute-start | bytes 393224 | tf_op jit(solution)/shard_map/ppermute | solution.py:20
  10.1 5.9 %collective-permute-start.3 = (f32[256,128]{1,0:T(8,128)S(1)}, f32[256,128]{1,0:T(8,128)S(1)}, u32[]{:S(2)}, u32[]{:S(2)}) collective-permute-start(f32[256,128]{1,0:T(8,128)S(1)} %constant_dynamic-slice_fusion.refs_0_), channel_id=1, source_target_pairs={{0,1},{1,0},{2,3},{3,2},{4,5},{5,4},{6,7},{7,6},{8,9},{9,8},{10,11... | collective-permute-start | bytes 393224 | tf_op jit(solution)/shard_map/ppermute | solution.py:20
  10.6 5.4 %collective-permute-start.5 = (f32[256,128]{1,0:T(8,128)S(1)}, f32[256,128]{1,0:T(8,128)S(1)}, u32[]{:S(2)}, u32[]{:S(2)}) collective-permute-start(f32[256,128]{1,0:T(8,128)S(1)} %collective-permute-done.1.refs_2_), channel_id=1, source_target_pairs={{0,1},{1,0},{2,3},{3,2},{4,5},{5,4},{6,7},{7,6},{8,9},{9,8},{10,11... | collective-permute-start | bytes 393224 | tf_op jit(solution)/shard_map/ppermute | solution.py:20
  11.9 4.1 %collective-permute-start.4 = (f32[256,128]{1,0:T(8,128)S(1)}, f32[256,128]{1,0:T(8,128)S(1)}, u32[]{:S(2)}, u32[]{:S(2)}) collective-permute-start(f32[256,128]{1,0:T(8,128)S(1)} %collective-permute-done.refs_1_), channel_id=1, source_target_pairs={{0,1},{1,0},{2,3},{3,2},{4,5},{5,4},{6,7},{7,6},{8,9},{9,8},{10,11... | collective-permute-start | bytes 393224 | tf_op jit(solution)/shard_map/ppermute | solution.py:20
  14.6 2.4 %collective-permute-start.6 = (f32[256,128]{1,0:T(8,128)S(1)}, f32[256,128]{1,0:T(8,128)S(1)}, u32[]{:S(2)}, u32[]{:S(2)}) collective-permute-start(f32[256,128]{1,0:T(8,128)S(1)} %collective-permute-done.2.refs_3_), channel_id=1, source_target_pairs={{0,1},{1,0},{2,3},{3,2},{4,5},{5,4},{6,7},{7,6},{8,9},{9,8},{10,11... | collective-permute-start | bytes 393224 | tf_op jit(solution)/shard_map/ppermute | solution.py:20

commit v6 on v5

--- a/solution.py
+++ b/solution.py
@@ -115,14 +115,14 @@
     device = lax.axis_index("bins")
     peer = lax.axis_index("fdot")
     part = peer & 1
-    column = (peer >> 1) & 1
+    column = (peer ^ (peer >> 1)) & 1
     phase_copy = pltpu.make_async_copy(phase_hbm, phase_ref, out_sem.at[0])
     phase_copy.start()
 
     sums = [jnp.zeros((8, LANES), F32)] * 4
     for i, source in enumerate(pieces):
         pair, cross = layout[i % len(layout)]
-        mask = pair + (1 - column if cross else column) if pair > 1 else pair
+        mask = pair + (column if cross == (i >= len(layout)) else 1 - column) if pair > 1 else pair
         half = part if i < len(layout) else 1 - part
         start = pl.multiple_of((device ^ mask) * (2 * block_rows) + half * block_rows, block_rows)
         for j in range(block_rows // 8):
@@ -199,22 +199,26 @@
     wide_lanes = lax.broadcasted_iota(jnp.int32, (segments, LANES), 1)
     def make_windows(n, stride):
         first_row = device * (block_rows * stride // 8) + 8
+        made = {}
+
+        def tile_at(c, row, shift):
+            if (c, row, shift) not in made:
+                source = (real, imag)[c]
+                tile = source[pl.ds(first_row + row, segments, stride=stride), :]
+                if shift:
+                    after = source[pl.ds(first_row + row + 1, segments, stride=stride), :]
+                    tile = jnp.where(wide_lanes >= shift, tile, after).astype(BF16)
+                    made[c, row, shift] = pltpu.roll(tile, LANES - shift, 1)
+                else:
+                    made[c, row, shift] = tile.astype(BF16)
+            return made[c, row, shift]
+
         for o in range(8):
-            ahead = 2 * stride * 8 * o - LANES // 2
-            skip, shift = ahead // LANES, ahead % LANES
-            for c, source in enumerate((real, imag)):
-                tiles = [
-                    source[pl.ds(first_row + (skip + j), segments, stride=stride), :]
-                    for j in range(3 if shift else 2)
-                ]
+            skip, shift = divmod(16 * stride * o - LANES // 2, LANES)
+            for c in range(2):
                 for half in range(2):
-                    if shift:
-                        tile = jnp.where(wide_lanes >= shift, tiles[half], tiles[half + 1])
-                        tile = pltpu.roll(tile.astype(BF16), LANES - shift, 1)
-                    else:
-                        tile = tiles[half].astype(BF16)
                     at = (2 * c + half) * LANES
-                    windows[n][o * segments : (o + 1) * segments, at : at + LANES] = tile
+                    windows[n][o * segments : (o + 1) * segments, at : at + LANES] = tile_at(c, skip + half, shift)
 
     copies = []
 
@@ -222,19 +226,17 @@
         total = [None] * 8
         for n, stride in enumerate(strides):
             plane = planes[t // share][n].at[t % share, h]
-            if stride == 8:
-                values = [plane[pl.ds(b, LANES // 8, stride=8), :] for b in range(8)]
-            else:
+            if stride < 8:
                 starts = [plane[pl.ds(c, LANES // 8, stride=stride), :] for c in range(stride + 1)]
                 values = []
                 for b in range(8):
                     least = stride * b // 8
                     ahead = phase_ref[n] + stride * b >= 8 * (least + 1)
                     values.append(jnp.where(ahead, starts[least + 1], starts[least]))
-            total = values if n == 0 else [x + y for x, y in zip(total, values)]
+                total = values if n == 0 else [x + y for x, y in zip(total, values)]
         for b in range(8):
-            acc[(2 * t + h) % 2, pl.ds(b, LANES // 8, stride=8), :] = total[b] * 0.125
-        turned = acc[(2 * t + h) % 2].T
+            acc[(2 * t + h) % 2, pl.ds(b, LANES // 8, stride=8), :] = total[b]
+        turned = ((acc[(2 * t + h) % 2] + planes[t // share][len(strides) - 1][t % share, h]) * 0.125).T
         for o in range(4):
             flat[t, pl.ds(4 * h + o, segments, stride=8), :] = turned[o * segments : (o + 1) * segments, :]
         if h:
@@ -320,7 +322,7 @@
 def from_across(value, pair):
     blocks, peers = lax.axis_size("bins"), lax.axis_size("fdot")
     pairs = [
-        (peers * d + f, peers * (d ^ (pair + 1 - (f >> 1) % 2)) + f)
+        (peers * d + f, peers * (d ^ (pair + 1 - (f ^ (f >> 1)) % 2)) + f)
         for d in range(blocks)
         for f in range(peers)
     ]

time: 23 us -> 22.5 us (0.978)
  the two profiles are of different devices: /device:TPU:31 before, /device:TPU:0 now
where the time goes in v6:
time: 22.5 us; the launch traced here: 22.3 us
  starting transfers between devices  9.01 us (40%)
  Pallas kernels  5.89 us (26%)
  waiting for transfers between devices  4.22 us (19%)
  local copies, waits for them, and re-layouts  3.14 us (14%)
    ppermute x1, starting transfers between devices, from_across(): return lax.ppermute(value, ('bins', 'fdot'), pairs)  5.11 us
    pallas_call x1, Pallas kernels, search(): pl.pallas_call(functools.partial(search_kernel, strides, (block_rows, blo...  4.96 us
    ppermute x6, starting transfers between devices, from_partner(): return lax.ppermute(value, axis, pairs)  3.9 us
    ppermute x6, waiting for transfers between devices, from_partner(): return lax.ppermute(value, axis, pairs)  3.76 us
    unnamed x6, local copies, waits for them, and re-layouts  2.44 us
    pallas_call x1, Pallas kernels, template_rows(): pl.pallas_call(functools.partial(template_kernel, math.pi / (rows * LANES...  0.93 us
    squeeze x1, local copies, waits for them, and re-layouts, body(): harm_map[:, 0, 3]  0.68 us
    ppermute x1, waiting for transfers between devices, from_across(): return lax.ppermute(value, ('bins', 'fdot'), pairs)  0.45 us
  transfers between devices with their start and end apart: 7, of which 4 were waited for; matrix products, arithmetic and copies ran while one was open for 3% of the time, Pallas kernels for 4%

profile of v6, /device:TPU:0, one launch (start us, length us, event | category | flops | bytes accessed | tf_op | source)
XLA Modules:
  0.0 22.3 jit_solution(15411449080072332897)
XLA Ops:
  0.0 0.0 copy-start
  0.0 0.9 %copy-done = f32[2,32768]{1,0:T(2,128)S(1)} copy-done((f32[2,32768]{1,0:T(2,128)S(1)}, f32[2,32768]{1,0:T(2,128)}, u32[]{:S(2)}) %copy-start) | copy-done | bytes 262168
  1.0 5.1 %collective-permute-start.1 = (f32[256,128]{1,0:T(8,128)S(1)}, f32[256,128]{1,0:T(8,128)S(1)}, u32[]{:S(2)}, u32[]{:S(2)}) collective-permute-start(f32[256,128]{1,0:T(8,128)S(1)} %constant_dynamic-slice_fusion.refs_0_), channel_id=1, source_target_pairs={{0,12},{1,9},{2,10},{3,15},{4,8},{5,13},{6,14},{7,11},{8,4},{9,1},... | collective-permute-start | bytes 393224 | tf_op jit(solution)/shard_map/ppermute | solution.py:329
  6.1 0.7 %slice_bitcast_fusion.phase_hbm = s32[7]{0:T(128)S(1)} fusion(s32[7,1,4]{0,2,1:T(4,128)} %param.7), kind=kLoop, calls=%fused_computation | loop fusion | bytes 56 | tf_op jit(solution)/shard_map/squeeze | solution.py:341
  6.8 0.0 copy-start.1
  6.8 0.8 %copy-done.1 = bf16[128,2,128]{2,1,0:T(2,128)(2,1)S(1)} copy-done((bf16[128,2,128]{2,1,0:T(2,128)(2,1)S(1)}, bf16[128,2,128]{2,1,0:T(2,128)(2,1)}, u32[]{:S(2)}) %copy-start.1) | copy-done | bytes 65560
  7.6 0.0 copy-start.2
  7.6 0.7 %copy-done.2 = s32[8]{0:T(128)S(1)} copy-done((s32[8]{0:T(128)S(1)}, s32[8]{0:T(128)}, u32[]{:S(2)}) %copy-start.2) | copy-done | bytes 56
  8.3 0.9 %template_rows.1 = (bf16[2048,512]{1,0:T(8,128)(2,1)S(1)}, bf16[224,512]{1,0:T(8,128)(2,1)S(1)}, f32[16,128]{1,0:T(8,128)S(1)}, f32[2,128,128]{2,1,0:T(8,128)S(1)}) custom-call(s32[8]{0:T(128)S(1)} %copy-done.2, bf16[128,2,128]{2,1,0:T(2,128)(2,1)S(1)} %copy-done.1), custom_call_target="tpu_custom_call" | custom-call | flops 1048576 | bytes 2097152 | tf_op jit(solution)/shard_map/template_rows/pallas_call | solution.py:80
  9.2 0.1 collective-permute-start
  9.3 0.5 %collective-permute-done.1.refs_2_ = f32[256,128]{1,0:T(8,128)S(1)} collective-permute-done((f32[256,128]{1,0:T(8,128)S(1)}, f32[256,128]{1,0:T(8,128)S(1)}, u32[]{:S(2)}, u32[]{:S(2)}) %collective-permute-start.1) | collective-permute-done | bytes 131104 | tf_op jit(solution)/shard_map/ppermute | solution.py:329
  9.7 3.3 %collective-permute-start.2 = (f32[256,128]{1,0:T(8,128)S(1)}, f32[256,128]{1,0:T(8,128)S(1)}, u32[]{:S(2)}, u32[]{:S(2)}) collective-permute-start(f32[256,128]{1,0:T(8,128)S(1)} %collective-permute-done.1.refs_2_), channel_id=1, source_target_pairs={{0,2},{1,3},{2,0},{3,1},{4,6},{5,7},{6,4},{7,5},{8,10},{9,11},{10,... | collective-permute-start | bytes 393224 | tf_op jit(solution)/shard_map/ppermute | solution.py:20
  13.0 0.0 collective-permute-start.3
  13.0 0.5 %collective-permute-start.5 = (f32[256,128]{1,0:T(8,128)S(1)}, f32[256,128]{1,0:T(8,128)S(1)}, u32[]{:S(2)}, u32[]{:S(2)}) collective-permute-start(f32[256,128]{1,0:T(8,128)S(1)} %collective-permute-done.1.refs_2_), channel_id=1, source_target_pairs={{0,1},{1,0},{2,3},{3,2},{4,5},{5,4},{6,7},{7,6},{8,9},{9,8},{10,11... | collective-permute-start | bytes 393224 | tf_op jit(solution)/shard_map/ppermute | solution.py:20
  13.5 0.7 %collective-permute-done.refs_1_ = f32[256,128]{1,0:T(8,128)S(1)} collective-permute-done((f32[256,128]{1,0:T(8,128)S(1)}, f32[256,128]{1,0:T(8,128)S(1)}, u32[]{:S(2)}, u32[]{:S(2)}) %collective-permute-start) | collective-permute-done | bytes 131104 | tf_op jit(solution)/shard_map/ppermute | solution.py:20
  14.2 0.0 collective-permute-start.4
  14.2 1.8 %collective-permute-done.2.refs_3_ = f32[256,128]{1,0:T(8,128)S(1)} collective-permute-done((f32[256,128]{1,0:T(8,128)S(1)}, f32[256,128]{1,0:T(8,128)S(1)}, u32[]{:S(2)}, u32[]{:S(2)}) %collective-permute-start.2) | collective-permute-done | bytes 131104 | tf_op jit(solution)/shard_map/ppermute | solution.py:20
  16.0 0.0 collective-permute-start.6
  16.0 0.0 collective-permute-done.3.refs_4_
  16.0 0.0 collective-permute-done.5.refs_6_
  16.0 0.0 collective-permute-done.4.refs_5_
  16.0 1.3 %collective-permute-done.6.refs_7_ = f32[256,128]{1,0:T(8,128)S(1)} collective-permute-done((f32[256,128]{1,0:T(8,128)S(1)}, f32[256,128]{1,0:T(8,128)S(1)}, u32[]{:S(2)}, u32[]{:S(2)}) %collective-permute-start.6) | collective-permute-done | bytes 131104 | tf_op jit(solution)/shard_map/ppermute | solution.py:20
  17.3 5.0 %search.1 = f32[256,8,128]{2,1,0:T(8,128)} custom-call(s32[7]{0:T(128)S(1)} %slice_bitcast_fusion.phase_hbm, f32[16,128]{1,0:T(8,128)S(1)} %get-tuple-element.17.base_ref, f32[2,128,128]{2,1,0:T(8,128)S(1)} %get-tuple-element.18.twist_ref, f32[256,128]{1,0:T(8,128)S(1)} %constant_dynamic-slice_fusion.refs_0_, f32[256,128]{1,0:T(8,128)S(1)} %collective-permute-done.refs_1_, ...), custom_call_target="tpu_custom_call" | custom-call | tf_op jit(solution)/shard_map/search/pallas_call | solution.py:299
  (1 shorter events, 0.0 us)
Async XLA Ops:
  0.0 1.0 %copy-start = (f32[2,32768]{1,0:T(2,128)S(1)}, f32[2,32768]{1,0:T(2,128)}, u32[]{:S(2)}) copy-start(f32[2,32768]{1,0:T(2,128)} %param.4) | copy-start | bytes 786436
  1.0 8.8 %collective-permute-start.1 = (f32[256,128]{1,0:T(8,128)S(1)}, f32[256,128]{1,0:T(8,128)S(1)}, u32[]{:S(2)}, u32[]{:S(2)}) collective-permute-start(f32[256,128]{1,0:T(8,128)S(1)} %constant_dynamic-slice_fusion.refs_0_), channel_id=1, source_target_pairs={{0,12},{1,9},{2,10},{3,15},{4,8},{5,13},{6,14},{7,11},{8,4},{9,1},... | collective-permute-start | bytes 393224 | tf_op jit(solution)/shard_map/ppermute | solution.py:329
  6.8 0.8 %copy-start.1 = (bf16[128,2,128]{2,1,0:T(2,128)(2,1)S(1)}, bf16[128,2,128]{2,1,0:T(2,128)(2,1)}, u32[]{:S(2)}) copy-start(bf16[128,2,128]{2,1,0:T(2,128)(2,1)} %bank_hbm.1) | copy-start | bytes 196612
  7.6 0.7 %copy-start.2 = (s32[8]{0:T(128)S(1)}, s32[8]{0:T(128)}, u32[]{:S(2)}) copy-start(s32[8]{0:T(128)} %index_hbm) | copy-start | bytes 100
  9.2 5.0 %collective-permute-start = (f32[256,128]{1,0:T(8,128)S(1)}, f32[256,128]{1,0:T(8,128)S(1)}, u32[]{:S(2)}, u32[]{:S(2)}) collective-permute-start(f32[256,128]{1,0:T(8,128)S(1)} %constant_dynamic-slice_fusion.refs_0_), channel_id=1, source_target_pairs={{0,4},{4,0},{8,12},{12,8},{1,5},{5,1},{9,13},{13,9},{2,6},{6,2},{1... | collective-permute-start | bytes 393224 | tf_op jit(solution)/shard_map/ppermute | solution.py:20
  9.7 6.3 %collective-permute-start.2 = (f32[256,128]{1,0:T(8,128)S(1)}, f32[256,128]{1,0:T(8,128)S(1)}, u32[]{:S(2)}, u32[]{:S(2)}) collective-permute-start(f32[256,128]{1,0:T(8,128)S(1)} %collective-permute-done.1.refs_2_), channel_id=1, source_target_pairs={{0,2},{1,3},{2,0},{3,1},{4,6},{5,7},{6,4},{7,5},{8,10},{9,11},{10,... | collective-permute-start | bytes 393224 | tf_op jit(solution)/shard_map/ppermute | solution.py:20
  13.0 3.0 %collective-permute-start.3 = (f32[256,128]{1,0:T(8,128)S(1)}, f32[256,128]{1,0:T(8,128)S(1)}, u32[]{:S(2)}, u32[]{:S(2)}) collective-permute-start(f32[256,128]{1,0:T(8,128)S(1)} %constant_dynamic-slice_fusion.refs_0_), channel_id=1, source_target_pairs={{0,1},{1,0},{2,3},{3,2},{4,5},{5,4},{6,7},{7,6},{8,9},{9,8},{10,11... | collective-permute-start | bytes 393224 | tf_op jit(solution)/shard_map/ppermute | solution.py:20
  13.0 3.0 %collective-permute-start.5 = (f32[256,128]{1,0:T(8,128)S(1)}, f32[256,128]{1,0:T(8,128)S(1)}, u32[]{:S(2)}, u32[]{:S(2)}) collective-permute-start(f32[256,128]{1,0:T(8,128)S(1)} %collective-permute-done.1.refs_2_), channel_id=1, source_target_pairs={{0,1},{1,0},{2,3},{3,2},{4,5},{5,4},{6,7},{7,6},{8,9},{9,8},{10,11... | collective-permute-start | bytes 393224 | tf_op jit(solution)/shard_map/ppermute | solution.py:20
  14.2 1.8 %collective-permute-start.4 = (f32[256,128]{1,0:T(8,128)S(1)}, f32[256,128]{1,0:T(8,128)S(1)}, u32[]{:S(2)}, u32[]{:S(2)}) collective-permute-start(f32[256,128]{1,0:T(8,128)S(1)} %collective-permute-done.refs_1_), channel_id=1, source_target_pairs={{0,1},{1,0},{2,3},{3,2},{4,5},{5,4},{6,7},{7,6},{8,9},{9,8},{10,11... | collective-permute-start | bytes 393224 | tf_op jit(solution)/shard_map/ppermute | solution.py:20
  16.0 1.3 %collective-permute-start.6 = (f32[256,128]{1,0:T(8,128)S(1)}, f32[256,128]{1,0:T(8,128)S(1)}, u32[]{:S(2)}, u32[]{:S(2)}) collective-permute-start(f32[256,128]{1,0:T(8,128)S(1)} %collective-permute-done.2.refs_3_), channel_id=1, source_target_pairs={{0,1},{1,0},{2,3},{3,2},{4,5},{5,4},{6,7},{7,6},{8,9},{9,8},{10,11... | collective-permute-start | bytes 393224 | tf_op jit(solution)/shard_map/ppermute | solution.py:20

commit v7 on v6

--- a/solution.py
+++ b/solution.py
@@ -21,9 +21,9 @@
 
 
 def template_kernel(
-    step, groups, index_hbm, bank_hbm, out_ref, extra_ref, base_ref, twist_ref, index_ref, bank_ref, sem
+    step, groups, index_hbm, phase_hbm, bank_hbm, out_ref, extra_ref, base_ref, twist_ref, wide_ref, index_ref, phase_ref, bank_ref, sem
 ):
-    pairs = ((index_hbm, index_ref), (bank_hbm, bank_ref))
+    pairs = ((index_hbm, index_ref), (bank_hbm, bank_ref), (phase_hbm, phase_ref))
     copies = [pltpu.make_async_copy(source, to, sem.at[i]) for i, (source, to) in enumerate(pairs)]
     for copy in copies:
         copy.start()
@@ -71,39 +71,45 @@
             extra_ref[low : low + 16, : 2 * LANES] = jnp.concatenate([real, imag]).astype(BF16)
             extra_ref[low : low + 16, 2 * LANES :] = jnp.concatenate([-imag, real]).astype(BF16)
 
-
-def template_rows(bank, fdot_index, rows):
+    copies[2].wait()
+    for n in range(phase_ref.shape[0]):
+        wide_ref[16 * n : 16 * n + 16, :] = jnp.full((16, LANES), phase_ref[n], jnp.int32)
+
+
+def template_rows(bank, fdot_index, phases, rows):
     count = fdot_index.shape[0]
     taps = bank.shape[2]
     height = 2 * count * taps
     vmem = pl.BlockSpec(memory_space=pltpu.VMEM)
     return pl.pallas_call(
         functools.partial(template_kernel, math.pi / (rows * LANES), GROUPS),
-        in_specs=[pl.BlockSpec(memory_space=pltpu.HBM)] * 2,
-        out_specs=[vmem] * 4,
+        in_specs=[pl.BlockSpec(memory_space=pltpu.HBM)] * 3,
+        out_specs=[vmem] * 5,
         out_shape=[
             jax.ShapeDtypeStruct((height, 4 * taps), BF16),
             jax.ShapeDtypeStruct((16 * GROUPS * len(STRIDE_TABLE), 4 * taps), BF16),
             jax.ShapeDtypeStruct((16, LANES), F32),
             jax.ShapeDtypeStruct((2, rows // 8, LANES), F32),
+            jax.ShapeDtypeStruct((16 * phases.shape[0], LANES), jnp.int32),
         ],
         scratch_shapes=[
             pltpu.SMEM(fdot_index.shape, jnp.int32),
+            pltpu.SMEM(phases.shape, jnp.int32),
             pltpu.VMEM(bank.shape, BF16),
-            pltpu.SemaphoreType.DMA((2,)),
+            pltpu.SemaphoreType.DMA((3,)),
         ],
         cost_estimate=pl.CostEstimate(
             flops=4 * height * taps, bytes_accessed=8 * height * taps, transcendentals=0
         ),
         compiler_params=pltpu.CompilerParams(vmem_limit_bytes=16 * 2**20),
         name="template_rows",
-    )(fdot_index, bank)
-
-
-def search_kernel(strides, sizes, phase_hbm, base_ref, twist_ref, *refs):
+    )(fdot_index, phases, bank)
+
+
+def search_kernel(strides, sizes, phase_ref, base_ref, twist_ref, *refs):
     block_rows, blocks, templates, layout = sizes
     pieces = refs[: 2 * len(layout)]
-    weights, extra, out_hbm, raw, real, imag, acc, flat, phase_ref, out_sem, *more = refs[2 * len(layout) :]
+    weights, extra, out_hbm, raw, real, imag, acc, flat, out_sem, *more = refs[2 * len(layout) :]
     windows = more[: len(strides)]
     more = more[len(strides) :]
     groups = GROUPS
@@ -116,8 +122,6 @@
     peer = lax.axis_index("fdot")
     part = peer & 1
     column = (peer ^ (peer >> 1)) & 1
-    phase_copy = pltpu.make_async_copy(phase_hbm, phase_ref, out_sem.at[0])
-    phase_copy.start()
 
     sums = [jnp.zeros((8, LANES), F32)] * 4
     for i, source in enumerate(pieces):
@@ -185,7 +189,7 @@
         imag[place, :] = out_imag * half_scale
         return 0
 
-    group = 16
+    group = 32
     lowest = jnp.maximum(device * (block_rows // 8) - 1, 0) // (8 * group)
     highest = jnp.minimum(((device + 1) * block_rows + 8 * group) // (8 * group), rows // (8 * group))
 
@@ -228,11 +232,13 @@
             plane = planes[t // share][n].at[t % share, h]
             if stride < 8:
                 starts = [plane[pl.ds(c, LANES // 8, stride=stride), :] for c in range(stride + 1)]
+                phase = phase_ref[16 * n : 16 * n + 16, :]
+                ahead = {over: phase >= 8 - over for over in {stride * b % 8 for b in range(8)} if over}
                 values = []
                 for b in range(8):
-                    least = stride * b // 8
-                    ahead = phase_ref[n] + stride * b >= 8 * (least + 1)
-                    values.append(jnp.where(ahead, starts[least + 1], starts[least]))
+                    least, over = divmod(stride * b, 8)
+                    value = starts[least]
+                    values.append(jnp.where(ahead[over], starts[least + 1], value) if over else value)
                 total = values if n == 0 else [x + y for x, y in zip(total, values)]
         for b in range(8):
             acc[(2 * t + h) % 2, pl.ds(b, LANES // 8, stride=8), :] = total[b]
@@ -243,7 +249,6 @@
             copies.append(pltpu.make_async_copy(flat.at[t], out_hbm.at[:, t, :], out_sem.at[t]))
             copies[-1].start()
 
-    phase_copy.wait()
     for g in range(groups):
         own = weights[2 * g * share * LANES : 2 * (g + 1) * share * LANES, :]
         own = own.reshape(2 * share, LANES, 4 * LANES)
@@ -299,11 +304,10 @@
     return pl.pallas_call(
         functools.partial(search_kernel, strides, (block_rows, blocks, templates, layout)),
         out_shape=jax.ShapeDtypeStruct((block_rows, templates, LANES), F32),
-        in_specs=[pl.BlockSpec(memory_space=pl.ANY)] + [vmem] * (4 + len(pieces)),
+        in_specs=[vmem] * (5 + len(pieces)),
         out_specs=pl.BlockSpec(memory_space=pltpu.HBM),
         scratch_shapes=[
             *[pltpu.VMEM(shape, kind) for shape, kind in scratch[:5]],
-            pltpu.SMEM(phases.shape, jnp.int32),
             pltpu.SemaphoreType.DMA((templates,)),
             *[pltpu.VMEM(shape, kind) for shape, kind in scratch[5:]],
         ],
@@ -339,7 +343,7 @@
     mine = lax.dynamic_slice(packed, (part * block_rows, jnp.int32(0)), (block_rows, LANES))
     far = [from_across(mine, pair) for pair in range(2, blocks, 2)]
     fdot_index, phases = lax.optimization_barrier((fdot_index, harm_map[:, 0, 3]))
-    weights, extra, base, twist = template_rows(bank, fdot_index, block_rows * blocks)
+    weights, extra, base, twist, phases = template_rows(bank, fdot_index, phases, block_rows * blocks)
     sent, base = lax.optimization_barrier((mine, base))
     held = [sent, from_partner(sent, "bins", 1)]
     layout = [(0, 0), (1, 0)]

time: 22.5 us -> 22.6 us (level)
  no operation moved by 1% of the time
where the time goes in v7:
time: 22.6 us; the launch traced here: 22.3 us
  starting transfers between devices  9.01 us (40%)
  Pallas kernels  5.97 us (26%)
  waiting for transfers between devices  4.19 us (19%)
  local copies, waits for them, and re-layouts  3.14 us (14%)
    ppermute x1, starting transfers between devices, from_across(): return lax.ppermute(value, ('bins', 'fdot'), pairs)  5.11 us
    pallas_call x1, Pallas kernels, search(): pl.pallas_call(functools.partial(search_kernel, strides, (block_rows, blo...  5.02 us
    ppermute x6, starting transfers between devices, from_partner(): return lax.ppermute(value, axis, pairs)  3.89 us
    ppermute x6, waiting for transfers between devices, from_partner(): return lax.ppermute(value, axis, pairs)  3.76 us
    unnamed x6, local copies, waits for them, and re-layouts  2.44 us
    pallas_call x1, Pallas kernels, template_rows(): pl.pallas_call(functools.partial(template_kernel, math.pi / (rows * LANES...  0.95 us
    squeeze x1, local copies, waits for them, and re-layouts, body(): harm_map[:, 0, 3]  0.68 us
  transfers between devices with their start and end apart: 7, of which 4 were waited for; matrix products, arithmetic and copies ran while one was open for 3% of the time, Pallas kernels for 4%

profile of v7, /device:TPU:0, one launch (start us, length us, event | category | flops | bytes accessed | tf_op | source)
XLA Modules:
  0.0 22.3 jit_solution(5877653193364614443)
XLA Ops:
  0.0 0.0 copy-start
  0.0 0.9 %copy-done = f32[2,32768]{1,0:T(2,128)S(1)} copy-done((f32[2,32768]{1,0:T(2,128)S(1)}, f32[2,32768]{1,0:T(2,128)}, u32[]{:S(2)}) %copy-start) | copy-done | bytes 262168
  1.0 5.1 %collective-permute-start.1 = (f32[256,128]{1,0:T(8,128)S(1)}, f32[256,128]{1,0:T(8,128)S(1)}, u32[]{:S(2)}, u32[]{:S(2)}) collective-permute-start(f32[256,128]{1,0:T(8,128)S(1)} %constant_dynamic-slice_fusion.refs_0_), channel_id=1, source_target_pairs={{0,12},{1,9},{2,10},{3,15},{4,8},{5,13},{6,14},{7,11},{8,4},{9,1},... | collective-permute-start | bytes 393224 | tf_op jit(solution)/shard_map/ppermute | solution.py:333
  6.1 0.7 %slice_bitcast_fusion.phase_hbm = s32[7]{0:T(128)S(1)} fusion(s32[7,1,4]{0,2,1:T(4,128)} %param.7), kind=kLoop, calls=%fused_computation | loop fusion | bytes 56 | tf_op jit(solution)/shard_map/squeeze | solution.py:345
  6.8 0.0 copy-start.1
  6.8 0.8 %copy-done.1 = bf16[128,2,128]{2,1,0:T(2,128)(2,1)S(1)} copy-done((bf16[128,2,128]{2,1,0:T(2,128)(2,1)S(1)}, bf16[128,2,128]{2,1,0:T(2,128)(2,1)}, u32[]{:S(2)}) %copy-start.1) | copy-done | bytes 65560
  7.6 0.0 copy-start.2
  7.6 0.7 %copy-done.2 = s32[8]{0:T(128)S(1)} copy-done((s32[8]{0:T(128)S(1)}, s32[8]{0:T(128)}, u32[]{:S(2)}) %copy-start.2) | copy-done | bytes 56
  8.3 0.9 %template_rows.1 = (bf16[2048,512]{1,0:T(8,128)(2,1)S(1)}, bf16[224,512]{1,0:T(8,128)(2,1)S(1)}, f32[16,128]{1,0:T(8,128)S(1)}, f32[2,128,128]{2,1,0:T(8,128)S(1)}, s32[112,128]{1,0:T(8,128)S(1)}) custom-call(s32[8]{0:T(128)S(1)} %copy-done.2, s32[7]{0:T(128)S(1)} %slice_bitcast_fusion.phase_hbm, bf16[128,2,128]{2,1,0:T(2,128)(2,1)S(1)} %copy-done.1), custom_call_target="tpu_custom_call" | custom-call | flops 1048576 | bytes 2097152 | tf_op jit(solution)/shard_map/template_rows/pallas_call | solution.py:84
  9.2 0.1 collective-permute-start
  9.3 0.4 %collective-permute-done.1.refs_2_ = f32[256,128]{1,0:T(8,128)S(1)} collective-permute-done((f32[256,128]{1,0:T(8,128)S(1)}, f32[256,128]{1,0:T(8,128)S(1)}, u32[]{:S(2)}, u32[]{:S(2)}) %collective-permute-start.1) | collective-permute-done | bytes 131104 | tf_op jit(solution)/shard_map/ppermute | solution.py:333
  9.7 3.3 %collective-permute-start.2 = (f32[256,128]{1,0:T(8,128)S(1)}, f32[256,128]{1,0:T(8,128)S(1)}, u32[]{:S(2)}, u32[]{:S(2)}) collective-permute-start(f32[256,128]{1,0:T(8,128)S(1)} %collective-permute-done.1.refs_2_), channel_id=1, source_target_pairs={{0,2},{1,3},{2,0},{3,1},{4,6},{5,7},{6,4},{7,5},{8,10},{9,11},{10,... | collective-permute-start | bytes 393224 | tf_op jit(solution)/shard_map/ppermute | solution.py:20
  13.0 0.0 collective-permute-start.3
  13.0 0.5 %collective-permute-start.5 = (f32[256,128]{1,0:T(8,128)S(1)}, f32[256,128]{1,0:T(8,128)S(1)}, u32[]{:S(2)}, u32[]{:S(2)}) collective-permute-start(f32[256,128]{1,0:T(8,128)S(1)} %collective-permute-done.1.refs_2_), channel_id=1, source_target_pairs={{0,1},{1,0},{2,3},{3,2},{4,5},{5,4},{6,7},{7,6},{8,9},{9,8},{10,11... | collective-permute-start | bytes 393224 | tf_op jit(solution)/shard_map/ppermute | solution.py:20
  13.5 0.7 %collective-permute-done.refs_1_ = f32[256,128]{1,0:T(8,128)S(1)} collective-permute-done((f32[256,128]{1,0:T(8,128)S(1)}, f32[256,128]{1,0:T(8,128)S(1)}, u32[]{:S(2)}, u32[]{:S(2)}) %collective-permute-start) | collective-permute-done | bytes 131104 | tf_op jit(solution)/shard_map/ppermute | solution.py:20
  14.3 0.0 collective-permute-start.4
  14.3 1.7 %collective-permute-done.2.refs_3_ = f32[256,128]{1,0:T(8,128)S(1)} collective-permute-done((f32[256,128]{1,0:T(8,128)S(1)}, f32[256,128]{1,0:T(8,128)S(1)}, u32[]{:S(2)}, u32[]{:S(2)}) %collective-permute-start.2) | collective-permute-done | bytes 131104 | tf_op jit(solution)/shard_map/ppermute | solution.py:20
  16.0 0.0 collective-permute-start.6
  16.0 0.0 collective-permute-done.3.refs_4_
  16.0 0.0 collective-permute-done.5.refs_6_
  16.0 0.0 collective-permute-done.4.refs_5_
  16.0 1.3 %collective-permute-done.6.refs_7_ = f32[256,128]{1,0:T(8,128)S(1)} collective-permute-done((f32[256,128]{1,0:T(8,128)S(1)}, f32[256,128]{1,0:T(8,128)S(1)}, u32[]{:S(2)}, u32[]{:S(2)}) %collective-permute-start.6) | collective-permute-done | bytes 131104 | tf_op jit(solution)/shard_map/ppermute | solution.py:20
  17.3 5.0 %search.1 = f32[256,8,128]{2,1,0:T(8,128)} custom-call(s32[112,128]{1,0:T(8,128)S(1)} %get-tuple-element.17.phase_ref, f32[16,128]{1,0:T(8,128)S(1)} %get-tuple-element.19.base_ref, f32[2,128,128]{2,1,0:T(8,128)S(1)} %get-tuple-element.20.twist_ref, f32[256,128]{1,0:T(8,128)S(1)} %constant_dynamic-slice_fusion.refs_0_, ...), custom_call_target="tpu_custom_call" | custom-call | tf_op jit(solution)/shard_map/search/pallas_call | solution.py:304
  (1 shorter events, 0.0 us)
Async XLA Ops:
  0.0 1.0 %copy-start = (f32[2,32768]{1,0:T(2,128)S(1)}, f32[2,32768]{1,0:T(2,128)}, u32[]{:S(2)}) copy-start(f32[2,32768]{1,0:T(2,128)} %param.4) | copy-start | bytes 786436
  1.0 8.8 %collective-permute-start.1 = (f32[256,128]{1,0:T(8,128)S(1)}, f32[256,128]{1,0:T(8,128)S(1)}, u32[]{:S(2)}, u32[]{:S(2)}) collective-permute-start(f32[256,128]{1,0:T(8,128)S(1)} %constant_dynamic-slice_fusion.refs_0_), channel_id=1, source_target_pairs={{0,12},{1,9},{2,10},{3,15},{4,8},{5,13},{6,14},{7,11},{8,4},{9,1},... | collective-permute-start | bytes 393224 | tf_op jit(solution)/shard_map/ppermute | solution.py:333
  6.8 0.8 %copy-start.1 = (bf16[128,2,128]{2,1,0:T(2,128)(2,1)S(1)}, bf16[128,2,128]{2,1,0:T(2,128)(2,1)}, u32[]{:S(2)}) copy-start(bf16[128,2,128]{2,1,0:T(2,128)(2,1)} %bank_hbm.1) | copy-start | bytes 196612
  7.6 0.7 %copy-start.2 = (s32[8]{0:T(128)S(1)}, s32[8]{0:T(128)}, u32[]{:S(2)}) copy-start(s32[8]{0:T(128)} %index_hbm) | copy-start | bytes 100
  9.2 5.0 %collective-permute-start = (f32[256,128]{1,0:T(8,128)S(1)}, f32[256,128]{1,0:T(8,128)S(1)}, u32[]{:S(2)}, u32[]{:S(2)}) collective-permute-start(f32[256,128]{1,0:T(8,128)S(1)} %constant_dynamic-slice_fusion.refs_0_), channel_id=1, source_target_pairs={{0,4},{4,0},{8,12},{12,8},{1,5},{5,1},{9,13},{13,9},{2,6},{6,2},{1... | collective-permute-start | bytes 393224 | tf_op jit(solution)/shard_map/ppermute | solution.py:20
  9.7 6.3 %collective-permute-start.2 = (f32[256,128]{1,0:T(8,128)S(1)}, f32[256,128]{1,0:T(8,128)S(1)}, u32[]{:S(2)}, u32[]{:S(2)}) collective-permute-start(f32[256,128]{1,0:T(8,128)S(1)} %collective-permute-done.1.refs_2_), channel_id=1, source_target_pairs={{0,2},{1,3},{2,0},{3,1},{4,6},{5,7},{6,4},{7,5},{8,10},{9,11},{10,... | collective-permute-start | bytes 393224 | tf_op jit(solution)/shard_map/ppermute | solution.py:20
  13.0 3.0 %collective-permute-start.3 = (f32[256,128]{1,0:T(8,128)S(1)}, f32[256,128]{1,0:T(8,128)S(1)}, u32[]{:S(2)}, u32[]{:S(2)}) collective-permute-start(f32[256,128]{1,0:T(8,128)S(1)} %constant_dynamic-slice_fusion.refs_0_), channel_id=1, source_target_pairs={{0,1},{1,0},{2,3},{3,2},{4,5},{5,4},{6,7},{7,6},{8,9},{9,8},{10,11... | collective-permute-start | bytes 393224 | tf_op jit(solution)/shard_map/ppermute | solution.py:20
  13.0 3.0 %collective-permute-start.5 = (f32[256,128]{1,0:T(8,128)S(1)}, f32[256,128]{1,0:T(8,128)S(1)}, u32[]{:S(2)}, u32[]{:S(2)}) collective-permute-start(f32[256,128]{1,0:T(8,128)S(1)} %collective-permute-done.1.refs_2_), channel_id=1, source_target_pairs={{0,1},{1,0},{2,3},{3,2},{4,5},{5,4},{6,7},{7,6},{8,9},{9,8},{10,11... | collective-permute-start | bytes 393224 | tf_op jit(solution)/shard_map/ppermute | solution.py:20
  14.3 1.7 %collective-permute-start.4 = (f32[256,128]{1,0:T(8,128)S(1)}, f32[256,128]{1,0:T(8,128)S(1)}, u32[]{:S(2)}, u32[]{:S(2)}) collective-permute-start(f32[256,128]{1,0:T(8,128)S(1)} %collective-permute-done.refs_1_), channel_id=1, source_target_pairs={{0,1},{1,0},{2,3},{3,2},{4,5},{5,4},{6,7},{7,6},{8,9},{9,8},{10,11... | collective-permute-start | bytes 393224 | tf_op jit(solution)/shard_map/ppermute | solution.py:20
  16.0 1.3 %collective-permute-start.6 = (f32[256,128]{1,0:T(8,128)S(1)}, f32[256,128]{1,0:T(8,128)S(1)}, u32[]{:S(2)}, u32[]{:S(2)}) collective-permute-start(f32[256,128]{1,0:T(8,128)S(1)} %collective-permute-done.2.refs_3_), channel_id=1, source_target_pairs={{0,1},{1,0},{2,3},{3,2},{4,5},{5,4},{6,7},{7,6},{8,9},{9,8},{10,11... | collective-permute-start | bytes 393224 | tf_op jit(solution)/shard_map/ppermute | solution.py:20

commit v8 on v7

--- a/solution.py
+++ b/solution.py
@@ -12,7 +12,7 @@
 STRIDE_TABLE = (4, 2, 6, 1, 3, 5, 7)
 F32 = jnp.float32
 BF16 = jnp.bfloat16
-GROUPS = 2
+GROUPS = 1
 
 
 def from_partner(value, axis, mask):

time: 22.6 us -> 22.4 us (level)
  no operation moved by 1% of the time
where the time goes in v8:
time: 22.4 us; the launch traced here: 22.2 us
  starting transfers between devices  9.01 us (40%)
  Pallas kernels  5.79 us (26%)
  waiting for transfers between devices  4.21 us (19%)
  local copies, waits for them, and re-layouts  3.14 us (14%)
    ppermute x1, starting transfers between devices, from_across(): return lax.ppermute(value, ('bins', 'fdot'), pairs)  5.11 us
    pallas_call x1, Pallas kernels, search(): pl.pallas_call(functools.partial(search_kernel, strides, (block_rows, blo...  4.85 us
    ppermute x6, starting transfers between devices, from_partner(): return lax.ppermute(value, axis, pairs)  3.9 us
    ppermute x6, waiting for transfers between devices, from_partner(): return lax.ppermute(value, axis, pairs)  3.76 us
    unnamed x6, local copies, waits for them, and re-layouts  2.44 us
    pallas_call x1, Pallas kernels, template_rows(): pl.pallas_call(functools.partial(template_kernel, math.pi / (rows * LANES...  0.93 us
    squeeze x1, local copies, waits for them, and re-layouts, body(): harm_map[:, 0, 3]  0.68 us
    ppermute x1, waiting for transfers between devices, from_across(): return lax.ppermute(value, ('bins', 'fdot'), pairs)  0.45 us
  transfers between devices with their start and end apart: 7, of which 4 were waited for; matrix products, arithmetic and copies ran while one was open for 3% of the time, Pallas kernels for 4%

profile of v8, /device:TPU:0, one launch (start us, length us, event | category | flops | bytes accessed | tf_op | source)
XLA Modules:
  0.0 22.2 jit_solution(9791323929019602752)
XLA Ops:
  0.0 0.0 copy-start
  0.0 0.9 %copy-done = f32[2,32768]{1,0:T(2,128)S(1)} copy-done((f32[2,32768]{1,0:T(2,128)S(1)}, f32[2,32768]{1,0:T(2,128)}, u32[]{:S(2)}) %copy-start) | copy-done | bytes 262168
  1.0 5.1 %collective-permute-start.1 = (f32[256,128]{1,0:T(8,128)S(1)}, f32[256,128]{1,0:T(8,128)S(1)}, u32[]{:S(2)}, u32[]{:S(2)}) collective-permute-start(f32[256,128]{1,0:T(8,128)S(1)} %constant_dynamic-slice_fusion.refs_0_), channel_id=1, source_target_pairs={{0,12},{1,9},{2,10},{3,15},{4,8},{5,13},{6,14},{7,11},{8,4},{9,1},... | collective-permute-start | bytes 393224 | tf_op jit(solution)/shard_map/ppermute | solution.py:333
  6.1 0.7 %slice_bitcast_fusion.phase_hbm = s32[7]{0:T(128)S(1)} fusion(s32[7,1,4]{0,2,1:T(4,128)} %param.7), kind=kLoop, calls=%fused_computation | loop fusion | bytes 56 | tf_op jit(solution)/shard_map/squeeze | solution.py:345
  6.8 0.0 copy-start.1
  6.8 0.8 %copy-done.1 = bf16[128,2,128]{2,1,0:T(2,128)(2,1)S(1)} copy-done((bf16[128,2,128]{2,1,0:T(2,128)(2,1)S(1)}, bf16[128,2,128]{2,1,0:T(2,128)(2,1)}, u32[]{:S(2)}) %copy-start.1) | copy-done | bytes 65560
  7.6 0.0 copy-start.2
  7.6 0.7 %copy-done.2 = s32[8]{0:T(128)S(1)} copy-done((s32[8]{0:T(128)S(1)}, s32[8]{0:T(128)}, u32[]{:S(2)}) %copy-start.2) | copy-done | bytes 56
  8.3 0.9 %template_rows.1 = (bf16[2048,512]{1,0:T(8,128)(2,1)S(1)}, bf16[112,512]{1,0:T(8,128)(2,1)S(1)}, f32[16,128]{1,0:T(8,128)S(1)}, f32[2,128,128]{2,1,0:T(8,128)S(1)}, s32[112,128]{1,0:T(8,128)S(1)}) custom-call(s32[8]{0:T(128)S(1)} %copy-done.2, s32[7]{0:T(128)S(1)} %slice_bitcast_fusion.phase_hbm, bf16[128,2,128]{2,1,0:T(2,128)(2,1)S(1)} %copy-done.1), custom_call_target="tpu_custom_call" | custom-call | flops 1048576 | bytes 2097152 | tf_op jit(solution)/shard_map/template_rows/pallas_call | solution.py:84
  9.2 0.1 collective-permute-start
  9.3 0.4 %collective-permute-done.1.refs_2_ = f32[256,128]{1,0:T(8,128)S(1)} collective-permute-done((f32[256,128]{1,0:T(8,128)S(1)}, f32[256,128]{1,0:T(8,128)S(1)}, u32[]{:S(2)}, u32[]{:S(2)}) %collective-permute-start.1) | collective-permute-done | bytes 131104 | tf_op jit(solution)/shard_map/ppermute | solution.py:333
  9.7 3.3 %collective-permute-start.2 = (f32[256,128]{1,0:T(8,128)S(1)}, f32[256,128]{1,0:T(8,128)S(1)}, u32[]{:S(2)}, u32[]{:S(2)}) collective-permute-start(f32[256,128]{1,0:T(8,128)S(1)} %collective-permute-done.1.refs_2_), channel_id=1, source_target_pairs={{0,2},{1,3},{2,0},{3,1},{4,6},{5,7},{6,4},{7,5},{8,10},{9,11},{10,... | collective-permute-start | bytes 393224 | tf_op jit(solution)/shard_map/ppermute | solution.py:20
  13.0 0.0 collective-permute-start.3
  13.0 0.5 %collective-permute-start.5 = (f32[256,128]{1,0:T(8,128)S(1)}, f32[256,128]{1,0:T(8,128)S(1)}, u32[]{:S(2)}, u32[]{:S(2)}) collective-permute-start(f32[256,128]{1,0:T(8,128)S(1)} %collective-permute-done.1.refs_2_), channel_id=1, source_target_pairs={{0,1},{1,0},{2,3},{3,2},{4,5},{5,4},{6,7},{7,6},{8,9},{9,8},{10,11... | collective-permute-start | bytes 393224 | tf_op jit(solution)/shard_map/ppermute | solution.py:20
  13.5 0.7 %collective-permute-done.refs_1_ = f32[256,128]{1,0:T(8,128)S(1)} collective-permute-done((f32[256,128]{1,0:T(8,128)S(1)}, f32[256,128]{1,0:T(8,128)S(1)}, u32[]{:S(2)}, u32[]{:S(2)}) %collective-permute-start) | collective-permute-done | bytes 131104 | tf_op jit(solution)/shard_map/ppermute | solution.py:20
  14.2 0.0 collective-permute-start.4
  14.2 1.7 %collective-permute-done.2.refs_3_ = f32[256,128]{1,0:T(8,128)S(1)} collective-permute-done((f32[256,128]{1,0:T(8,128)S(1)}, f32[256,128]{1,0:T(8,128)S(1)}, u32[]{:S(2)}, u32[]{:S(2)}) %collective-permute-start.2) | collective-permute-done | bytes 131104 | tf_op jit(solution)/shard_map/ppermute | solution.py:20
  16.0 0.0 collective-permute-start.6
  16.0 0.0 collective-permute-done.3.refs_4_
  16.0 0.0 collective-permute-done.5.refs_6_
  16.0 0.0 collective-permute-done.4.refs_5_
  16.0 1.3 %collective-permute-done.6.refs_7_ = f32[256,128]{1,0:T(8,128)S(1)} collective-permute-done((f32[256,128]{1,0:T(8,128)S(1)}, f32[256,128]{1,0:T(8,128)S(1)}, u32[]{:S(2)}, u32[]{:S(2)}) %collective-permute-start.6) | collective-permute-done | bytes 131104 | tf_op jit(solution)/shard_map/ppermute | solution.py:20
  17.3 4.9 %search.1 = f32[256,8,128]{2,1,0:T(8,128)} custom-call(s32[112,128]{1,0:T(8,128)S(1)} %get-tuple-element.17.phase_ref, f32[16,128]{1,0:T(8,128)S(1)} %get-tuple-element.19.base_ref, f32[2,128,128]{2,1,0:T(8,128)S(1)} %get-tuple-element.20.twist_ref, f32[256,128]{1,0:T(8,128)S(1)} %constant_dynamic-slice_fusion.refs_0_, ...), custom_call_target="tpu_custom_call" | custom-call | tf_op jit(solution)/shard_map/search/pallas_call | solution.py:304
  (1 shorter events, 0.0 us)
Async XLA Ops:
  0.0 1.0 %copy-start = (f32[2,32768]{1,0:T(2,128)S(1)}, f32[2,32768]{1,0:T(2,128)}, u32[]{:S(2)}) copy-start(f32[2,32768]{1,0:T(2,128)} %param.4) | copy-start | bytes 786436
  1.0 8.8 %collective-permute-start.1 = (f32[256,128]{1,0:T(8,128)S(1)}, f32[256,128]{1,0:T(8,128)S(1)}, u32[]{:S(2)}, u32[]{:S(2)}) collective-permute-start(f32[256,128]{1,0:T(8,128)S(1)} %constant_dynamic-slice_fusion.refs_0_), channel_id=1, source_target_pairs={{0,12},{1,9},{2,10},{3,15},{4,8},{5,13},{6,14},{7,11},{8,4},{9,1},... | collective-permute-start | bytes 393224 | tf_op jit(solution)/shard_map/ppermute | solution.py:333
  6.8 0.8 %copy-start.1 = (bf16[128,2,128]{2,1,0:T(2,128)(2,1)S(1)}, bf16[128,2,128]{2,1,0:T(2,128)(2,1)}, u32[]{:S(2)}) copy-start(bf16[128,2,128]{2,1,0:T(2,128)(2,1)} %bank_hbm.1) | copy-start | bytes 196612
  7.6 0.7 %copy-start.2 = (s32[8]{0:T(128)S(1)}, s32[8]{0:T(128)}, u32[]{:S(2)}) copy-start(s32[8]{0:T(128)} %index_hbm) | copy-start | bytes 100
  9.2 5.0 %collective-permute-start = (f32[256,128]{1,0:T(8,128)S(1)}, f32[256,128]{1,0:T(8,128)S(1)}, u32[]{:S(2)}, u32[]{:S(2)}) collective-permute-start(f32[256,128]{1,0:T(8,128)S(1)} %constant_dynamic-slice_fusion.refs_0_), channel_id=1, source_target_pairs={{0,4},{4,0},{8,12},{12,8},{1,5},{5,1},{9,13},{13,9},{2,6},{6,2},{1... | collective-permute-start | bytes 393224 | tf_op jit(solution)/shard_map/ppermute | solution.py:20
  9.7 6.3 %collective-permute-start.2 = (f32[256,128]{1,0:T(8,128)S(1)}, f32[256,128]{1,0:T(8,128)S(1)}, u32[]{:S(2)}, u32[]{:S(2)}) collective-permute-start(f32[256,128]{1,0:T(8,128)S(1)} %collective-permute-done.1.refs_2_), channel_id=1, source_target_pairs={{0,2},{1,3},{2,0},{3,1},{4,6},{5,7},{6,4},{7,5},{8,10},{9,11},{10,... | collective-permute-start | bytes 393224 | tf_op jit(solution)/shard_map/ppermute | solution.py:20
  13.0 3.0 %collective-permute-start.3 = (f32[256,128]{1,0:T(8,128)S(1)}, f32[256,128]{1,0:T(8,128)S(1)}, u32[]{:S(2)}, u32[]{:S(2)}) collective-permute-start(f32[256,128]{1,0:T(8,128)S(1)} %constant_dynamic-slice_fusion.refs_0_), channel_id=1, source_target_pairs={{0,1},{1,0},{2,3},{3,2},{4,5},{5,4},{6,7},{7,6},{8,9},{9,8},{10,11... | collective-permute-start | bytes 393224 | tf_op jit(solution)/shard_map/ppermute | solution.py:20
  13.0 3.0 %collective-permute-start.5 = (f32[256,128]{1,0:T(8,128)S(1)}, f32[256,128]{1,0:T(8,128)S(1)}, u32[]{:S(2)}, u32[]{:S(2)}) collective-permute-start(f32[256,128]{1,0:T(8,128)S(1)} %collective-permute-done.1.refs_2_), channel_id=1, source_target_pairs={{0,1},{1,0},{2,3},{3,2},{4,5},{5,4},{6,7},{7,6},{8,9},{9,8},{10,11... | collective-permute-start | bytes 393224 | tf_op jit(solution)/shard_map/ppermute | solution.py:20
  14.2 1.8 %collective-permute-start.4 = (f32[256,128]{1,0:T(8,128)S(1)}, f32[256,128]{1,0:T(8,128)S(1)}, u32[]{:S(2)}, u32[]{:S(2)}) collective-permute-start(f32[256,128]{1,0:T(8,128)S(1)} %collective-permute-done.refs_1_), channel_id=1, source_target_pairs={{0,1},{1,0},{2,3},{3,2},{4,5},{5,4},{6,7},{7,6},{8,9},{9,8},{10,11... | collective-permute-start | bytes 393224 | tf_op jit(solution)/shard_map/ppermute | solution.py:20
  16.0 1.3 %collective-permute-start.6 = (f32[256,128]{1,0:T(8,128)S(1)}, f32[256,128]{1,0:T(8,128)S(1)}, u32[]{:S(2)}, u32[]{:S(2)}) collective-permute-start(f32[256,128]{1,0:T(8,128)S(1)} %collective-permute-done.2.refs_3_), channel_id=1, source_target_pairs={{0,1},{1,0},{2,3},{3,2},{4,5},{5,4},{6,7},{7,6},{8,9},{9,8},{10,11... | collective-permute-start | bytes 393224 | tf_op jit(solution)/shard_map/ppermute | solution.py:20

commit v9 on v8

--- a/solution.py
+++ b/solution.py
@@ -189,7 +189,7 @@
         imag[place, :] = out_imag * half_scale
         return 0
 
-    group = 32
+    group = 16
     lowest = jnp.maximum(device * (block_rows // 8) - 1, 0) // (8 * group)
     highest = jnp.minimum(((device + 1) * block_rows + 8 * group) // (8 * group), rows // (8 * group))
 

time: 22.4 us -> 22.4 us (level)
  no operation moved by 1% of the time
where the time goes in v9:
time: 22.4 us; the launch traced here: 22.2 us
  starting transfers between devices  9.01 us (40%)
  Pallas kernels  5.78 us (26%)
  waiting for transfers between devices  4.21 us (19%)
  local copies, waits for them, and re-layouts  3.14 us (14%)
    ppermute x1, starting transfers between devices, from_across(): return lax.ppermute(value, ('bins', 'fdot'), pairs)  5.11 us
    pallas_call x1, Pallas kernels, search(): pl.pallas_call(functools.partial(search_kernel, strides, (block_rows, blo...  4.85 us
    ppermute x6, starting transfers between devices, from_partner(): return lax.ppermute(value, axis, pairs)  3.9 us
    ppermute x6, waiting for transfers between devices, from_partner(): return lax.ppermute(value, axis, pairs)  3.76 us
    unnamed x6, local copies, waits for them, and re-layouts  2.44 us
    pallas_call x1, Pallas kernels, template_rows(): pl.pallas_call(functools.partial(template_kernel, math.pi / (rows * LANES...  0.93 us
    squeeze x1, local copies, waits for them, and re-layouts, body(): harm_map[:, 0, 3]  0.68 us
    ppermute x1, waiting for transfers between devices, from_across(): return lax.ppermute(value, ('bins', 'fdot'), pairs)  0.45 us
  transfers between devices with their start and end apart: 7, of which 4 were waited for; matrix products, arithmetic and copies ran while one was open for 3% of the time, Pallas kernels for 4%

profile of v9, /device:TPU:0, one launch (start us, length us, event | category | flops | bytes accessed | tf_op | source)
XLA Modules:
  0.0 22.2 jit_solution(13863606389473139353)
XLA Ops:
  0.0 0.0 copy-start
  0.0 0.9 %copy-done = f32[2,32768]{1,0:T(2,128)S(1)} copy-done((f32[2,32768]{1,0:T(2,128)S(1)}, f32[2,32768]{1,0:T(2,128)}, u32[]{:S(2)}) %copy-start) | copy-done | bytes 262168
  1.0 5.1 %collective-permute-start.1 = (f32[256,128]{1,0:T(8,128)S(1)}, f32[256,128]{1,0:T(8,128)S(1)}, u32[]{:S(2)}, u32[]{:S(2)}) collective-permute-start(f32[256,128]{1,0:T(8,128)S(1)} %constant_dynamic-slice_fusion.refs_0_), channel_id=1, source_target_pairs={{0,12},{1,9},{2,10},{3,15},{4,8},{5,13},{6,14},{7,11},{8,4},{9,1},... | collective-permute-start | bytes 393224 | tf_op jit(solution)/shard_map/ppermute | solution.py:333
  6.1 0.7 %slice_bitcast_fusion.phase_hbm = s32[7]{0:T(128)S(1)} fusion(s32[7,1,4]{0,2,1:T(4,128)} %param.7), kind=kLoop, calls=%fused_computation | loop fusion | bytes 56 | tf_op jit(solution)/shard_map/squeeze | solution.py:345
  6.8 0.0 copy-start.1
  6.8 0.8 %copy-done.1 = bf16[128,2,128]{2,1,0:T(2,128)(2,1)S(1)} copy-done((bf16[128,2,128]{2,1,0:T(2,128)(2,1)S(1)}, bf16[128,2,128]{2,1,0:T(2,128)(2,1)}, u32[]{:S(2)}) %copy-start.1) | copy-done | bytes 65560
  7.6 0.0 copy-start.2
  7.6 0.7 %copy-done.2 = s32[8]{0:T(128)S(1)} copy-done((s32[8]{0:T(128)S(1)}, s32[8]{0:T(128)}, u32[]{:S(2)}) %copy-start.2) | copy-done | bytes 56
  8.3 0.9 %template_rows.1 = (bf16[2048,512]{1,0:T(8,128)(2,1)S(1)}, bf16[112,512]{1,0:T(8,128)(2,1)S(1)}, f32[16,128]{1,0:T(8,128)S(1)}, f32[2,128,128]{2,1,0:T(8,128)S(1)}, s32[112,128]{1,0:T(8,128)S(1)}) custom-call(s32[8]{0:T(128)S(1)} %copy-done.2, s32[7]{0:T(128)S(1)} %slice_bitcast_fusion.phase_hbm, bf16[128,2,128]{2,1,0:T(2,128)(2,1)S(1)} %copy-done.1), custom_call_target="tpu_custom_call" | custom-call | flops 1048576 | bytes 2097152 | tf_op jit(solution)/shard_map/template_rows/pallas_call | solution.py:84
  9.2 0.1 collective-permute-start
  9.3 0.4 %collective-permute-done.1.refs_2_ = f32[256,128]{1,0:T(8,128)S(1)} collective-permute-done((f32[256,128]{1,0:T(8,128)S(1)}, f32[256,128]{1,0:T(8,128)S(1)}, u32[]{:S(2)}, u32[]{:S(2)}) %collective-permute-start.1) | collective-permute-done | bytes 131104 | tf_op jit(solution)/shard_map/ppermute | solution.py:333
  9.7 3.3 %collective-permute-start.2 = (f32[256,128]{1,0:T(8,128)S(1)}, f32[256,128]{1,0:T(8,128)S(1)}, u32[]{:S(2)}, u32[]{:S(2)}) collective-permute-start(f32[256,128]{1,0:T(8,128)S(1)} %collective-permute-done.1.refs_2_), channel_id=1, source_target_pairs={{0,2},{1,3},{2,0},{3,1},{4,6},{5,7},{6,4},{7,5},{8,10},{9,11},{10,... | collective-permute-start | bytes 393224 | tf_op jit(solution)/shard_map/ppermute | solution.py:20
  13.0 0.0 collective-permute-start.3
  13.0 0.5 %collective-permute-start.5 = (f32[256,128]{1,0:T(8,128)S(1)}, f32[256,128]{1,0:T(8,128)S(1)}, u32[]{:S(2)}, u32[]{:S(2)}) collective-permute-start(f32[256,128]{1,0:T(8,128)S(1)} %collective-permute-done.1.refs_2_), channel_id=1, source_target_pairs={{0,1},{1,0},{2,3},{3,2},{4,5},{5,4},{6,7},{7,6},{8,9},{9,8},{10,11... | collective-permute-start | bytes 393224 | tf_op jit(solution)/shard_map/ppermute | solution.py:20
  13.5 0.7 %collective-permute-done.refs_1_ = f32[256,128]{1,0:T(8,128)S(1)} collective-permute-done((f32[256,128]{1,0:T(8,128)S(1)}, f32[256,128]{1,0:T(8,128)S(1)}, u32[]{:S(2)}, u32[]{:S(2)}) %collective-permute-start) | collective-permute-done | bytes 131104 | tf_op jit(solution)/shard_map/ppermute | solution.py:20
  14.2 0.0 collective-permute-start.4
  14.2 1.7 %collective-permute-done.2.refs_3_ = f32[256,128]{1,0:T(8,128)S(1)} collective-permute-done((f32[256,128]{1,0:T(8,128)S(1)}, f32[256,128]{1,0:T(8,128)S(1)}, u32[]{:S(2)}, u32[]{:S(2)}) %collective-permute-start.2) | collective-permute-done | bytes 131104 | tf_op jit(solution)/shard_map/ppermute | solution.py:20
  16.0 0.0 collective-permute-start.6
  16.0 0.0 collective-permute-done.3.refs_4_
  16.0 0.0 collective-permute-done.5.refs_6_
  16.0 0.0 collective-permute-done.4.refs_5_
  16.0 1.3 %collective-permute-done.6.refs_7_ = f32[256,128]{1,0:T(8,128)S(1)} collective-permute-done((f32[256,128]{1,0:T(8,128)S(1)}, f32[256,128]{1,0:T(8,128)S(1)}, u32[]{:S(2)}, u32[]{:S(2)}) %collective-permute-start.6) | collective-permute-done | bytes 131104 | tf_op jit(solution)/shard_map/ppermute | solution.py:20
  17.3 4.9 %search.1 = f32[256,8,128]{2,1,0:T(8,128)} custom-call(s32[112,128]{1,0:T(8,128)S(1)} %get-tuple-element.17.phase_ref, f32[16,128]{1,0:T(8,128)S(1)} %get-tuple-element.19.base_ref, f32[2,128,128]{2,1,0:T(8,128)S(1)} %get-tuple-element.20.twist_ref, f32[256,128]{1,0:T(8,128)S(1)} %constant_dynamic-slice_fusion.refs_0_, ...), custom_call_target="tpu_custom_call" | custom-call | tf_op jit(solution)/shard_map/search/pallas_call | solution.py:304
  (1 shorter events, 0.0 us)
Async XLA Ops:
  0.0 1.0 %copy-start = (f32[2,32768]{1,0:T(2,128)S(1)}, f32[2,32768]{1,0:T(2,128)}, u32[]{:S(2)}) copy-start(f32[2,32768]{1,0:T(2,128)} %param.4) | copy-start | bytes 786436
  1.0 8.8 %collective-permute-start.1 = (f32[256,128]{1,0:T(8,128)S(1)}, f32[256,128]{1,0:T(8,128)S(1)}, u32[]{:S(2)}, u32[]{:S(2)}) collective-permute-start(f32[256,128]{1,0:T(8,128)S(1)} %constant_dynamic-slice_fusion.refs_0_), channel_id=1, source_target_pairs={{0,12},{1,9},{2,10},{3,15},{4,8},{5,13},{6,14},{7,11},{8,4},{9,1},... | collective-permute-start | bytes 393224 | tf_op jit(solution)/shard_map/ppermute | solution.py:333
  6.8 0.8 %copy-start.1 = (bf16[128,2,128]{2,1,0:T(2,128)(2,1)S(1)}, bf16[128,2,128]{2,1,0:T(2,128)(2,1)}, u32[]{:S(2)}) copy-start(bf16[128,2,128]{2,1,0:T(2,128)(2,1)} %bank_hbm.1) | copy-start | bytes 196612
  7.6 0.7 %copy-start.2 = (s32[8]{0:T(128)S(1)}, s32[8]{0:T(128)}, u32[]{:S(2)}) copy-start(s32[8]{0:T(128)} %index_hbm) | copy-start | bytes 100
  9.2 5.0 %collective-permute-start = (f32[256,128]{1,0:T(8,128)S(1)}, f32[256,128]{1,0:T(8,128)S(1)}, u32[]{:S(2)}, u32[]{:S(2)}) collective-permute-start(f32[256,128]{1,0:T(8,128)S(1)} %constant_dynamic-slice_fusion.refs_0_), channel_id=1, source_target_pairs={{0,4},{4,0},{8,12},{12,8},{1,5},{5,1},{9,13},{13,9},{2,6},{6,2},{1... | collective-permute-start | bytes 393224 | tf_op jit(solution)/shard_map/ppermute | solution.py:20
  9.7 6.3 %collective-permute-start.2 = (f32[256,128]{1,0:T(8,128)S(1)}, f32[256,128]{1,0:T(8,128)S(1)}, u32[]{:S(2)}, u32[]{:S(2)}) collective-permute-start(f32[256,128]{1,0:T(8,128)S(1)} %collective-permute-done.1.refs_2_), channel_id=1, source_target_pairs={{0,2},{1,3},{2,0},{3,1},{4,6},{5,7},{6,4},{7,5},{8,10},{9,11},{10,... | collective-permute-start | bytes 393224 | tf_op jit(solution)/shard_map/ppermute | solution.py:20
  13.0 3.0 %collective-permute-start.3 = (f32[256,128]{1,0:T(8,128)S(1)}, f32[256,128]{1,0:T(8,128)S(1)}, u32[]{:S(2)}, u32[]{:S(2)}) collective-permute-start(f32[256,128]{1,0:T(8,128)S(1)} %constant_dynamic-slice_fusion.refs_0_), channel_id=1, source_target_pairs={{0,1},{1,0},{2,3},{3,2},{4,5},{5,4},{6,7},{7,6},{8,9},{9,8},{10,11... | collective-permute-start | bytes 393224 | tf_op jit(solution)/shard_map/ppermute | solution.py:20
  13.0 3.0 %collective-permute-start.5 = (f32[256,128]{1,0:T(8,128)S(1)}, f32[256,128]{1,0:T(8,128)S(1)}, u32[]{:S(2)}, u32[]{:S(2)}) collective-permute-start(f32[256,128]{1,0:T(8,128)S(1)} %collective-permute-done.1.refs_2_), channel_id=1, source_target_pairs={{0,1},{1,0},{2,3},{3,2},{4,5},{5,4},{6,7},{7,6},{8,9},{9,8},{10,11... | collective-permute-start | bytes 393224 | tf_op jit(solution)/shard_map/ppermute | solution.py:20
  14.2 1.8 %collective-permute-start.4 = (f32[256,128]{1,0:T(8,128)S(1)}, f32[256,128]{1,0:T(8,128)S(1)}, u32[]{:S(2)}, u32[]{:S(2)}) collective-permute-start(f32[256,128]{1,0:T(8,128)S(1)} %collective-permute-done.refs_1_), channel_id=1, source_target_pairs={{0,1},{1,0},{2,3},{3,2},{4,5},{5,4},{6,7},{7,6},{8,9},{9,8},{10,11... | collective-permute-start | bytes 393224 | tf_op jit(solution)/shard_map/ppermute | solution.py:20
  16.0 1.3 %collective-permute-start.6 = (f32[256,128]{1,0:T(8,128)S(1)}, f32[256,128]{1,0:T(8,128)S(1)}, u32[]{:S(2)}, u32[]{:S(2)}) collective-permute-start(f32[256,128]{1,0:T(8,128)S(1)} %collective-permute-done.2.refs_3_), channel_id=1, source_target_pairs={{0,1},{1,0},{2,3},{3,2},{4,5},{5,4},{6,7},{7,6},{8,9},{9,8},{10,11... | collective-permute-start | bytes 393224 | tf_op jit(solution)/shard_map/ppermute | solution.py:20
